TPU v7x, 32 devices: a whole 2x2x4 slice. The times are simulated.
32 devices in a mesh: gx: 4 (over x, core), gy: 4 (over z), sec: 2 (over y).
Axes of the slice: x: 2, y: 2, z: 4, core: 2. Of those that a mesh axis runs over, the one named last changes fastest.
Arguments:
- pressure: float32 [32, 32, 256], P('gx', 'gy', 'sec'), may hold values from -6 to 6
- fluid_velocity: float32 [3, 32, 32, 256], P(None, 'gx', 'gy', 'sec'), may hold values from -6 to 6
- positions: float32 [3, 524288], P(None, ('gx', 'gy', 'sec')), may hold values from -24 to 24
- velocities: float32 [3, 524288], P(None, ('gx', 'gy', 'sec')), may hold values from -6 to 6
- volumes: float32 [524288], P(('gx', 'gy', 'sec')), may hold values from 0.05 to 0.4
- cells: int32 [524288], P(('gx', 'gy', 'sec')), may hold values from 0 to 16383
- partners: int32 [8, 524288], P(None, ('gx', 'gy', 'sec')), may hold values from 0 to 127
- departures: int32 [4, 32768], P(None, ('gx', 'gy', 'sec')), may hold values from 0 to 16383, as said below
Outputs:
- pressure_out: float32 [32, 32, 256], P('gx', 'gy', 'sec')
- velocity_out: float32 [3, 32, 32, 256], P(None, 'gx', 'gy', 'sec')
- positions_out: float32 [3, 524288], P(None, ('gx', 'gy', 'sec'))
- velocities_out: float32 [3, 524288], P(None, ('gx', 'gy', 'sec'))
Inputs may be any that keep to these rules, and one draw needn't show every extreme that they name: Within each tile half's 1024 columns, the 4 x 1024 entries of departures are distinct particle indices of that tile half. cells[n] = x * 8 * 256 + y * 256 + z with x, y the cell's place within the tile and z its place along the whole depth.
All inputs are finite; a program needn't handle non-finite values.
Results may differ from a plain program's by a relative error of at most 0.00008.
Values sent between devices are 32-bit elements; how exact they have to be, the bound alone decides.
No kernel may reach another device: no remote copies, remote signals or barrier semaphores. Data moves between devices by JAX's collectives and lax.ppermute only.
A program may use at most 128 MiB of HBM per device.

v0:
```python
import math

import jax
import jax.numpy as jnp
from jax import lax
from jax.sharding import PartitionSpec as P

SWEEPS = 4
PAIRS = 8
BLOCK = 128


TIME_STEP = 0.1
RELAX_RATE = 0.5
STIFFNESS = 1.0
DAMPING = 0.5
RANGE_SQUARED = 16.0
GRAVITY = 1.0


def with_halo(block, sides, width):
    for axis, dim in sides:
        count = lax.axis_size(axis)
        forward = [(i, i + 1) for i in range(count - 1)]
        forward.append((count - 1, 0))
        backward = [(target, source) for source, target in forward]
        low = lax.ppermute(
            lax.slice_in_dim(block, block.shape[dim] - width, None, axis=dim), axis, forward
        )
        high = lax.ppermute(lax.slice_in_dim(block, 0, width, axis=dim), axis, backward)
        block = jnp.concatenate([low, block, high], axis=dim)
    return block


def shifted(block, axis, distance):
    devices = range(lax.axis_size(axis))
    route = [((i - distance) % len(devices), i) for i in devices]
    return lax.ppermute(block, axis, route)


def inner(values, direction, offset):
    slicer = [slice(1, values.shape[position] - 1) for position in range(3)]
    slicer[direction] = slice(1 + offset, values.shape[direction] - 1 + offset)
    return values[tuple(slicer)]


def extend(values, width):
    return with_halo(values[None], (("gx", 1), ("gy", 2), ("sec", 3)), width)[0]


def relax(grown, face_coeffs, diagonal, divergence):
    neighbours = jnp.zeros_like(diagonal)
    for direction in range(3):
        upper_face, lower_face = face_coeffs[direction]
        neighbours = (
            neighbours
            + upper_face * inner(grown, direction, 1)
            + lower_face * inner(grown, direction, -1)
        )
    return (neighbours - divergence) / diagonal


def block_contact(inputs):
    state_group, pair_group = inputs
    picker = (pair_group[..., None] == lax.iota(jnp.int32, BLOCK)).astype(jnp.float32)
    other = jnp.einsum("cgj,kgij->ckgi", state_group, picker, precision=lax.Precision.HIGHEST)
    separation = state_group[:3, None] - other[:3]
    distance_sq = jnp.sum(separation * separation, axis=0)
    weight = 1.0 / (1.0 + distance_sq / RANGE_SQUARED)
    pushed = weight[None] * (STIFFNESS * separation + DAMPING * (other[3:] - state_group[3:, None]))
    return jnp.sum(pushed, axis=1)


def contact_force(places, speeds, partner_rows):
    blocks = places.shape[1] // BLOCK
    group = math.gcd(blocks, 16)
    groups = blocks // group
    state = (
        jnp.concatenate([places, speeds], axis=0)
        .reshape(6, groups, group, BLOCK)
        .transpose(1, 0, 2, 3)
    )
    pair_rows = partner_rows.reshape(PAIRS, groups, group, BLOCK).transpose(1, 0, 2, 3)
    result = lax.map(block_contact, (state, pair_rows))
    return result.transpose(1, 0, 2, 3).reshape(3, -1)


def advance(places, speeds, volumes, void_at, flow_at, contact):
    drag_rate = RELAX_RATE * jnp.exp(-2.65 * jnp.log(void_at) - 2.0 / 3.0 * jnp.log(volumes))
    gravity_vec = jnp.array([-GRAVITY, 0.0, 0.0], dtype=jnp.float32)[:, None]
    moved_speed = (speeds + TIME_STEP * (drag_rate * flow_at + contact + gravity_vec)) / (
        1.0 + TIME_STEP * drag_rate
    )
    return (places + TIME_STEP * moved_speed, moved_speed)


def body(pressure, fluid_velocity, positions, velocities, volumes, cells, partners, departures):
    size_x, size_y, size_z = pressure.shape
    column_z = size_z * lax.axis_size("sec")
    column = jax.ops.segment_sum(volumes, cells, num_segments=size_x * size_y * column_z).reshape(
        size_x, size_y, column_z
    )
    solid_half = lax.psum_scatter(column, "sec", scatter_dimension=2, tiled=True)
    voidage = 1.0 / (1.0 + solid_half)
    sweep_depth = 1
    fluid_state = jnp.concatenate([voidage[None], fluid_velocity], axis=0)
    extended = with_halo(fluid_state, (("gx", 1), ("gy", 2), ("sec", 3)), sweep_depth)
    void_ext = extended[0]
    centre = inner(void_ext, 0, 0)
    face_coeffs = []
    diagonal = jnp.zeros_like(centre)
    divergence = jnp.zeros_like(centre)
    for direction in range(3):
        upper_face = 0.5 * (centre + inner(void_ext, direction, 1))
        lower_face = 0.5 * (centre + inner(void_ext, direction, -1))
        face_coeffs.append((upper_face, lower_face))
        diagonal = diagonal + upper_face + lower_face
        flux_part = void_ext * extended[1 + direction]
        divergence = divergence + 0.5 * (
            inner(flux_part, direction, 1) - inner(flux_part, direction, -1)
        )
    current = pressure
    for group_index in range(SWEEPS // sweep_depth):
        grown = extend(current, sweep_depth)
        grown = relax(grown, face_coeffs, diagonal, divergence)
        current = grown
    grown = extend(current, 1)
    new_velocity = jnp.stack(
        [
            fluid_velocity[direction]
            - 0.5 * (inner(grown, direction, 1) - inner(grown, direction, -1))
            for direction in range(3)
        ]
    )
    outgoing = jnp.concatenate([voidage[None], new_velocity], axis=0)
    column_rows = lax.all_gather(outgoing, "sec", axis=3, tiled=True)
    column_void = column_rows[0]
    column_flow = column_rows[1:]
    void_at = column_void.reshape(-1)[cells]
    flow_at = column_flow.reshape(3, -1)[:, cells]
    contact = contact_force(positions, velocities, partners)
    moved_place, moved_speed = advance(positions, velocities, volumes, void_at, flow_at, contact)
    particle_state = jnp.concatenate([moved_place, moved_speed], axis=0)
    leaving = particle_state[:, departures]
    for offset, sent_row, slot_row in ((1, 0, 1), (-1, 1, 0)):
        arrived = shifted(leaving[:, sent_row], "gx", offset)
        particle_state = particle_state.at[:, departures[slot_row]].set(arrived)
    for offset, sent_row, slot_row in ((1, 2, 3), (-1, 3, 2)):
        arrived = shifted(leaving[:, sent_row], "gy", offset)
        particle_state = particle_state.at[:, departures[slot_row]].set(arrived)
    return (current, new_velocity, particle_state[:3], particle_state[3:])


def solution(mesh):
    placed = (
        P("gx", "gy", "sec"),
        P(None, "gx", "gy", "sec"),
        P(None, ("gx", "gy", "sec")),
        P(None, ("gx", "gy", "sec")),
        P(("gx", "gy", "sec")),
        P(("gx", "gy", "sec")),
        P(None, ("gx", "gy", "sec")),
        P(None, ("gx", "gy", "sec")),
    )
    return jax.shard_map(
        body,
        mesh=mesh,
        in_specs=placed,
        out_specs=(
            P("gx", "gy", "sec"),
            P(None, "gx", "gy", "sec"),
            P(None, ("gx", "gy", "sec")),
            P(None, ("gx", "gy", "sec")),
        ),
        check_vma=False,
    )
```

profile of v0, /device:TPU:1, one launch (start us, length us, event | category | flops | bytes accessed | tf_op | source)
XLA Modules:
  0.0 539.4 jit_solution(12067058192355811597)
XLA Ops:
  7.2 86.1 %scatter_custom_fusion = f32[16384]{0:T(1024)S(1)} fusion(s32[16384]{0:T(1024)} %param.16, f32[16384]{0:T(1024)} %param.15, f32[]{:T(128)} %constant.25.clone.1), kind=kCustom, calls=%fused_computation.166 | custom fusion | flops 16384 | bytes 66048 | tf_op jit(solution)/shard_map/scatter-add | solution.py:100
  94.7 2.6 collective-permute-start.6
  98.1 2.3 collective-permute-done.7
  101.2 1.3 collective-permute-start.8
  102.5 2.1 collective-permute-start.9
  104.6 1.2 reduce-scatter.2.cloned.1.call-done
  107.3 2.0 collective-permute-start
  110.2 2.3 collective-permute-done.1
  112.5 1.0 pad_maximum_fusion.14
  113.5 1.2 collective-permute-start.2
  114.8 2.1 collective-permute-start.3
  117.3 1.2 collective-permute-start.11
  119.9 1.2 collective-permute-start.5
  121.5 1.8 collective-permute-done.11
  124.2 6.1 %collective-permute-done.4 = f32[4,10,10,1]{3,2,1,0:T(8,128)S(1)} collective-permute-done((f32[4,10,10,1]{3,2,1,0:T(8,128)S(1)}, f32[4,10,10,1]{3,2,1,0:T(8,128)S(1)}, u32[]{:S(2)}, u32[]{:S(2)}) %collective-permute-start.4) | collective-permute-done | bytes 1632 | tf_op jit(solution)/shard_map/ppermute | solution.py:27
  130.2 6.9 %collective-permute-done.5 = f32[4,10,10,1]{3,2,1,0:T(8,128)S(1)} collective-permute-done((f32[4,10,10,1]{3,2,1,0:T(8,128)S(1)}, f32[4,10,10,1]{3,2,1,0:T(8,128)S(1)}, u32[]{:S(2)}, u32[]{:S(2)}) %collective-permute-start.5) | collective-permute-done | bytes 1632 | tf_op jit(solution)/shard_map/ppermute | solution.py:30
  137.2 1.4 pad_maximum_fusion
  140.3 2.3 collective-permute-done.13
  142.7 3.3 collective-permute-start.15
  145.9 1.0 collective-permute-done.14
  148.6 1.8 collective-permute-done.16
  150.4 1.5 collective-permute-done.17
  152.2 2.9 collective-permute-start.18
  155.9 2.3 collective-permute-done.19
  158.2 3.4 collective-permute-start.21
  163.0 1.2 collective-permute-start.23
  164.2 2.5 collective-permute-done.22
  166.7 1.8 collective-permute-done.23
  168.8 1.1 collective-permute-start.24
  170.6 2.3 collective-permute-done.25
  173.6 2.8 collective-permute-start.27
  176.4 69.6 %while.10 = (s32[]{:T(128)}, f32[8,3,16,128]{3,1,2,0:T(4,128)S(1)}, f32[8,6,16,128]{3,1,2,0:T(8,128)S(1)}, s32[8,8,16,128]{3,1,2,0:T(8,128)}, s32[]{:T(128)}, /*index=5*/s32[]{:T(128)}, s32[]{}) while((s32[]{:T(128)}, f32[8,3,16,128]{3,1,2,0:T(4,128)S(1)}, f32[8,6,16,128]{3,1,2,0:T(8,128)S(1)}, s32[8,8,16,128]{3,1,2,0:T(8,128)}, s32[]{:T(128)}, ...), condition=%wide.region_5.6_spmd, body=%wide.region_2.5_spmd.sunk | while | flops 153561088 | bytes 1769589 | solution.py:84
  177.3 7.4 %fusion.105 = f32[6,8,16,128]{3,0,1,2:T(8,128)S(1)} fusion(s32[8,16,128]{2,0,1:T(8,128)S(1)} %dynamic-slice_bitcast_fusion.5, f32[8,6,16,128]{3,1,2,0:T(8,128)S(1)} %get-tuple-element.162, s32[]{:T(128)S(6)} %copy.53), kind=kOutput, calls=%fused_computation.11.clone.1 | convolution fusion | flops 153092096 | bytes 524292 | tf_op jit(solution)/shard_map/while/body/eval_jaxpr/cgj,kgij->ckgi/dot_general | solution.py:66
  186.0 7.4 %fusion.105 = f32[6,8,16,128]{3,0,1,2:T(8,128)S(1)} fusion(s32[8,16,128]{2,0,1:T(8,128)S(1)} %dynamic-slice_bitcast_fusion.5, f32[8,6,16,128]{3,1,2,0:T(8,128)S(1)} %get-tuple-element.162, s32[]{:T(128)S(6)} %copy.53), kind=kOutput, calls=%fused_computation.11.clone.1 | convolution fusion | flops 153092096 | bytes 524292 | tf_op jit(solution)/shard_map/while/body/eval_jaxpr/cgj,kgij->ckgi/dot_general | solution.py:66
  194.7 7.4 %fusion.105 = f32[6,8,16,128]{3,0,1,2:T(8,128)S(1)} fusion(s32[8,16,128]{2,0,1:T(8,128)S(1)} %dynamic-slice_bitcast_fusion.5, f32[8,6,16,128]{3,1,2,0:T(8,128)S(1)} %get-tuple-element.162, s32[]{:T(128)S(6)} %copy.53), kind=kOutput, calls=%fused_computation.11.clone.1 | convolution fusion | flops 153092096 | bytes 524292 | tf_op jit(solution)/shard_map/while/body/eval_jaxpr/cgj,kgij->ckgi/dot_general | solution.py:66
  203.4 7.4 %fusion.105 = f32[6,8,16,128]{3,0,1,2:T(8,128)S(1)} fusion(s32[8,16,128]{2,0,1:T(8,128)S(1)} %dynamic-slice_bitcast_fusion.5, f32[8,6,16,128]{3,1,2,0:T(8,128)S(1)} %get-tuple-element.162, s32[]{:T(128)S(6)} %copy.53), kind=kOutput, calls=%fused_computation.11.clone.1 | convolution fusion | flops 153092096 | bytes 524292 | tf_op jit(solution)/shard_map/while/body/eval_jaxpr/cgj,kgij->ckgi/dot_general | solution.py:66
  212.1 7.4 %fusion.105 = f32[6,8,16,128]{3,0,1,2:T(8,128)S(1)} fusion(s32[8,16,128]{2,0,1:T(8,128)S(1)} %dynamic-slice_bitcast_fusion.5, f32[8,6,16,128]{3,1,2,0:T(8,128)S(1)} %get-tuple-element.162, s32[]{:T(128)S(6)} %copy.53), kind=kOutput, calls=%fused_computation.11.clone.1 | convolution fusion | flops 153092096 | bytes 524292 | tf_op jit(solution)/shard_map/while/body/eval_jaxpr/cgj,kgij->ckgi/dot_general | solution.py:66
  220.8 7.4 %fusion.105 = f32[6,8,16,128]{3,0,1,2:T(8,128)S(1)} fusion(s32[8,16,128]{2,0,1:T(8,128)S(1)} %dynamic-slice_bitcast_fusion.5, f32[8,6,16,128]{3,1,2,0:T(8,128)S(1)} %get-tuple-element.162, s32[]{:T(128)S(6)} %copy.53), kind=kOutput, calls=%fused_computation.11.clone.1 | convolution fusion | flops 153092096 | bytes 524292 | tf_op jit(solution)/shard_map/while/body/eval_jaxpr/cgj,kgij->ckgi/dot_general | solution.py:66
  229.5 7.4 %fusion.105 = f32[6,8,16,128]{3,0,1,2:T(8,128)S(1)} fusion(s32[8,16,128]{2,0,1:T(8,128)S(1)} %dynamic-slice_bitcast_fusion.5, f32[8,6,16,128]{3,1,2,0:T(8,128)S(1)} %get-tuple-element.162, s32[]{:T(128)S(6)} %copy.53), kind=kOutput, calls=%fused_computation.11.clone.1 | convolution fusion | flops 153092096 | bytes 524292 | tf_op jit(solution)/shard_map/while/body/eval_jaxpr/cgj,kgij->ckgi/dot_general | solution.py:66
  238.2 7.4 %fusion.105 = f32[6,8,16,128]{3,0,1,2:T(8,128)S(1)} fusion(s32[8,16,128]{2,0,1:T(8,128)S(1)} %dynamic-slice_bitcast_fusion.5, f32[8,6,16,128]{3,1,2,0:T(8,128)S(1)} %get-tuple-element.162, s32[]{:T(128)S(6)} %copy.53), kind=kOutput, calls=%fused_computation.11.clone.1 | convolution fusion | flops 153092096 | bytes 524292 | tf_op jit(solution)/shard_map/while/body/eval_jaxpr/cgj,kgij->ckgi/dot_general | solution.py:66
  247.7 2.2 collective-permute-done.28
  249.9 1.8 collective-permute-done.29
  252.0 2.0 collective-permute-start.30
  254.7 2.3 collective-permute-done.31
  257.1 3.3 collective-permute-start.33
  263.0 2.2 collective-permute-done.34
  265.2 1.8 collective-permute-done.35
  267.2 4.5 all_gather.3
  271.8 90.5 %gather_fusion = f32[16384]{0:T(1024)S(1)} fusion(f32[16384]{0:T(1024)S(1)} %bitcast.145, s32[16384]{0:T(1024)S(1)} %fusion.27), kind=kCustom, calls=%fused_computation | custom fusion | bytes 196608 | tf_op jit(solution)/shard_map/gather | solution.py:139
  362.4 4.7 copy.40
  367.1 57.8 %gather_fusion.1 = f32[16384,3]{1,0:T(8,128)} fusion(f32[3,16384]{0,1:T(8,128)} %bitcast.146, s32[16384]{0:T(1024)S(1)} %fusion.27), kind=kCustom, calls=%fused_computation.1 | custom fusion | bytes 458752 | tf_op jit(solution)/shard_map/gather | solution.py:140
  424.9 5.4 %copy.41 = f32[16384,3]{0,1:T(4,128)S(1)} copy(f32[16384,3]{1,0:T(8,128)} %gather_fusion.1) | data formatting | bytes 393216 | tf_op jit(solution)/shard_map/gather | solution.py:140
  430.7 5.3 copy.43
  436.0 14.1 %gather_fusion.2 = f32[4096,6]{1,0:T(8,128)S(1)} fusion(f32[6,16384]{0,1:T(8,128)} %copy.43, s32[4096]{0:T(1024)S(1)} %bitcast_clamp_fusion), kind=kCustom, calls=%fused_computation.2 | custom fusion | bytes 212992 | tf_op jit(solution)/shard_map/gather | solution.py:144
  451.1 3.5 collective-permute-start.39
  454.6 2.7 collective-permute-start.37
  458.1 10.8 %collective-permute-done.36 = f32[6,1024]{0,1:T(8,128)S(1)} collective-permute-done((f32[6,1024]{0,1:T(8,128)S(1)}, f32[6,1024]{0,1:T(8,128)S(1)}, u32[]{:S(2)}, u32[]{:S(2)}) %collective-permute-start.36) | collective-permute-done | bytes 24608 | tf_op jit(solution)/shard_map/ppermute | solution.py:38
  468.9 9.7 %scatter_custom_fusion.1 = f32[6,16384]{0,1:T(8,128)} fusion(f32[6,16384]{0,1:T(8,128)} %copy.43, s32[1024]{0:T(1024)S(1)} %bitcast.162, f32[6,1024]{0,1:T(8,128)S(1)} %collective-permute-done.36), kind=kCustom, calls=%fused_computation.40 | custom fusion | bytes 917504 | tf_op jit(solution)/shard_map/scatter | solution.py:147
  478.7 9.7 %scatter_custom_fusion.2 = f32[6,16384]{0,1:T(8,128)} fusion(f32[6,16384]{0,1:T(8,128)} %scatter_custom_fusion.1, s32[1024]{0:T(1024)S(1)} %bitcast.161, f32[6,1024]{0,1:T(8,128)S(1)} %collective-permute-done.37), kind=kCustom, calls=%fused_computation.38 | custom fusion | bytes 917504 | tf_op jit(solution)/shard_map/scatter | solution.py:147
  488.4 9.7 %scatter_custom_fusion.3 = f32[6,16384]{0,1:T(8,128)} fusion(f32[6,16384]{0,1:T(8,128)} %scatter_custom_fusion.2, s32[1024]{0:T(1024)S(1)} %bitcast.160, f32[6,1024]{0,1:T(8,128)S(1)} %collective-permute-done.38), kind=kCustom, calls=%fused_computation.36 | custom fusion | bytes 917504 | tf_op jit(solution)/shard_map/scatter | solution.py:150
  498.2 9.7 %scatter_custom_fusion.4 = f32[6,16384]{0,1:T(8,128)} fusion(f32[6,16384]{0,1:T(8,128)} %scatter_custom_fusion.3, s32[1024]{0:T(1024)S(1)} %bitcast.159, f32[6,1024]{0,1:T(8,128)S(1)} %collective-permute-done.39), kind=kCustom, calls=%fused_computation.34 | custom fusion | bytes 917504 | tf_op jit(solution)/shard_map/scatter | solution.py:150
  507.9 12.8 %fusion.89 = (f32[3,16384]{0,1:T(8,128)}, f32[3,16384]{0,1:T(8,128)}) fusion(f32[6,16384]{0,1:T(8,128)} %scatter_custom_fusion.4), kind=kLoop, calls=%fused_computation.195 | loop fusion | bytes 786432 | tf_op jit(solution)/shard_map/slice | solution.py:151
  520.7 5.9 %copy.45 = f32[3,16384]{1,0:T(4,128)} copy(f32[3,16384]{0,1:T(8,128)} %get-tuple-element.63) | data formatting | bytes 393216
  526.6 5.9 %copy.44 = f32[3,16384]{1,0:T(4,128)} copy(f32[3,16384]{0,1:T(8,128)} %get-tuple-element.64) | data formatting | bytes 393216
  (161 shorter events, 34.1 us)
Async XLA Ops:
  7.2 162.7 %copy-start.2 = (f32[3,16384]{1,0:T(4,128)S(1)}, f32[3,16384]{1,0:T(4,128)}, u32[]{:S(2)}) copy-start(f32[3,16384]{1,0:T(4,128)} %param.14) | copy-start | bytes 589828
  7.2 162.7 %copy-start.1 = (f32[3,16384]{1,0:T(4,128)S(1)}, f32[3,16384]{1,0:T(4,128)}, u32[]{:S(2)}) copy-start(f32[3,16384]{1,0:T(4,128)} %param.13) | copy-start | bytes 589828
  7.2 98.6 %reduce-scatter.2.cloned.1.call-start = ((), (), s32[]{:S(2)}) async-start(), calls=%async_computation.1 | async-start | bytes 98304 | tf_op jit(solution)/shard_map/reduce_scatter | solution.py:103
  94.7 3.4 collective-permute-start.6
  97.3 3.0 collective-permute-start.7
  101.2 8.2 %collective-permute-start.8 = (f32[1,10,1,128]{3,2,1,0:T(1,128)S(1)}, f32[1,10,1,128]{3,2,1,0:T(1,128)S(1)}, u32[]{:S(2)}, u32[]{:S(2)}) collective-permute-start(f32[1,10,1,128]{3,2,1,0:T(1,128)S(1)} %get-tuple-element.101), channel_id=1, source_target_pairs={{0,2},{2,4},{4,6},{6,0},{1,3},{3,5},{5,7},{7,1},{8,10},{10,12},{12... | collective-permute-start | bytes 15368 | tf_op jit(solution)/shard_map/ppermute | solution.py:27
  102.5 6.9 %collective-permute-start.9 = (f32[1,10,1,128]{3,2,1,0:T(1,128)S(1)}, f32[1,10,1,128]{3,2,1,0:T(1,128)S(1)}, u32[]{:S(2)}, u32[]{:S(2)}) collective-permute-start(f32[1,10,1,128]{3,2,1,0:T(1,128)S(1)} %get-tuple-element.102), channel_id=1, source_target_pairs={{2,0},{4,2},{6,4},{0,6},{3,1},{5,3},{7,5},{1,7},{10,8},{12,10},{14... | collective-permute-start | bytes 15368 | tf_op jit(solution)/shard_map/ppermute | solution.py:30
  107.3 2.9 collective-permute-start
  109.4 3.2 collective-permute-start.1
  113.5 4.9 collective-permute-start.2
  114.8 3.7 collective-permute-start.3
  116.9 4.5 collective-permute-start.10
  117.3 6.0 %collective-permute-start.11 = (f32[1,10,10,1]{3,2,1,0:T(8,128)S(1)}, f32[1,10,10,1]{3,2,1,0:T(8,128)S(1)}, u32[]{:S(2)}, u32[]{:S(2)}) collective-permute-start(f32[1,10,10,1]{3,2,1,0:T(8,128)S(1)} %get-tuple-element.92), channel_id=1, source_target_pairs={{1,0},{0,1},{3,2},{2,3},{5,4},{4,5},{7,6},{6,7},{9,8},{8,9},{11,10... | collective-permute-start | bytes 1208 | tf_op jit(solution)/shard_map/ppermute | solution.py:30
  119.6 10.6 %collective-permute-start.4 = (f32[4,10,10,1]{3,2,1,0:T(8,128)S(1)}, f32[4,10,10,1]{3,2,1,0:T(8,128)S(1)}, u32[]{:S(2)}, u32[]{:S(2)}) collective-permute-start(f32[4,10,10,1]{3,2,1,0:T(8,128)S(1)} %get-tuple-element.72), channel_id=1, source_target_pairs={{0,1},{1,0},{2,3},{3,2},{4,5},{5,4},{6,7},{7,6},{8,9},{9,8},{10,11... | collective-permute-start | bytes 4808 | tf_op jit(solution)/shard_map/ppermute | solution.py:27
  119.9 17.3 %collective-permute-start.5 = (f32[4,10,10,1]{3,2,1,0:T(8,128)S(1)}, f32[4,10,10,1]{3,2,1,0:T(8,128)S(1)}, u32[]{:S(2)}, u32[]{:S(2)}) collective-permute-start(f32[4,10,10,1]{3,2,1,0:T(8,128)S(1)} %get-tuple-element.73), channel_id=1, source_target_pairs={{1,0},{0,1},{3,2},{2,3},{5,4},{4,5},{7,6},{6,7},{9,8},{8,9},{11,10... | collective-permute-start | bytes 4808 | tf_op jit(solution)/shard_map/ppermute | solution.py:30
  138.9 1.4 collective-permute-start.12
  139.6 3.0 collective-permute-start.13
  142.6 4.3 collective-permute-start.14
  142.7 4.3 collective-permute-start.15
  147.0 3.4 collective-permute-start.16
  147.6 4.3 collective-permute-start.17
  152.2 3.7 collective-permute-start.18
  155.1 3.0 collective-permute-start.19
  158.1 4.4 collective-permute-start.20
  158.2 4.3 collective-permute-start.21
  162.6 4.1 collective-permute-start.22
  163.0 5.5 %collective-permute-start.23 = (f32[1,10,10,1]{3,2,1,0:T(8,128)S(1)}, f32[1,10,10,1]{3,2,1,0:T(8,128)S(1)}, u32[]{:S(2)}, u32[]{:S(2)}) collective-permute-start(f32[1,10,10,1]{3,2,1,0:T(8,128)S(1)} %get-tuple-element.88), channel_id=1, source_target_pairs={{1,0},{0,1},{3,2},{2,3},{5,4},{4,5},{7,6},{6,7},{9,8},{8,9},{11,10... | collective-permute-start | bytes 1208 | tf_op jit(solution)/shard_map/ppermute | solution.py:30
  168.8 1.8 collective-permute-start.24
  169.9 3.0 collective-permute-start.25
  172.9 73.0 %collective-permute-start.26 = (f32[1,10,1,128]{3,2,1,0:T(1,128)S(1)}, f32[1,10,1,128]{3,2,1,0:T(1,128)S(1)}, u32[]{:S(2)}, u32[]{:S(2)}) collective-permute-start(f32[1,10,1,128]{3,2,1,0:T(1,128)S(1)} %get-tuple-element.95), channel_id=1, source_target_pairs={{0,2},{2,4},{4,6},{6,0},{1,3},{3,5},{5,7},{7,1},{8,10},{10,12},{12... | collective-permute-start | bytes 15368 | tf_op jit(solution)/shard_map/ppermute | solution.py:27
  173.6 72.4 %collective-permute-start.27 = (f32[1,10,1,128]{3,2,1,0:T(1,128)S(1)}, f32[1,10,1,128]{3,2,1,0:T(1,128)S(1)}, u32[]{:S(2)}, u32[]{:S(2)}) collective-permute-start(f32[1,10,1,128]{3,2,1,0:T(1,128)S(1)} %get-tuple-element.96), channel_id=1, source_target_pairs={{2,0},{4,2},{6,4},{0,6},{3,1},{5,3},{7,5},{1,7},{10,8},{12,10},{14... | collective-permute-start | bytes 15368 | tf_op jit(solution)/shard_map/ppermute | solution.py:30
  176.4 71.3 %copy-start.4 = (s32[16384]{0:T(1024)S(1)}, s32[16384]{0:T(1024)}, u32[]{:S(2)}) copy-start(s32[16384]{0:T(1024)} %param.16) | copy-start | bytes 196612
  176.4 77.6 %copy-start.5 = (s32[4,1024]{1,0:T(4,128)S(1)}, s32[4,1024]{1,0:T(4,128)}, u32[]{:S(2)}) copy-start(s32[4,1024]{1,0:T(4,128)} %param.18) | copy-start | bytes 49156
  176.4 90.7 %copy-start = (f32[3,8,8,128]{3,2,1,0:T(8,128)S(1)}, f32[3,8,8,128]{3,2,1,0:T(8,128)}, u32[]{:S(2)}) copy-start(f32[3,8,8,128]{3,2,1,0:T(8,128)} %param.12) | copy-start | bytes 294916
  246.1 3.8 collective-permute-start.28
  247.0 4.6 collective-permute-start.29
  251.9 110.4 %copy-start.3 = (f32[8,8,128]{2,1,0:T(8,128)}, f32[8,8,128]{2,1,0:T(8,128)S(1)}, u32[]{:S(2)}) copy-start(f32[8,8,128]{2,1,0:T(8,128)S(1)} %fusion.39) | copy-start | bytes 98308
  252.0 2.8 collective-permute-start.30
  254.0 3.0 collective-permute-start.31
  257.0 4.3 collective-permute-start.32
  257.1 4.3 collective-permute-start.33
  261.4 3.7 collective-permute-start.34
  262.4 4.6 collective-permute-start.35
  271.8 90.6 %copy-start.6 = (f32[16384]{0:T(1024)S(1)}, f32[16384]{0:T(1024)}, u32[]{:S(2)}) copy-start(f32[16384]{0:T(1024)} %param.15) | copy-start | bytes 196612
  362.4 67.9 %copy-start.7 = (f32[3]{0:T(128)S(1)}, f32[3]{0:T(128)}, u32[]{:S(2)}) copy-start(f32[3]{0:T(128)} %constant.13.clone) | copy-start | bytes 40
  451.1 47.1 %collective-permute-start.39 = (f32[6,1024]{0,1:T(8,128)S(1)}, f32[6,1024]{0,1:T(8,128)S(1)}, u32[]{:S(2)}, u32[]{:S(2)}) collective-permute-start(f32[6,1024]{0,1:T(8,128)S(1)} %get-tuple-element.65), channel_id=1, source_target_pairs={{2,0},{4,2},{6,4},{0,6},{3,1},{5,3},{7,5},{1,7},{10,8},{12,10},{14... | collective-permute-start | bytes 73736 | tf_op jit(solution)/shard_map/ppermute | solution.py:38
  454.6 33.8 %collective-permute-start.38 = (f32[6,1024]{0,1:T(8,128)S(1)}, f32[6,1024]{0,1:T(8,128)S(1)}, u32[]{:S(2)}, u32[]{:S(2)}) collective-permute-start(f32[6,1024]{0,1:T(8,128)S(1)} %get-tuple-element.66), channel_id=1, source_target_pairs={{6,0},{0,2},{2,4},{4,6},{7,1},{1,3},{3,5},{5,7},{14,8},{8,10},{10,... | collective-permute-start | bytes 73736 | tf_op jit(solution)/shard_map/ppermute | solution.py:38
  454.6 24.0 %collective-permute-start.37 = (f32[6,1024]{0,1:T(8,128)}, f32[6,1024]{0,1:T(8,128)S(1)}, u32[]{:S(2)}, u32[]{:S(2)}) collective-permute-start(f32[6,1024]{0,1:T(8,128)} %get-tuple-element.67), channel_id=1, source_target_pairs={{8,0},{16,8},{24,16},{0,24},{9,1},{17,9},{25,17},{1,25},{10,2},{18... | collective-permute-start | bytes 73736 | tf_op jit(solution)/shard_map/ppermute | solution.py:38
  457.3 11.6 %collective-permute-start.36 = (f32[6,1024]{0,1:T(8,128)S(1)}, f32[6,1024]{0,1:T(8,128)S(1)}, u32[]{:S(2)}, u32[]{:S(2)}) collective-permute-start(f32[6,1024]{0,1:T(8,128)S(1)} %get-tuple-element.68), channel_id=1, source_target_pairs={{24,0},{0,8},{8,16},{16,24},{25,1},{1,9},{9,17},{17,25},{26,2},{2,... | collective-permute-start | bytes 73736 | tf_op jit(solution)/shard_map/ppermute | solution.py:38
Sparse Core Ops, SparseCore 0:
  94.1 11.6 reduce-scatter.1
where the time goes:
time: 543 us; the launch traced here: 539 us
  local copies, waits for them, and re-layouts  252 us (46%)
  other arithmetic  99.2 us (18%)
  waiting for transfers between devices  63 us (12%)
  matrix products  59.1 us (11%)
  starting transfers between devices  47.2 us (9%)
  between operations  14.5 us (3%)
    gather x1, local copies, waits for them, and re-layouts, body(): void_at = column_void.reshape(-1)[cells]  90.5 us
    scatter-add x1, other arithmetic, body(): jax.ops.segment_sum(volumes, cells, num_segments=size_x * size_y * column_z)  86.1 us
    gather x2, local copies, waits for them, and re-layouts, body(): flow_at = column_flow.reshape(3, -1)[:, cells]  63.2 us
    dot_general x8, matrix products, block_contact(): jnp.einsum('cgj,kgij->ckgi', state_group, picker, precision=lax.Precision...  59.1 us
    scatter x4, local copies, waits for them, and re-layouts, body(): particle_state = particle_state.at[:, departures[slot_row]].set(arrived)  39 us
    ppermute x18, waiting for transfers between devices, with_halo(): lax.ppermute(lax.slice_in_dim(block, 0, width, axis=dim), axis, backward)  29.1 us
    ppermute x18, starting transfers between devices, with_halo(): lax.ppermute(lax.slice_in_dim(block, 0, width, axis=dim), axis, backward)  22.8 us
    ppermute x18, waiting for transfers between devices, with_halo(): lax.ppermute(lax.slice_in_dim(block, block.shape[dim] - width, None, axis...  21.8 us
  transfers between devices with their start and end apart: 41, of which 29 were waited for; matrix products, arithmetic and copies ran while one was open for 20% of the time, Pallas kernels for 0%

commit v1 on v0

v1 whole, which is shorter than its diff:
```python
import functools

import jax
import jax.numpy as jnp
from jax import lax
from jax.experimental import pallas as pl
from jax.experimental.pallas import tpu as pltpu
from jax.sharding import PartitionSpec as P

SWEEPS = 4
PAIRS = 8
BLOCK = 128
LANES = 128
HALO = SWEEPS + 1

TIME_STEP = 0.1
RELAX_RATE = 0.5
DAMPING = 0.5
RANGE_SQUARED = 16.0
GRAVITY = 1.0

F32 = jnp.float32
BF16 = jnp.bfloat16
NT = (((1,), (1,)), ((), ()))


def call(kernel, outs, *args, scratch=(), flops=0, smem=()):
    outs_list = [jax.ShapeDtypeStruct(shape, dtype) for shape, dtype in outs]
    moved = sum(a.size * a.dtype.itemsize for a in list(args) + outs_list)
    vmem = pl.BlockSpec(memory_space=pltpu.VMEM)
    scalar = pl.BlockSpec(memory_space=pltpu.SMEM)
    return pl.pallas_call(
        kernel,
        out_shape=outs_list,
        in_specs=[scalar if i in smem else vmem for i in range(len(args))],
        out_specs=[vmem] * len(outs_list),
        scratch_shapes=list(scratch),
        compiler_params=pltpu.CompilerParams(vmem_limit_bytes=40 * 1024 * 1024),
        cost_estimate=pl.CostEstimate(flops=flops, bytes_accessed=moved, transcendentals=0),
    )(*args)


def split(values):
    high = values.astype(BF16)
    return high, (values - high.astype(F32)).astype(BF16)


def row16(row):
    return jnp.broadcast_to(row, (16, row.shape[1])).astype(BF16)


def counters():
    base = lax.broadcasted_iota(jnp.int32, (16, LANES), 0)
    return [(base + 16 * k).astype(F32).astype(BF16) for k in range(8)]


def one_hot(row, counts, values=None):
    wide = row16(row)
    zero = jnp.zeros((16, LANES), BF16)
    if values is None:
        values = jnp.ones((16, LANES), BF16)
    return jnp.concatenate([jnp.where(wide == c, values, zero) for c in counts], axis=0)


def cell_split(cells, sec):
    high = (cells >> 8) + 64 * (((cells >> 7) & 1) ^ sec)
    return high, cells & (LANES - 1)


def deposit_kernel(sec_ref, vol_ref, cell_ref, p_ref, v_ref, out_ref, hi_ref, lo_ref, va_ref, vb_ref):
    sec = sec_ref[0]
    high, low = cell_split(cell_ref[...], sec)
    hi_ref[...] = high.astype(F32)
    lo_ref[...] = low.astype(F32)
    vol = vol_ref[...]
    part = vol.astype(BF16).astype(F32)
    va_ref[...] = part
    vb_ref[...] = vol - part
    counts = counters()
    rows_each = 16
    steps = vol_ref.shape[0] // rows_each

    def step(i, acc):
        lefts, rights = [], []
        for r in range(rows_each):
            at = pl.ds(i * rows_each + r, 1)
            lefts.append(one_hot(hi_ref[at, :], counts))
            low_row = row16(lo_ref[at, :])
            zero = jnp.zeros((16, LANES), BF16)
            va, vb = row16(va_ref[at, :]), row16(vb_ref[at, :])
            hits = [low_row == c for c in counts]
            rights.append(
                jnp.concatenate(
                    [jnp.where(h, va, zero) for h in hits] + [jnp.where(h, vb, zero) for h in hits],
                    axis=0,
                )
            )
        left = jnp.concatenate(lefts, axis=1)
        right = jnp.concatenate(rights, axis=1)
        return acc + lax.dot_general(left, right, NT, preferred_element_type=F32)

    acc = lax.fori_loop(0, steps, step, jnp.zeros((LANES, 2 * LANES), F32))
    out_ref[0:128, :] = acc[:, :LANES] + acc[:, LANES:]
    out_ref[128:192, :] = p_ref[...].reshape(64, LANES)
    out_ref[192:384, :] = v_ref[...].reshape(192, LANES)


def contact_kernel(vol_ref, pos_ref, vel_ref, pair_ref, base_ref):
    blocks = pos_ref.shape[1] // BLOCK
    base_ref[6] = RELAX_RATE * jnp.exp((-2.0 / 3.0) * jnp.log(vol_ref[...]))

    def step(b, carry):
        at = pl.ds(pl.multiple_of(b * BLOCK, BLOCK), BLOCK)
        index = pair_ref[:, at]
        mine = [pos_ref[d : d + 1, at] for d in range(3)] + [vel_ref[d : d + 1, at] for d in range(3)]
        wide = [jnp.broadcast_to(m, (PAIRS, BLOCK)) for m in mine]
        other = [jnp.take_along_axis(w, index, axis=1, mode="promise_in_bounds") for w in wide]
        apart = [wide[d] - other[d] for d in range(3)]
        dist = apart[0] * apart[0] + apart[1] * apart[1] + apart[2] * apart[2]
        weight = 1.0 / (1.0 + dist * (1.0 / RANGE_SQUARED))
        for d in range(3):
            push = weight * (apart[d] + DAMPING * (other[3 + d] - wide[3 + d]))
            force = jnp.sum(push, axis=0, keepdims=True)
            if d == 0:
                force = force - GRAVITY
            base_ref[d, pl.ds(b, 1), :] = mine[d]
            base_ref[3 + d, pl.ds(b, 1), :] = mine[3 + d] + TIME_STEP * force
        return carry

    lax.fori_loop(0, blocks, step, 0, unroll=4)


def table_of(fields, table_ref):
    for f, values in enumerate(fields):
        high, low = split(jnp.swapaxes(values, 0, 1))
        table_ref[f * LANES : (f + 1) * LANES, :LANES] = high
        table_ref[f * LANES : (f + 1) * LANES, LANES:] = low


def pick(table_ref, fields, high_rows, low_rows, counts):
    hot = jnp.concatenate([one_hot(row, counts) for row in high_rows], axis=1)
    hot = jnp.concatenate([hot, hot], axis=0)
    lane = lax.broadcasted_iota(jnp.int32, (LANES, LANES), 0).astype(F32)
    hits = [jnp.broadcast_to(row, (LANES, LANES)) == lane for row in low_rows]
    found = []
    for f in range(fields):
        rows = jnp.dot(table_ref[f * LANES : (f + 1) * LANES, :], hot, preferred_element_type=F32)
        found.append(
            [
                jnp.sum(jnp.where(hit, rows[:, LANES * h : LANES * (h + 1)], 0.0), axis=0, keepdims=True)
                for h, hit in enumerate(hits)
            ]
        )
    return found


def leave_kernel(sec_ref, base_ref, cell_ref, dep_ref, out_ref, mask_ref, hi_ref, lo_ref, table_ref):
    sec = sec_ref[0]
    high, low = cell_split(cell_ref[...], sec)
    cell = (high * LANES + low).astype(F32)
    table_of([base_ref[f] for f in range(7)] + [cell], table_ref)
    dep = dep_ref[...]
    hi_ref[...] = (dep >> 7).astype(F32)
    lo_ref[...] = (dep & (LANES - 1)).astype(F32)
    counts = counters()
    mask = jnp.zeros((LANES, LANES), F32)
    movers = dep_ref.shape[1]
    for r in range(4):

        def step(i, mask):
            ats = [pl.ds(pl.multiple_of(i * 256 + 128 * h, 128), 128) for h in range(2)]
            his = [hi_ref[r : r + 1, at] for at in ats]
            los = [lo_ref[r : r + 1, at] for at in ats]
            found = pick(table_ref, 8, his, los, counts)
            for f in range(8):
                for h in range(2):
                    out_ref[f, pl.ds(r * (movers // LANES) + i * 2 + h, 1), :] = found[f][h]
            left = jnp.concatenate([one_hot(row, counts) for row in his], axis=1)
            right = jnp.concatenate([one_hot(row, counts) for row in los], axis=1)
            return mask + lax.dot_general(left, right, NT, preferred_element_type=F32)

        mask = lax.fori_loop(0, movers // 256, step, mask)
    mask_ref[...] = mask


def tile_kernel(mine_ref, got_ref, tile_ref, up_ref, down_ref):
    own = mine_ref[0:64, :] + got_ref[64:128, :]
    far = mine_ref[64:128, :] + got_ref[0:64, :]
    tile_ref[0] = 1.0 / (1.0 + own)
    tile_ref[1] = 1.0 / (1.0 + far)
    for f in range(4):
        tile_ref[2 + 2 * f] = mine_ref[128 + 64 * f : 192 + 64 * f, :]
        tile_ref[3 + 2 * f] = got_ref[128 + 64 * f : 192 + 64 * f, :]
    for g in range(10):
        for j in range(HALO):
            up_ref[g, 8 * j : 8 * j + 8, :] = tile_ref[g, pl.ds(8 - HALO + j, 8, stride=8), :]
            down_ref[g, 8 * j : 8 * j + 8, :] = tile_ref[g, pl.ds(j, 8, stride=8), :]


def side_kernel(tile_ref, low_ref, high_ref, up_ref, down_ref):
    for g in range(10):
        for x in range(8):
            slab = jnp.concatenate(
                [
                    low_ref[g, pl.ds(8 + x, 4, stride=8), :],
                    tile_ref[g, 8 * x : 8 * x + 8, :],
                    high_ref[g, pl.ds(x, 4, stride=8), :],
                ],
                axis=0,
            )
            if x >= 8 - HALO:
                at = x - (8 - HALO)
                up_ref[g, 16 * at : 16 * at + 16, :] = slab
            if x < HALO:
                down_ref[g, 16 * x : 16 * x + 16, :] = slab


def fluid_kernel(
    tile_ref, ylow_ref, yhigh_ref, xlow_ref, xhigh_ref, leave_ref,
    p_out_ref, v_out_ref, table_ref, sent_ref,
    grid_ref, other_ref, invd_ref, div_ref, face_ref,
):
    size = 8 + 2 * HALO
    for f in range(5):
        for h in range(2):
            g = 2 * f + h
            lanes = slice(LANES * h, LANES * (h + 1))
            for j in range(HALO):
                grid_ref[f, j, 0:16, lanes] = xlow_ref[g, 16 * j : 16 * j + 16, :]
                grid_ref[f, j, 16:24, lanes] = jnp.ones((8, LANES), F32)
                grid_ref[f, 8 + HALO + j, 0:16, lanes] = xhigh_ref[g, 16 * j : 16 * j + 16, :]
                grid_ref[f, 8 + HALO + j, 16:24, lanes] = jnp.ones((8, LANES), F32)
            for x in range(8):
                grid_ref[f, HALO + x, 0:24, lanes] = jnp.concatenate(
                    [
                        ylow_ref[g, pl.ds(8 + x, 4, stride=8), :],
                        tile_ref[g, 8 * x : 8 * x + 8, :],
                        yhigh_ref[g, pl.ds(x, 5, stride=8), :],
                        jnp.ones((6, LANES), F32),
                        ylow_ref[g, x : x + 1, :],
                    ],
                    axis=0,
                )

    def around(values):
        return (
            pltpu.roll(values, 23, 0),
            pltpu.roll(values, 1, 0),
            pltpu.roll(values, 255, 1),
            pltpu.roll(values, 1, 1),
        )

    def setup(x, carry):
        void = grid_ref[0, x]
        above, below = grid_ref[0, x + 1], grid_ref[0, x - 1]
        sides = around(void)
        total = 6.0 * void + above + below
        for k in range(4):
            total = total + sides[k]
            face_ref[k, x] = void + sides[k]
        invd_ref[x] = 1.0 / total
        ys = around(void * grid_ref[3, x])
        zs = around(void * grid_ref[4, x])
        div_ref[x] = (
            above * grid_ref[2, x + 1] - below * grid_ref[2, x - 1] + ys[0] - ys[1] + zs[2] - zs[3]
        )
        return carry

    lax.fori_loop(1, size - 1, setup, 0)

    for t in range(SWEEPS):
        source = grid_ref.at[1] if t % 2 == 0 else other_ref
        target = other_ref if t % 2 == 0 else grid_ref.at[1]

        def sweep(x, carry):
            void = grid_ref[0, x]
            sides = around(source[x])
            total = (void + grid_ref[0, x + 1]) * source[x + 1] - div_ref[x]
            total = total + (void + grid_ref[0, x - 1]) * source[x - 1]
            for k in range(4):
                total = total + face_ref[k, x] * sides[k]
            target[x] = total * invd_ref[x]
            return carry

        lax.fori_loop(1 + t, size - 1 - t, sweep, 0)

    final = grid_ref.at[1]
    tables = [[], [], [], []]
    for x in range(8):
        values = final[HALO + x]
        sides = around(values)
        flows = (
            grid_ref[2, HALO + x] - 0.5 * (final[HALO + x + 1] - final[HALO + x - 1]),
            grid_ref[3, HALO + x] - 0.5 * (sides[0] - sides[1]),
            grid_ref[4, HALO + x] - 0.5 * (sides[2] - sides[3]),
        )
        p_out_ref[x] = values[4:12, :LANES]
        drag = jnp.exp(-2.65 * jnp.log(grid_ref[0, HALO + x]))[4:12]
        tables[0].append(drag)
        for d in range(3):
            kept = flows[d][4:12]
            v_out_ref[d, x] = kept[:, :LANES]
            tables[1 + d].append(kept)
    fields = []
    for f in range(4):
        whole = jnp.concatenate(tables[f], axis=0)
        fields.append(jnp.concatenate([whole[:, :LANES], whole[:, LANES:]], axis=0))
    table_of(fields, table_ref)

    counts = counters()
    count = leave_ref.shape[1]

    def step(i, carry):
        his, los = [], []
        for h in range(2):
            cell = leave_ref[7, pl.ds(2 * i + h, 1), :].astype(jnp.int32)
            his.append((cell >> 7).astype(F32))
            los.append((cell & (LANES - 1)).astype(F32))
        found = pick(table_ref, 4, his, los, counts)
        for f in range(4):
            for h in range(2):
                sent_ref[f, pl.ds(2 * i + h, 1), :] = found[f][h]
        return carry

    lax.fori_loop(0, count // 2, step, 0)
    drag = TIME_STEP * sent_ref[0] * leave_ref[6]
    scale = 1.0 / (1.0 + drag)
    speeds = [(leave_ref[3 + d] + drag * sent_ref[1 + d]) * scale for d in range(3)]
    for d in range(3):
        sent_ref[3 + d] = speeds[d]
        sent_ref[d] = leave_ref[d] + TIME_STEP * speeds[d]


def main_kernel(sec_ref, table_ref, cell_ref, base_ref, out_ref, hi_ref, lo_ref):
    sec = sec_ref[0]
    high, low = cell_split(cell_ref[...], sec)
    hi_ref[...] = high.astype(F32)
    lo_ref[...] = low.astype(F32)
    counts = counters()
    rows = cell_ref.shape[0]

    def step(i, carry):
        ats = [pl.ds(2 * i + h, 1) for h in range(2)]
        found = pick(table_ref, 4, [hi_ref[at, :] for at in ats], [lo_ref[at, :] for at in ats], counts)
        for f in range(4):
            for h in range(2):
                out_ref[f, ats[h], :] = found[f][h]
        return carry

    lax.fori_loop(0, rows // 2, step, 0)
    drag = TIME_STEP * out_ref[0] * base_ref[6]
    scale = 1.0 / (1.0 + drag)
    speeds = [(base_ref[3 + d] + drag * out_ref[1 + d]) * scale for d in range(3)]
    for d in range(3):
        out_ref[3 + d] = speeds[d]
        out_ref[d] = base_ref[d] + TIME_STEP * speeds[d]


def settle_kernel(
    dep_ref, mask_ref, moved_ref, a_ref, b_ref, c_ref, d_ref, pos_ref, vel_ref,
    hi_ref, lo_ref, left_ref, right_ref, keep_ref,
):
    dep = dep_ref[...]
    hi_ref[...] = (dep >> 7).astype(F32)
    lo_ref[...] = (dep & (LANES - 1)).astype(F32)
    counts = counters()
    movers = dep_ref.shape[1]
    per = movers // LANES
    arrivals = (b_ref, a_ref, d_ref, c_ref)
    for r in range(4):
        for q in range(per):
            left_ref[:, (r * per + q) * LANES : (r * per + q + 1) * LANES] = one_hot(
                hi_ref[r : r + 1, q * LANES : (q + 1) * LANES], counts
            )
    zero = jnp.zeros((16, LANES), BF16)
    for f in range(6):
        for r in range(4):
            for q in range(per):
                value = arrivals[r][f, q : q + 1, :]
                part = value.astype(BF16).astype(F32)
                va, vb = row16(part), row16(value - part)
                low = row16(lo_ref[r : r + 1, q * LANES : (q + 1) * LANES])
                hits = [low == c for c in counts]
                lanes = slice((r * per + q) * LANES, (r * per + q + 1) * LANES)
                right_ref[:, lanes] = jnp.concatenate(
                    [jnp.where(h, va, zero) for h in hits] + [jnp.where(h, vb, zero) for h in hits],
                    axis=0,
                )
        placed = lax.dot_general(left_ref[...], right_ref[...], NT, preferred_element_type=F32)
        placed = placed[:, :LANES] + placed[:, LANES:]
        keep_ref[f] = jnp.where(mask_ref[...] > 0.5, placed, moved_ref[f])

    def spread(b, carry):
        at = pl.ds(pl.multiple_of(b * LANES, LANES), LANES)
        for d in range(3):
            pos_ref[d : d + 1, at] = keep_ref[d, pl.ds(b, 1), :]
            vel_ref[d : d + 1, at] = keep_ref[3 + d, pl.ds(b, 1), :]
        return carry

    lax.fori_loop(0, moved_ref.shape[1], spread, 0, unroll=4)


def shifted(block, axis, distance):
    count = lax.axis_size(axis)
    return lax.ppermute(block, axis, [((i - distance) % count, i) for i in range(count)])


def body(pressure, fluid_velocity, positions, velocities, volumes, cells, partners, departures):
    particles = volumes.shape[0]
    rows = particles // LANES
    movers = departures.shape[1]
    sec = lax.axis_index("sec").astype(jnp.int32).reshape(1)
    vol2 = volumes.reshape(rows, LANES)
    cell2 = cells.reshape(rows, LANES)
    dense = pltpu.VMEM((rows, LANES), F32)

    (mine,) = call(
        deposit_kernel, [((384, LANES), F32)], sec, vol2, cell2, pressure, fluid_velocity,
        scratch=[dense] * 4, smem=(0,), flops=2 * particles * 128 * 256,
    )
    got = shifted(mine, "sec", 1)
    (base,) = call(
        contact_kernel, [((7, rows, LANES), F32)], vol2, positions, velocities, partners,
        flops=particles * 8 * 500,
    )
    tile, up, down = call(
        tile_kernel, [((10, 64, LANES), F32), ((10, 40, LANES), F32), ((10, 40, LANES), F32)], mine, got,
    )
    ylow = shifted(up, "gy", 1)
    yhigh = shifted(down, "gy", -1)
    leave, mask = call(
        leave_kernel, [((8, 4 * movers // LANES, LANES), F32), ((LANES, LANES), F32)],
        sec, base, cell2, departures,
        scratch=[
            pltpu.VMEM((4, movers), F32), pltpu.VMEM((4, movers), F32), pltpu.VMEM((8 * LANES, 2 * LANES), BF16),
        ],
        smem=(0,), flops=2 * 4 * movers * 1024 * 256,
    )
    xup, xdown = call(
        side_kernel, [((10, 80, LANES), F32), ((10, 80, LANES), F32)], tile, ylow, yhigh,
    )
    xlow = shifted(xup, "gx", 1)
    xhigh = shifted(xdown, "gx", -1)
    size = 8 + 2 * HALO
    grid = pltpu.VMEM((size, 24, 2 * LANES), F32)
    p_out, v_out, table, sent = call(
        fluid_kernel,
        [
            (pressure.shape, F32), (fluid_velocity.shape, F32), ((4 * LANES, 2 * LANES), BF16),
            ((6, 4 * movers // LANES, LANES), F32),
        ],
        tile, ylow, yhigh, xlow, xhigh, leave,
        scratch=[pltpu.VMEM((5, size, 24, 2 * LANES), F32), grid, grid, grid, pltpu.VMEM((4, size, 24, 2 * LANES), F32)],
        flops=2 * 4 * movers * 512 * 256,
    )
    per = movers // LANES
    arrived = [
        shifted(sent[:, row * per : (row + 1) * per], axis, offset)
        for row, axis, offset in ((0, "gx", 1), (1, "gx", -1), (2, "gy", 1), (3, "gy", -1))
    ]
    (moved,) = call(
        main_kernel, [((6, rows, LANES), F32)], sec, table, cell2, base,
        scratch=[dense] * 2, smem=(0,), flops=2 * particles * 512 * 256,
    )
    pos_out, vel_out = call(
        settle_kernel, [(positions.shape, F32), (velocities.shape, F32)],
        departures, mask, moved, *arrived,
        scratch=[
            pltpu.VMEM((4, movers), F32), pltpu.VMEM((4, movers), F32),
            pltpu.VMEM((LANES, 4 * movers), BF16), pltpu.VMEM((2 * LANES, 4 * movers), BF16),
            pltpu.VMEM((6, rows, LANES), F32),
        ],
        flops=2 * 4 * movers * 128 * 1536,
    )
    return p_out, v_out, pos_out, vel_out


def solution(mesh):
    placed = (
        P("gx", "gy", "sec"),
        P(None, "gx", "gy", "sec"),
        P(None, ("gx", "gy", "sec")),
        P(None, ("gx", "gy", "sec")),
        P(("gx", "gy", "sec")),
        P(("gx", "gy", "sec")),
        P(None, ("gx", "gy", "sec")),
        P(None, ("gx", "gy", "sec")),
    )
    return jax.shard_map(
        body,
        mesh=mesh,
        in_specs=placed,
        out_specs=(
            P("gx", "gy", "sec"),
            P(None, "gx", "gy", "sec"),
            P(None, ("gx", "gy", "sec")),
            P(None, ("gx", "gy", "sec")),
        ),
        check_vma=False,
    )
```

time: 543 us -> 76.9 us (0.14)
  local copies, waits for them, and re-layouts: 252 us -> 3.36 us
  other arithmetic: 99.2 us -> 0 us
  matrix products: 59.1 us -> 0 us
  waiting for transfers between devices: 63 us -> 13.2 us
  Pallas kernels: 0 us -> 47.3 us
  starting transfers between devices: 47.2 us -> 11.9 us
  between operations: 14.5 us -> 0.79 us
    gather x4 -> x0, local copies, waits for them, and re-layouts: 168 us -> none  [the longest x1 90.5 us: body(): void_at = column_void.reshape(-1)[cells]]
    scatter-add x1 -> x0, other arithmetic: 86.1 us -> none  [body(): jax.ops.segment_sum(volumes, cells, num_segments=size_x * size_y * column_z)]
    dot_general x8 -> x0, matrix products: 59.1 us -> none  [block_contact(): jnp.einsum('cgj,kgij->ckgi', state_group, picker, precision=lax.Precision...]
    ppermute x40 -> x9, waiting for transfers between devices: 61.7 us -> 13.2 us  [shifted(): lax.ppermute(block, axis, [((i - distance) % count, i) for i in range(cou...]
    pallas_call x0 -> x8, Pallas kernels: none -> 47.3 us  [call(): pl.pallas_call(kernel, out_shape=outs_list, in_specs=[scalar if i in smem...]
    scatter x4 -> x0, local copies, waits for them, and re-layouts: 39 us -> none  [body(): particle_state = particle_state.at[:, departures[slot_row]].set(arrived)]
    ppermute x40 -> x9, starting transfers between devices: 47.1 us -> 11.9 us  [shifted(): lax.ppermute(block, axis, [((i - distance) % count, i) for i in range(cou...]
    slice x14 -> x1, local copies, waits for them, and re-layouts: 18.8 us -> 0.01 us  [body(): sent[:, row * per:(row + 1) * per]]
  transfers between devices with their start and end apart: 41 -> 9, of which waited for: 29 -> 3; matrix products, arithmetic and copies ran while one was open for 20% -> 0% of each run, Pallas kernels for 0% -> 34%
where the time goes in v1:
time: 76.9 us; the launch traced here: 76.5 us
  Pallas kernels  47.3 us (62%)
  waiting for transfers between devices  13.2 us (17%)
  starting transfers between devices  11.9 us (15%)
  local copies, waits for them, and re-layouts  3.36 us (4%)
  between operations  0.79 us (1%)
    pallas_call x8, Pallas kernels, call(): pl.pallas_call(kernel, out_shape=outs_list, in_specs=[scalar if i in smem...  47.3 us
    ppermute x9, waiting for transfers between devices, shifted(): lax.ppermute(block, axis, [((i - distance) % count, i) for i in range(cou...  13.2 us
    ppermute x9, starting transfers between devices, shifted(): lax.ppermute(block, axis, [((i - distance) % count, i) for i in range(cou...  11.9 us
    unnamed x20, local copies, waits for them, and re-layouts  3.35 us
  transfers between devices with their start and end apart: 9, of which 3 were waited for; matrix products, arithmetic and copies ran while one was open for 0% of the time, Pallas kernels for 34%

profile of v1, /device:TPU:1, one launch (start us, length us, event | category | flops | bytes accessed | tf_op | source)
XLA Modules:
  0.0 76.5 jit_solution(7841791934563620492)
XLA Ops:
  0.6 0.0 copy-start.3
  0.6 0.8 %copy-done.3 = f32[16384]{0:T(1024)S(1)} copy-done((f32[16384]{0:T(1024)S(1)}, f32[16384]{0:T(1024)}, u32[]{:S(2)}) %copy-start.3) | copy-done | bytes 65560
  1.5 0.0 copy-start.5
  1.5 0.9 %copy-done.5 = f32[3,8,8,128]{3,2,1,0:T(8,128)S(1)} copy-done((f32[3,8,8,128]{3,2,1,0:T(8,128)S(1)}, f32[3,8,8,128]{3,2,1,0:T(8,128)}, u32[]{:S(2)}) %copy-start.5) | copy-done | bytes 98328
  2.4 0.0 copy-start.6
  2.4 0.8 %copy-done.6 = s32[16384]{0:T(1024)S(1)} copy-done((s32[16384]{0:T(1024)S(1)}, s32[16384]{0:T(1024)}, u32[]{:S(2)}) %copy-start.6) | copy-done | bytes 65560
  3.2 0.0 copy-start.8
  3.2 0.8 copy-done.8
  4.0 3.9 %shard_map.111.mine_ref = f32[384,128]{1,0:T(8,128)S(1)} custom-call(s32[1]{0:T(128)} %bitcast.sec_ref, f32[128,128]{1,0:T(8,128)S(1)} %bitcast.3, s32[128,128]{1,0:T(8,128)S(1)} %bitcast.5, f32[8,8,128]{2,1,0:T(8,128)S(1)} %copy-done.8, f32[3,8,8,128]{3,2,1,0:T(8,128)S(1)} %copy-done.5), custom_call_target="tpu_custom_call" | custom-call | flops 1073741824 | bytes 458756 | tf_op jit(solution)/shard_map/pallas_call | solution.py:32
  7.9 0.0 copy-start
  7.9 2.1 %collective-permute-start = (f32[384,128]{1,0:T(8,128)S(1)}, f32[384,128]{1,0:T(8,128)S(1)}, u32[]{:S(2)}, u32[]{:S(2)}) collective-permute-start(f32[384,128]{1,0:T(8,128)S(1)} %shard_map.111.mine_ref), channel_id=1, source_target_pairs={{1,0},{0,1},{3,2},{2,3},{5,4},{4,5},{7,6},{6,7},{9,8},{8,9},{11,10... | collective-permute-start | bytes 589832 | tf_op jit(solution)/shard_map/ppermute | solution.py:405
  10.0 4.6 %collective-permute-done.got_ref = f32[384,128]{1,0:T(8,128)S(1)} collective-permute-done((f32[384,128]{1,0:T(8,128)S(1)}, f32[384,128]{1,0:T(8,128)S(1)}, u32[]{:S(2)}, u32[]{:S(2)}) %collective-permute-start) | collective-permute-done | bytes 196640 | tf_op jit(solution)/shard_map/ppermute | solution.py:405
  14.6 0.1 shard_map.112
  14.7 1.2 %collective-permute-start.1 = (f32[10,40,128]{2,1,0:T(8,128)S(1)}, f32[10,40,128]{2,1,0:T(8,128)S(1)}, u32[]{:S(2)}, u32[]{:S(2)}) collective-permute-start(f32[10,40,128]{2,1,0:T(8,128)S(1)} %get-tuple-element.18), channel_id=1, source_target_pairs={{6,0},{0,2},{2,4},{4,6},{7,1},{1,3},{3,5},{5,7},{14,8},{8,10},{10,... | collective-permute-start | bytes 614408 | tf_op jit(solution)/shard_map/ppermute | solution.py:405
  16.0 2.1 %collective-permute-start.2 = (f32[10,40,128]{2,1,0:T(8,128)S(1)}, f32[10,40,128]{2,1,0:T(8,128)S(1)}, u32[]{:S(2)}, u32[]{:S(2)}) collective-permute-start(f32[10,40,128]{2,1,0:T(8,128)S(1)} %get-tuple-element.19), channel_id=1, source_target_pairs={{2,0},{4,2},{6,4},{0,6},{3,1},{5,3},{7,5},{1,7},{10,8},{12,10},{14... | collective-permute-start | bytes 614408 | tf_op jit(solution)/shard_map/ppermute | solution.py:405
  18.1 3.9 %collective-permute-done.1.low_ref.ylow_ref = f32[10,40,128]{2,1,0:T(8,128)S(1)} collective-permute-done((f32[10,40,128]{2,1,0:T(8,128)S(1)}, f32[10,40,128]{2,1,0:T(8,128)S(1)}, u32[]{:S(2)}, u32[]{:S(2)}) %collective-permute-start.1) | collective-permute-done | bytes 204832 | tf_op jit(solution)/shard_map/ppermute | solution.py:405
  22.0 4.7 %collective-permute-done.2.high_ref.yhigh_ref = f32[10,40,128]{2,1,0:T(8,128)S(1)} collective-permute-done((f32[10,40,128]{2,1,0:T(8,128)S(1)}, f32[10,40,128]{2,1,0:T(8,128)S(1)}, u32[]{:S(2)}, u32[]{:S(2)}) %collective-permute-start.2) | collective-permute-done | bytes 204832 | tf_op jit(solution)/shard_map/ppermute | solution.py:405
  26.6 0.0 copy-start.1
  26.6 0.0 copy-start.2
  26.6 0.0 copy-start.4
  26.6 0.1 shard_map.113
  26.7 2.4 %collective-permute-start.3 = (f32[10,80,128]{2,1,0:T(8,128)S(1)}, f32[10,80,128]{2,1,0:T(8,128)S(1)}, u32[]{:S(2)}, u32[]{:S(2)}) collective-permute-start(f32[10,80,128]{2,1,0:T(8,128)S(1)} %get-tuple-element.20), channel_id=1, source_target_pairs={{24,0},{0,8},{8,16},{16,24},{25,1},{1,9},{9,17},{17,25},{26,2},{2,... | collective-permute-start | bytes 1228808 | tf_op jit(solution)/shard_map/ppermute | solution.py:405
  29.1 0.0 copy-start.7
  29.1 0.0 copy-start.9
  29.1 0.0 collective-permute-start.4
  29.1 0.0 copy-done
  29.1 0.0 copy-done.1
  29.1 0.0 copy-done.2
  29.1 0.0 copy-done.4
  29.2 4.5 %shard_map.114.base_ref = f32[7,128,128]{2,1,0:T(8,128)S(1)} custom-call(f32[128,128]{1,0:T(8,128)S(1)} %bitcast.4, f32[3,16384]{1,0:T(4,128)S(1)} %copy-done.1, f32[3,16384]{1,0:T(4,128)S(1)} %copy-done.2, s32[8,16384]{1,0:T(8,128)S(1)} %copy-done), custom_call_target="tpu_custom_call" | custom-call | flops 65536000 | bytes 1441792 | tf_op jit(solution)/shard_map/pallas_call | solution.py:32
  33.7 0.0 copy-done.7
  33.7 0.0 copy-done.9
  33.7 5.6 %shard_map.115 = (f32[8,32,128]{2,1,0:T(8,128)S(1)}, f32[128,128]{1,0:T(8,128)S(1)}) custom-call(s32[1]{0:T(128)} %bitcast.sec_ref, f32[7,128,128]{2,1,0:T(8,128)S(1)} %shard_map.114.base_ref, s32[128,128]{1,0:T(8,128)S(1)} %bitcast.6, s32[4,1024]{1,0:T(4,128)S(1)} %copy-done.9), custom_call_target="tpu_custom_call" | custom-call | flops 2147483648 | bytes 737284 | tf_op jit(solution)/shard_map/pallas_call | solution.py:32
  39.3 0.0 collective-permute-done.3.xlow_ref
  39.3 0.0 collective-permute-done.4.xhigh_ref
  39.3 11.0 %shard_map.116 = (f32[8,8,128]{2,1,0:T(8,128)}, f32[3,8,8,128]{3,2,1,0:T(8,128)}, bf16[512,256]{1,0:T(8,128)(2,1)S(1)}, f32[6,32,128]{2,1,0:T(8,128)S(1)}) custom-call(f32[10,64,128]{2,1,0:T(8,128)S(1)} %get-tuple-element.17.tile_ref, f32[10,40,128]{2,1,0:T(8,128)S(1)} %collective-permute-done.1.low_ref.ylow_ref, ...), custom_call_target="tpu_custom_call" | custom-call | flops 1073741824 | bytes 2179072 | tf_op jit(solution)/shard_map/pallas_call | solution.py:32
  50.3 2.0 %collective-permute-start.8 = (f32[6,8,128]{2,1,0:T(8,128)S(1)}, f32[6,8,128]{2,1,0:T(8,128)S(1)}, u32[]{:S(2)}, u32[]{:S(2)}) collective-permute-start(f32[6,8,128]{2,1,0:T(8,128)S(1)} %get-tuple-element.30), channel_id=1, source_target_pairs={{2,0},{4,2},{6,4},{0,6},{3,1},{5,3},{7,5},{1,7},{10,8},{12,10},{14... | collective-permute-start | bytes 73736 | tf_op jit(solution)/shard_map/ppermute | solution.py:405
  52.4 0.0 collective-permute-start.7
  52.4 0.9 %collective-permute-start.6 = (f32[6,8,128]{2,1,0:T(8,128)S(1)}, f32[6,8,128]{2,1,0:T(8,128)S(1)}, u32[]{:S(2)}, u32[]{:S(2)}) collective-permute-start(f32[6,8,128]{2,1,0:T(8,128)S(1)} %get-tuple-element.32), channel_id=1, source_target_pairs={{8,0},{16,8},{24,16},{0,24},{9,1},{17,9},{25,17},{1,25},{10,2},{18... | collective-permute-start | bytes 73736 | tf_op jit(solution)/shard_map/ppermute | solution.py:405
  53.3 1.1 %collective-permute-start.5 = (f32[6,8,128]{2,1,0:T(8,128)S(1)}, f32[6,8,128]{2,1,0:T(8,128)S(1)}, u32[]{:S(2)}, u32[]{:S(2)}) collective-permute-start(f32[6,8,128]{2,1,0:T(8,128)S(1)} %get-tuple-element.33), channel_id=1, source_target_pairs={{24,0},{0,8},{8,16},{16,24},{25,1},{1,9},{9,17},{17,25},{26,2},{2,... | collective-permute-start | bytes 73736 | tf_op jit(solution)/shard_map/ppermute | solution.py:405
  54.4 15.7 %shard_map.117.moved_ref = f32[6,128,128]{2,1,0:T(8,128)S(1)} custom-call(s32[1]{0:T(128)} %bitcast.sec_ref, bf16[512,256]{1,0:T(8,128)(2,1)S(1)} %get-tuple-element.26.table_ref, s32[128,128]{1,0:T(8,128)S(1)} %bitcast.7, f32[7,128,128]{2,1,0:T(8,128)S(1)} %shard_map.114.base_ref), custom_call_target="tpu_custom_call" | custom-call | flops 4294967296 | bytes 1179652 | tf_op jit(solution)/shard_map/pallas_call | solution.py:32
  70.1 0.0 collective-permute-done.8.d_ref
  70.1 0.0 collective-permute-done.7.c_ref
  70.1 0.0 collective-permute-done.6.b_ref
  70.1 0.0 collective-permute-done.5.a_ref
  70.2 6.4 %shard_map.118 = (f32[3,16384]{1,0:T(4,128)}, f32[3,16384]{1,0:T(4,128)}) custom-call(s32[4,1024]{1,0:T(4,128)S(1)} %copy-done.9, f32[128,128]{1,0:T(8,128)S(1)} %get-tuple-element.25.mask_ref, f32[6,128,128]{2,1,0:T(8,128)S(1)} %shard_map.117.moved_ref, f32[6,8,128]{2,1,0:T(8,128)S(1)} %collective-permute-done.5.a_ref, ...), custom_call_target="tpu_custom_call" | custom-call | flops 1610612736 | bytes 966656 | tf_op jit(solution)/shard_map/pallas_call | solution.py:32
  (1 shorter events, 0.0 us)
Async XLA Ops:
  0.6 0.8 %copy-start.3 = (f32[16384]{0:T(1024)S(1)}, f32[16384]{0:T(1024)}, u32[]{:S(2)}) copy-start(f32[16384]{0:T(1024)} %param.12) | copy-start | bytes 196612
  1.5 0.9 %copy-start.5 = (f32[3,8,8,128]{3,2,1,0:T(8,128)S(1)}, f32[3,8,8,128]{3,2,1,0:T(8,128)}, u32[]{:S(2)}) copy-start(f32[3,8,8,128]{3,2,1,0:T(8,128)} %v_ref.1) | copy-start | bytes 294916
  2.4 0.8 %copy-start.6 = (s32[16384]{0:T(1024)S(1)}, s32[16384]{0:T(1024)}, u32[]{:S(2)}) copy-start(s32[16384]{0:T(1024)} %param.13) | copy-start | bytes 196612
  3.2 0.8 copy-start.8
  7.9 21.3 %copy-start = (s32[8,16384]{1,0:T(8,128)S(1)}, s32[8,16384]{1,0:T(8,128)}, u32[]{:S(2)}) copy-start(s32[8,16384]{1,0:T(8,128)} %pair_ref.1) | copy-start | bytes 1572868
  7.9 6.8 %collective-permute-start = (f32[384,128]{1,0:T(8,128)S(1)}, f32[384,128]{1,0:T(8,128)S(1)}, u32[]{:S(2)}, u32[]{:S(2)}) collective-permute-start(f32[384,128]{1,0:T(8,128)S(1)} %shard_map.111.mine_ref), channel_id=1, source_target_pairs={{1,0},{0,1},{3,2},{2,3},{5,4},{4,5},{7,6},{6,7},{9,8},{8,9},{11,10... | collective-permute-start | bytes 589832 | tf_op jit(solution)/shard_map/ppermute | solution.py:405
  14.7 7.2 %collective-permute-start.1 = (f32[10,40,128]{2,1,0:T(8,128)S(1)}, f32[10,40,128]{2,1,0:T(8,128)S(1)}, u32[]{:S(2)}, u32[]{:S(2)}) collective-permute-start(f32[10,40,128]{2,1,0:T(8,128)S(1)} %get-tuple-element.18), channel_id=1, source_target_pairs={{6,0},{0,2},{2,4},{4,6},{7,1},{1,3},{3,5},{5,7},{14,8},{8,10},{10,... | collective-permute-start | bytes 614408 | tf_op jit(solution)/shard_map/ppermute | solution.py:405
  16.0 10.7 %collective-permute-start.2 = (f32[10,40,128]{2,1,0:T(8,128)S(1)}, f32[10,40,128]{2,1,0:T(8,128)S(1)}, u32[]{:S(2)}, u32[]{:S(2)}) collective-permute-start(f32[10,40,128]{2,1,0:T(8,128)S(1)} %get-tuple-element.19), channel_id=1, source_target_pairs={{2,0},{4,2},{6,4},{0,6},{3,1},{5,3},{7,5},{1,7},{10,8},{12,10},{14... | collective-permute-start | bytes 614408 | tf_op jit(solution)/shard_map/ppermute | solution.py:405
  26.6 2.5 %copy-start.1 = (f32[3,16384]{1,0:T(4,128)S(1)}, f32[3,16384]{1,0:T(4,128)}, u32[]{:S(2)}) copy-start(f32[3,16384]{1,0:T(4,128)} %pos_ref.1) | copy-start | bytes 589828
  26.6 2.5 %copy-start.2 = (f32[3,16384]{1,0:T(4,128)S(1)}, f32[3,16384]{1,0:T(4,128)}, u32[]{:S(2)}) copy-start(f32[3,16384]{1,0:T(4,128)} %vel_ref.1) | copy-start | bytes 589828
  26.6 2.5 %copy-start.4 = (f32[16384]{0:T(1024)S(1)}, f32[16384]{0:T(1024)}, u32[]{:S(2)}) copy-start(f32[16384]{0:T(1024)} %param.12) | copy-start | bytes 196612
  26.7 12.6 %collective-permute-start.3 = (f32[10,80,128]{2,1,0:T(8,128)S(1)}, f32[10,80,128]{2,1,0:T(8,128)S(1)}, u32[]{:S(2)}, u32[]{:S(2)}) collective-permute-start(f32[10,80,128]{2,1,0:T(8,128)S(1)} %get-tuple-element.20), channel_id=1, source_target_pairs={{24,0},{0,8},{8,16},{16,24},{25,1},{1,9},{9,17},{17,25},{26,2},{2,... | collective-permute-start | bytes 1228808 | tf_op jit(solution)/shard_map/ppermute | solution.py:405
  29.1 4.6 %copy-start.7 = (s32[16384]{0:T(1024)S(1)}, s32[16384]{0:T(1024)}, u32[]{:S(2)}) copy-start(s32[16384]{0:T(1024)} %param.13) | copy-start | bytes 196612
  29.1 4.6 %copy-start.9 = (s32[4,1024]{1,0:T(4,128)S(1)}, s32[4,1024]{1,0:T(4,128)}, u32[]{:S(2)}) copy-start(s32[4,1024]{1,0:T(4,128)} %dep_ref.3) | copy-start | bytes 49156
  29.1 10.2 %collective-permute-start.4 = (f32[10,80,128]{2,1,0:T(8,128)S(1)}, f32[10,80,128]{2,1,0:T(8,128)S(1)}, u32[]{:S(2)}, u32[]{:S(2)}) collective-permute-start(f32[10,80,128]{2,1,0:T(8,128)S(1)} %get-tuple-element.21), channel_id=1, source_target_pairs={{8,0},{16,8},{24,16},{0,24},{9,1},{17,9},{25,17},{1,25},{10,2},{18... | collective-permute-start | bytes 1228808 | tf_op jit(solution)/shard_map/ppermute | solution.py:405
  50.3 19.8 %collective-permute-start.8 = (f32[6,8,128]{2,1,0:T(8,128)S(1)}, f32[6,8,128]{2,1,0:T(8,128)S(1)}, u32[]{:S(2)}, u32[]{:S(2)}) collective-permute-start(f32[6,8,128]{2,1,0:T(8,128)S(1)} %get-tuple-element.30), channel_id=1, source_target_pairs={{2,0},{4,2},{6,4},{0,6},{3,1},{5,3},{7,5},{1,7},{10,8},{12,10},{14... | collective-permute-start | bytes 73736 | tf_op jit(solution)/shard_map/ppermute | solution.py:405
  52.4 17.8 %collective-permute-start.7 = (f32[6,8,128]{2,1,0:T(8,128)S(1)}, f32[6,8,128]{2,1,0:T(8,128)S(1)}, u32[]{:S(2)}, u32[]{:S(2)}) collective-permute-start(f32[6,8,128]{2,1,0:T(8,128)S(1)} %get-tuple-element.31), channel_id=1, source_target_pairs={{6,0},{0,2},{2,4},{4,6},{7,1},{1,3},{3,5},{5,7},{14,8},{8,10},{10,... | collective-permute-start | bytes 73736 | tf_op jit(solution)/shard_map/ppermute | solution.py:405
  52.4 17.8 %collective-permute-start.6 = (f32[6,8,128]{2,1,0:T(8,128)S(1)}, f32[6,8,128]{2,1,0:T(8,128)S(1)}, u32[]{:S(2)}, u32[]{:S(2)}) collective-permute-start(f32[6,8,128]{2,1,0:T(8,128)S(1)} %get-tuple-element.32), channel_id=1, source_target_pairs={{8,0},{16,8},{24,16},{0,24},{9,1},{17,9},{25,17},{1,25},{10,2},{18... | collective-permute-start | bytes 73736 | tf_op jit(solution)/shard_map/ppermute | solution.py:405
  53.3 16.8 %collective-permute-start.5 = (f32[6,8,128]{2,1,0:T(8,128)S(1)}, f32[6,8,128]{2,1,0:T(8,128)S(1)}, u32[]{:S(2)}, u32[]{:S(2)}) collective-permute-start(f32[6,8,128]{2,1,0:T(8,128)S(1)} %get-tuple-element.33), channel_id=1, source_target_pairs={{24,0},{0,8},{8,16},{16,24},{25,1},{1,9},{9,17},{17,25},{26,2},{2,... | collective-permute-start | bytes 73736 | tf_op jit(solution)/shard_map/ppermute | solution.py:405

commit v2 on v1

v2 whole, which is shorter than its diff:
```python
import jax
import jax.numpy as jnp
from jax import lax
from jax.experimental import pallas as pl
from jax.experimental.pallas import tpu as pltpu
from jax.sharding import PartitionSpec as P

SWEEPS = 4
PAIRS = 8
BLOCK = 128
LANES = 128
HALO = SWEEPS + 1

TIME_STEP = 0.1
RELAX_RATE = 0.5
DAMPING = 0.5
RANGE_SQUARED = 16.0
GRAVITY = 1.0

F32 = jnp.float32
BF16 = jnp.bfloat16
NT = (((1,), (1,)), ((), ()))


def call(kernel, outs, *args, scratch=(), busy_us=0.1, smem=(), loose=()):
    outs_list = [jax.ShapeDtypeStruct(shape, dtype) for shape, dtype in outs]
    vmem = pl.BlockSpec(memory_space=pltpu.VMEM)
    scalar = pl.BlockSpec(memory_space=pltpu.SMEM)
    anywhere = pl.BlockSpec(memory_space=pl.ANY)
    specs = [scalar if i in smem else anywhere if i in loose else vmem for i in range(len(args))]
    return pl.pallas_call(
        kernel,
        out_shape=outs_list,
        in_specs=specs,
        out_specs=[vmem] * len(outs_list),
        scratch_shapes=list(scratch),
        compiler_params=pltpu.CompilerParams(vmem_limit_bytes=24 * 1024 * 1024),
        cost_estimate=pl.CostEstimate(flops=int(busy_us * 1.15e9), bytes_accessed=4096, transcendentals=0),
    )(*args)


def split(values):
    high = values.astype(BF16)
    return high, (values - high.astype(F32)).astype(BF16)


def row16(row):
    return jnp.broadcast_to(row, (16, row.shape[1])).astype(BF16)


def counters():
    base = lax.broadcasted_iota(jnp.int32, (16, LANES), 0)
    return [(base + 16 * k).astype(F32).astype(BF16) for k in range(8)]


def one_hot(row, counts, values=None):
    wide = row16(row)
    zero = jnp.zeros((16, LANES), BF16)
    if values is None:
        values = jnp.ones((16, LANES), BF16)
    return jnp.concatenate([jnp.where(wide == c, values, zero) for c in counts], axis=0)


def cell_split(cells, sec):
    high = (cells >> 8) + 64 * (((cells >> 7) & 1) ^ sec)
    return high, cells & (LANES - 1)


def deposit_kernel(
    sec_ref, vol_in, cell_in, out_ref, vol_ref, cell_ref, hi_ref, lo_ref, va_ref, vb_ref, sems,
):
    copies = [
        pltpu.make_async_copy(vol_in, vol_ref, sems.at[0]),
        pltpu.make_async_copy(cell_in, cell_ref, sems.at[1]),
    ]
    for copy in copies:
        copy.start()
    for copy in copies:
        copy.wait()
    sec = sec_ref[0]
    high, low = cell_split(cell_ref[...], sec)
    hi_ref[...] = high.astype(F32)
    lo_ref[...] = low.astype(F32)
    vol = vol_ref[...]
    part = vol.astype(BF16).astype(F32)
    va_ref[...] = part
    vb_ref[...] = vol - part
    counts = counters()
    zero = jnp.zeros((16, LANES), BF16)
    rows_each = 16
    steps = vol_ref.shape[0] // rows_each

    def step(i, acc):
        lefts, rights = [], []
        for r in range(rows_each):
            at = pl.ds(i * rows_each + r, 1)
            lefts.append(one_hot(hi_ref[at, :], counts))
            low_row = row16(lo_ref[at, :])
            va, vb = row16(va_ref[at, :]), row16(vb_ref[at, :])
            hits = [low_row == c for c in counts]
            rights.append(
                jnp.concatenate(
                    [jnp.where(h, va, zero) for h in hits] + [jnp.where(h, vb, zero) for h in hits],
                    axis=0,
                )
            )
        left = jnp.concatenate(lefts, axis=1)
        right = jnp.concatenate(rights, axis=1)
        return acc + lax.dot_general(left, right, NT, preferred_element_type=F32)

    acc = lax.fori_loop(0, steps, step, jnp.zeros((LANES, 2 * LANES), F32), unroll=2)
    out_ref[...] = acc[:, :LANES] + acc[:, LANES:]


def contact_kernel(vol_ref, pos_ref, vel_ref, pair_ref, after_ref, base_ref):
    blocks = pos_ref.shape[1] // BLOCK
    base_ref[6] = RELAX_RATE * jnp.exp((-2.0 / 3.0) * jnp.log(vol_ref[...]))

    def step(b, carry):
        at = pl.ds(pl.multiple_of(b * BLOCK, BLOCK), BLOCK)
        index = pair_ref[:, at]
        mine = [pos_ref[d : d + 1, at] for d in range(3)] + [vel_ref[d : d + 1, at] for d in range(3)]
        wide = [jnp.broadcast_to(m, (PAIRS, BLOCK)) for m in mine]
        other = [jnp.take_along_axis(w, index, axis=1, mode="promise_in_bounds") for w in wide]
        apart = [wide[d] - other[d] for d in range(3)]
        dist = apart[0] * apart[0] + apart[1] * apart[1] + apart[2] * apart[2]
        weight = 1.0 / (1.0 + dist * (1.0 / RANGE_SQUARED))
        for d in range(3):
            push = weight * (apart[d] + DAMPING * (other[3 + d] - wide[3 + d]))
            force = jnp.sum(push, axis=0, keepdims=True)
            if d == 0:
                force = force - GRAVITY
            base_ref[d, pl.ds(b, 1), :] = mine[d]
            base_ref[3 + d, pl.ds(b, 1), :] = mine[3 + d] + TIME_STEP * force
        return carry

    lax.fori_loop(0, blocks, step, 0, unroll=8)


def table_of(fields, table_ref):
    for f, values in enumerate(fields):
        high, low = split(jnp.swapaxes(values, 0, 1))
        table_ref[f * LANES : (f + 1) * LANES, :LANES] = high
        table_ref[f * LANES : (f + 1) * LANES, LANES:] = low


def pick(table_ref, fields, high_rows, low_rows, counts):
    hot = jnp.concatenate([one_hot(row, counts) for row in high_rows], axis=1)
    hot = jnp.concatenate([hot, hot], axis=0)
    lane = lax.broadcasted_iota(jnp.int32, (LANES, LANES), 0).astype(F32)
    hits = [jnp.broadcast_to(row, (LANES, LANES)) == lane for row in low_rows]
    found = []
    for f in range(fields):
        rows = jnp.dot(table_ref[f * LANES : (f + 1) * LANES, :], hot, preferred_element_type=F32)
        found.append(
            [
                jnp.sum(jnp.where(hit, rows[:, LANES * h : LANES * (h + 1)], 0.0), axis=0, keepdims=True)
                for h, hit in enumerate(hits)
            ]
        )
    return found


def leave_kernel(
    sec_ref, base_ref, cell_ref, dep_ref, after_ref, out_ref, mask_ref, left_ref, low_ref, hi_ref, lo_ref, table_ref
):
    sec = sec_ref[0]
    high, low = cell_split(cell_ref[...], sec)
    cell = (high * LANES + low).astype(F32)
    table_of([base_ref[f] for f in range(7)] + [cell], table_ref)
    counts = counters()
    per = dep_ref.shape[1] // LANES
    for r in range(4):
        for q in range(per):
            row = dep_ref[r : r + 1, q * LANES : (q + 1) * LANES]
            k = r * per + q
            hi_row, lo_row = (row >> 7).astype(F32), (row & (LANES - 1)).astype(F32)
            hi_ref[k : k + 1, :] = hi_row
            lo_ref[k : k + 1, :] = lo_row
            left_ref[:, k * LANES : (k + 1) * LANES] = one_hot(hi_row, counts)
            low_ref[:, k * LANES : (k + 1) * LANES] = one_hot(lo_row, counts)

    def step(i, carry):
        ats = [pl.ds(2 * i + h, 1) for h in range(2)]
        found = pick(table_ref, 8, [hi_ref[at, :] for at in ats], [lo_ref[at, :] for at in ats], counts)
        for f in range(8):
            for h in range(2):
                out_ref[f, ats[h], :] = found[f][h]
        return carry

    lax.fori_loop(0, 2 * per, step, 0, unroll=8)
    mask_ref[...] = lax.dot_general(left_ref[...], low_ref[...], NT, preferred_element_type=F32)


def slices_y(tile_ref, fields, up_ref, down_ref):
    for g in range(fields):
        for j in range(HALO):
            up_ref[g, 8 * j : 8 * j + 8, :] = tile_ref[g, pl.ds(8 - HALO + j, 8, stride=8), :]
            down_ref[g, 8 * j : 8 * j + 8, :] = tile_ref[g, pl.ds(j, 8, stride=8), :]


def early_kernel(p_ref, v_ref, far_p_ref, far_v_ref, tile_ref, up_ref, down_ref):
    tile_ref[0] = p_ref[...]
    tile_ref[1] = far_p_ref[...]
    for d in range(3):
        tile_ref[2 + 2 * d] = v_ref[64 * d : 64 * d + 64, :]
        tile_ref[3 + 2 * d] = far_v_ref[64 * d : 64 * d + 64, :]
    slices_y(tile_ref, 8, up_ref, down_ref)


def tile_kernel(mine_ref, got_ref, after_ref, tile_ref, up_ref, down_ref):
    own = mine_ref[0:64, :] + got_ref[64:128, :]
    far = mine_ref[64:128, :] + got_ref[0:64, :]
    tile_ref[0] = 1.0 / (1.0 + own)
    tile_ref[1] = 1.0 / (1.0 + far)
    slices_y(tile_ref, 2, up_ref, down_ref)


def side_kernel(tile_ref, low_ref, high_ref, after_ref, up_ref, down_ref):
    for g in range(tile_ref.shape[0]):
        for x in range(8):
            slab = jnp.concatenate(
                [
                    low_ref[g, pl.ds(8 + x, 4, stride=8), :],
                    tile_ref[g, 8 * x : 8 * x + 8, :],
                    high_ref[g, pl.ds(x, 4, stride=8), :],
                ],
                axis=0,
            )
            if x >= 8 - HALO:
                at = x - (8 - HALO)
                up_ref[g, 16 * at : 16 * at + 16, :] = slab
            if x < HALO:
                down_ref[g, 16 * x : 16 * x + 16, :] = slab


def assemble(tile_ref, ylow_ref, yhigh_ref, xlow_ref, xhigh_ref, grid_ref):
    filler = jnp.ones((8, LANES), F32)
    for g in range(tile_ref.shape[0]):
        f, h = g // 2, g % 2
        lanes = slice(LANES * h, LANES * (h + 1))
        for j in range(HALO):
            grid_ref[f, j, 0:16, lanes] = xlow_ref[g, 16 * j : 16 * j + 16, :]
            grid_ref[f, j, 16:24, lanes] = filler
            grid_ref[f, 8 + HALO + j, 0:16, lanes] = xhigh_ref[g, 16 * j : 16 * j + 16, :]
            grid_ref[f, 8 + HALO + j, 16:24, lanes] = filler
        for x in range(8):
            grid_ref[f, HALO + x, 0:24, lanes] = jnp.concatenate(
                [
                    ylow_ref[g, pl.ds(8 + x, 4, stride=8), :],
                    tile_ref[g, 8 * x : 8 * x + 8, :],
                    yhigh_ref[g, pl.ds(x, 5, stride=8), :],
                    filler[:6],
                    ylow_ref[g, x : x + 1, :],
                ],
                axis=0,
            )


def y_sides(values):
    return pltpu.roll(values, 23, 0), pltpu.roll(values, 1, 0)


def z_sides(values):
    return pltpu.roll(values, 2 * LANES - 1, 1), pltpu.roll(values, 1, 1)


def fluid_kernel(
    tile_ref, ylow_ref, yhigh_ref, xlow_ref, xhigh_ref, flow_ref, leave_ref,
    p_out_ref, v_out_ref, table_ref, sent_ref,
    void_ref, even_ref, odd_ref, invd_ref, div_ref, face_ref,
):
    size = 8 + 2 * HALO
    assemble(tile_ref, ylow_ref, yhigh_ref, xlow_ref, xhigh_ref, void_ref)

    for x in range(1, size - 1):
        void = void_ref[0, x]
        above, below = void_ref[0, x + 1], void_ref[0, x - 1]
        sides = y_sides(void) + z_sides(void)
        total = 6.0 * void + above + below
        for k in range(4):
            total = total + sides[k]
            face_ref[k, x] = void + sides[k]
        invd_ref[x] = 1.0 / total
        ys = y_sides(void * flow_ref[2, x])
        zs = z_sides(void * flow_ref[3, x])
        div_ref[x] = (
            above * flow_ref[1, x + 1] - below * flow_ref[1, x - 1] + (ys[0] - ys[1]) + (zs[0] - zs[1])
        )

    for t in range(SWEEPS):
        source = flow_ref.at[0] if t == 0 else even_ref if t % 2 == 0 else odd_ref
        target = odd_ref if t % 2 == 0 else even_ref
        for x in range(1 + t, size - 1 - t):
            void = void_ref[0, x]
            values = source[x]
            sides = y_sides(values) + z_sides(values)
            total = (void + void_ref[0, x + 1]) * source[x + 1] - div_ref[x]
            total = total + (void + void_ref[0, x - 1]) * source[x - 1]
            for k in range(4):
                total = total + face_ref[k, x] * sides[k]
            target[x] = total * invd_ref[x]

    final = even_ref if SWEEPS % 2 == 0 else odd_ref
    tables = [[], [], [], []]
    for x in range(8):
        values = final[HALO + x]
        ys, zs = y_sides(values), z_sides(values)
        flows = (
            flow_ref[1, HALO + x] - 0.5 * (final[HALO + x + 1] - final[HALO + x - 1]),
            flow_ref[2, HALO + x] - 0.5 * (ys[0] - ys[1]),
            flow_ref[3, HALO + x] - 0.5 * (zs[0] - zs[1]),
        )
        p_out_ref[x] = values[4:12, :LANES]
        tables[0].append(jnp.exp(-2.65 * jnp.log(void_ref[0, HALO + x][4:12])))
        for d in range(3):
            kept = flows[d][4:12]
            v_out_ref[d, x] = kept[:, :LANES]
            tables[1 + d].append(kept)
    fields = []
    for f in range(4):
        whole = jnp.concatenate(tables[f], axis=0)
        fields.append(jnp.concatenate([whole[:, :LANES], whole[:, LANES:]], axis=0))
    table_of(fields, table_ref)

    counts = counters()
    count = leave_ref.shape[1]

    def step(i, carry):
        his, los = [], []
        for h in range(2):
            cell = leave_ref[7, pl.ds(2 * i + h, 1), :].astype(jnp.int32)
            his.append((cell >> 7).astype(F32))
            los.append((cell & (LANES - 1)).astype(F32))
        found = pick(table_ref, 4, his, los, counts)
        for f in range(4):
            for h in range(2):
                sent_ref[f, pl.ds(2 * i + h, 1), :] = found[f][h]
        return carry

    lax.fori_loop(0, count // 2, step, 0, unroll=8)
    drag = TIME_STEP * sent_ref[0] * leave_ref[6]
    scale = 1.0 / (1.0 + drag)
    speeds = [(leave_ref[3 + d] + drag * sent_ref[1 + d]) * scale for d in range(3)]
    for d in range(3):
        sent_ref[3 + d] = speeds[d]
        sent_ref[d] = leave_ref[d] + TIME_STEP * speeds[d]


def flow_kernel(tile_ref, ylow_ref, yhigh_ref, xlow_ref, xhigh_ref, flow_ref):
    assemble(tile_ref, ylow_ref, yhigh_ref, xlow_ref, xhigh_ref, flow_ref)


def main_kernel(sec_ref, table_ref, cell_ref, base_ref, out_ref, hi_ref, lo_ref):
    sec = sec_ref[0]
    high, low = cell_split(cell_ref[...], sec)
    hi_ref[...] = high.astype(F32)
    lo_ref[...] = low.astype(F32)
    counts = counters()
    rows = cell_ref.shape[0]

    def step(i, carry):
        ats = [pl.ds(2 * i + h, 1) for h in range(2)]
        found = pick(table_ref, 4, [hi_ref[at, :] for at in ats], [lo_ref[at, :] for at in ats], counts)
        for f in range(4):
            for h in range(2):
                out_ref[f, ats[h], :] = found[f][h]
        return carry

    lax.fori_loop(0, rows // 2, step, 0, unroll=16)
    drag = TIME_STEP * out_ref[0] * base_ref[6]
    scale = 1.0 / (1.0 + drag)
    speeds = [(base_ref[3 + d] + drag * out_ref[1 + d]) * scale for d in range(3)]
    for d in range(3):
        out_ref[3 + d] = speeds[d]
        out_ref[d] = base_ref[d] + TIME_STEP * speeds[d]


def settle_kernel(
    left_ref, low_ref, mask_ref, moved_ref, a_ref, b_ref, c_ref, d_ref, pos_ref, vel_ref, right_ref, keep_ref,
):
    per = a_ref.shape[1]
    arrivals = (b_ref, a_ref, d_ref, c_ref)
    stays = mask_ref[...] < 0.5
    for f in range(6):
        for r in range(4):
            for q in range(per):
                value = arrivals[r][f, q : q + 1, :]
                part = value.astype(BF16).astype(F32)
                lanes = slice((r * per + q) * LANES, (r * per + q + 1) * LANES)
                for k, wide in enumerate((row16(part), row16(value - part))):
                    for m in range(8):
                        right_ref[f % 2, LANES * k + 16 * m : LANES * k + 16 * m + 16, lanes] = (
                            low_ref[16 * m : 16 * m + 16, lanes] * wide
                        )
        placed = lax.dot_general(left_ref[...], right_ref[f % 2], NT, preferred_element_type=F32)
        placed = placed[:, :LANES] + placed[:, LANES:]
        keep_ref[f] = jnp.where(stays, moved_ref[f], placed)

    def spread(b, carry):
        at = pl.ds(pl.multiple_of(b * LANES, LANES), LANES)
        for d in range(3):
            pos_ref[d : d + 1, at] = keep_ref[d, pl.ds(b, 1), :]
            vel_ref[d : d + 1, at] = keep_ref[3 + d, pl.ds(b, 1), :]
        return carry

    lax.fori_loop(0, moved_ref.shape[1], spread, 0, unroll=16)


def shifted(block, axis, distance):
    count = lax.axis_size(axis)
    return lax.ppermute(block, axis, [((i - distance) % count, i) for i in range(count)])


def body(pressure, fluid_velocity, positions, velocities, volumes, cells, partners, departures):
    particles = volumes.shape[0]
    rows = particles // LANES
    movers = departures.shape[1]
    sec = lax.axis_index("sec").astype(jnp.int32).reshape(1)
    vol2 = volumes.reshape(rows, LANES)
    cell2 = cells.reshape(rows, LANES)
    near_p = pressure.reshape(64, LANES)
    near_v = fluid_velocity.reshape(192, LANES)
    dense = pltpu.VMEM((rows, LANES), F32)
    size = 8 + 2 * HALO
    leavers = 4 * movers // LANES

    far_p = shifted(near_p, "sec", 1)
    far_v = shifted(near_v, "sec", 1)
    (mine,) = call(
        deposit_kernel, [((LANES, LANES), F32)], sec, vol2, cell2,
        scratch=[dense, pltpu.VMEM((rows, LANES), jnp.int32)] + [dense] * 4 + [pltpu.SemaphoreType.DMA((2,))],
        smem=(0,), loose=(1, 2), busy_us=4,
    )
    got = shifted(mine, "sec", 1)
    state, state_up, state_down = call(
        early_kernel, [((8, 64, LANES), F32), ((8, 40, LANES), F32), ((8, 40, LANES), F32)],
        near_p, near_v, far_p, far_v,
    )
    state_ylow = shifted(state_up, "gy", 1)
    state_yhigh = shifted(state_down, "gy", -1)
    (base,) = call(
        contact_kernel, [((7, rows, LANES), F32)], vol2, positions, velocities, partners, state,
        loose=(4,), busy_us=4,
    )
    tile, up, down = call(
        tile_kernel, [((2, 64, LANES), F32), ((2, 40, LANES), F32), ((2, 40, LANES), F32)], mine, got, base,
        loose=(2,),
    )
    ylow = shifted(up, "gy", 1)
    yhigh = shifted(down, "gy", -1)
    state_xup, state_xdown = call(
        side_kernel, [((8, 80, LANES), F32), ((8, 80, LANES), F32)], state, state_ylow, state_yhigh, up, loose=(3,),
    )
    state_xlow = shifted(state_xup, "gx", 1)
    state_xhigh = shifted(state_xdown, "gx", -1)
    leave, mask, left, low = call(
        leave_kernel,
        [
            ((8, leavers, LANES), F32), ((LANES, LANES), F32), ((LANES, 4 * movers), BF16),
            ((LANES, 4 * movers), BF16),
        ],
        sec, base, cell2, departures, state_xup,
        scratch=[
            pltpu.VMEM((leavers, LANES), F32), pltpu.VMEM((leavers, LANES), F32),
            pltpu.VMEM((8 * LANES, 2 * LANES), BF16),
        ],
        smem=(0,), loose=(4,), busy_us=4,
    )
    xup, xdown = call(
        side_kernel, [((2, 80, LANES), F32), ((2, 80, LANES), F32)], tile, ylow, yhigh, leave, loose=(3,),
    )
    xlow = shifted(xup, "gx", 1)
    xhigh = shifted(xdown, "gx", -1)
    (flow,) = call(
        flow_kernel, [((4, size, 24, 2 * LANES), F32)], state, state_ylow, state_yhigh, state_xlow, state_xhigh,
        busy_us=1,
    )
    grid = pltpu.VMEM((size, 24, 2 * LANES), F32)
    p_out, v_out, table, sent = call(
        fluid_kernel,
        [
            (pressure.shape, F32), (fluid_velocity.shape, F32), ((4 * LANES, 2 * LANES), BF16),
            ((6, leavers, LANES), F32),
        ],
        tile, ylow, yhigh, xlow, xhigh, flow, leave,
        scratch=[
            pltpu.VMEM((1, size, 24, 2 * LANES), F32), grid, grid, grid, grid,
            pltpu.VMEM((4, size, 24, 2 * LANES), F32),
        ],
        busy_us=6,
    )
    per = movers // LANES
    arrived = [
        shifted(sent[:, row * per : (row + 1) * per], axis, offset)
        for row, axis, offset in ((0, "gx", 1), (1, "gx", -1), (2, "gy", 1), (3, "gy", -1))
    ]
    (moved,) = call(
        main_kernel, [((6, rows, LANES), F32)], sec, table, cell2, base,
        scratch=[dense] * 2, smem=(0,), busy_us=6,
    )
    pos_out, vel_out = call(
        settle_kernel, [(positions.shape, F32), (velocities.shape, F32)],
        left, low, mask, moved, *arrived,
        scratch=[pltpu.VMEM((2, 2 * LANES, 4 * movers), BF16), pltpu.VMEM((6, rows, LANES), F32)],
        busy_us=4,
    )
    return p_out, v_out, pos_out, vel_out


def solution(mesh):
    placed = (
        P("gx", "gy", "sec"),
        P(None, "gx", "gy", "sec"),
        P(None, ("gx", "gy", "sec")),
        P(None, ("gx", "gy", "sec")),
        P(("gx", "gy", "sec")),
        P(("gx", "gy", "sec")),
        P(None, ("gx", "gy", "sec")),
        P(None, ("gx", "gy", "sec")),
    )
    return jax.shard_map(
        body,
        mesh=mesh,
        in_specs=placed,
        out_specs=(
            P("gx", "gy", "sec"),
            P(None, "gx", "gy", "sec"),
            P(None, ("gx", "gy", "sec")),
            P(None, ("gx", "gy", "sec")),
        ),
        check_vma=False,
    )
```

time: 76.9 us -> 52.2 us (0.68)
  Pallas kernels: 47.3 us -> 25.1 us
  waiting for transfers between devices: 13.2 us -> 8.06 us
  starting transfers between devices: 11.9 us -> 16.3 us
  local copies, waits for them, and re-layouts: 3.36 us -> 1.72 us
    pallas_call x8 -> x11, Pallas kernels: 47.3 us -> 25.1 us  [call(): pl.pallas_call(kernel, out_shape=outs_list, in_specs=specs, out_specs=[vm...]
    ppermute x9 -> x15, waiting for transfers between devices: 13.2 us -> 8.06 us  [shifted(): lax.ppermute(block, axis, [((i - distance) % count, i) for i in range(cou...]
    ppermute x9 -> x15, starting transfers between devices: 11.9 us -> 16.3 us  [shifted(): lax.ppermute(block, axis, [((i - distance) % count, i) for i in range(cou...]
    unnamed x20, local copies, waits for them, and re-layouts: 3.35 us -> 1.71 us
  transfers between devices with their start and end apart: 9 -> 15, of which waited for: 3 -> 3; matrix products, arithmetic and copies ran while one was open for 0% -> 0% of each run, Pallas kernels for 34% -> 30%
where the time goes in v2:
time: 52.2 us; the launch traced here: 52 us
  Pallas kernels  25.1 us (48%)
  starting transfers between devices  16.3 us (31%)
  waiting for transfers between devices  8.06 us (15%)
  local copies, waits for them, and re-layouts  1.72 us (3%)
  between operations  0.84 us (2%)
    pallas_call x11, Pallas kernels, call(): pl.pallas_call(kernel, out_shape=outs_list, in_specs=specs, out_specs=[vm...  25.1 us
    ppermute x15, starting transfers between devices, shifted(): lax.ppermute(block, axis, [((i - distance) % count, i) for i in range(cou...  16.3 us
    ppermute x15, waiting for transfers between devices, shifted(): lax.ppermute(block, axis, [((i - distance) % count, i) for i in range(cou...  8.06 us
    unnamed x20, local copies, waits for them, and re-layouts  1.71 us
  transfers between devices with their start and end apart: 15, of which 3 were waited for; matrix products, arithmetic and copies ran while one was open for 0% of the time, Pallas kernels for 30%

profile of v2, /device:TPU:1, one launch (start us, length us, event | category | flops | bytes accessed | tf_op | source)
XLA Modules:
  0.0 52.0 jit_solution(15826599406674725932)
XLA Ops:
  0.6 2.1 %collective-permute-start.1 = (f32[64,128]{1,0:T(8,128)}, f32[64,128]{1,0:T(8,128)S(1)}, u32[]{:S(2)}, u32[]{:S(2)}) collective-permute-start(f32[64,128]{1,0:T(8,128)} %bitcast.12), channel_id=1, source_target_pairs={{1,0},{0,1},{3,2},{2,3},{5,4},{4,5},{7,6},{6,7},{9,8},{8,9},{11,10... | collective-permute-start | bytes 98312 | tf_op jit(solution)/shard_map/ppermute | solution.py:412
  2.8 0.1 collective-permute-start.2
  2.8 0.0 copy-start.4
  2.8 0.8 %copy-done.4 = f32[16384]{0:T(1024)S(1)} copy-done((f32[16384]{0:T(1024)S(1)}, f32[16384]{0:T(1024)}, u32[]{:S(2)}) %copy-start.4) | copy-done | bytes 65560
  3.7 0.0 copy-start.6
  3.7 0.8 %copy-done.6 = s32[16384]{0:T(1024)S(1)} copy-done((s32[16384]{0:T(1024)S(1)}, s32[16384]{0:T(1024)}, u32[]{:S(2)}) %copy-start.6) | copy-done | bytes 65560
  4.5 0.0 copy-start.3
  4.5 0.0 copy-start.8
  4.5 0.0 copy-start
  4.5 0.0 copy-start.1
  4.5 0.0 copy-start.2
  4.5 0.0 copy-start.5
  4.6 3.5 %shard_map.111.mine_ref = f32[128,128]{1,0:T(8,128)S(1)} custom-call(s32[1]{0:T(128)} %bitcast.sec_ref, f32[128,128]{1,0:T(8,128)S(1)} %bitcast.7, s32[128,128]{1,0:T(8,128)S(1)} %bitcast.9), custom_call_target="tpu_custom_call" | custom-call | flops 4600000000 | bytes 4096 | tf_op jit(solution)/shard_map/pallas_call | solution.py:31
  8.1 1.5 %collective-permute-start = (f32[128,128]{1,0:T(8,128)S(1)}, f32[128,128]{1,0:T(8,128)S(1)}, u32[]{:S(2)}, u32[]{:S(2)}) collective-permute-start(f32[128,128]{1,0:T(8,128)S(1)} %shard_map.111.mine_ref), channel_id=1, source_target_pairs={{1,0},{0,1},{3,2},{2,3},{5,4},{4,5},{7,6},{6,7},{9,8},{8,9},{11,10... | collective-permute-start | bytes 196616 | tf_op jit(solution)/shard_map/ppermute | solution.py:412
  9.5 0.0 collective-permute-done.1.far_p_ref
  9.5 0.0 collective-permute-done.2.far_v_ref
  9.5 0.0 copy-done.3
  9.5 0.0 copy-done.8
  9.5 0.1 shard_map.112
  9.6 1.3 %collective-permute-start.5 = (f32[8,40,128]{2,1,0:T(8,128)S(1)}, f32[8,40,128]{2,1,0:T(8,128)S(1)}, u32[]{:S(2)}, u32[]{:S(2)}) collective-permute-start(f32[8,40,128]{2,1,0:T(8,128)S(1)} %get-tuple-element.28), channel_id=1, source_target_pairs={{6,0},{0,2},{2,4},{4,6},{7,1},{1,3},{3,5},{5,7},{14,8},{8,10},{10,... | collective-permute-start | bytes 491528 | tf_op jit(solution)/shard_map/ppermute | solution.py:412
  11.0 2.1 %collective-permute-start.6 = (f32[8,40,128]{2,1,0:T(8,128)S(1)}, f32[8,40,128]{2,1,0:T(8,128)S(1)}, u32[]{:S(2)}, u32[]{:S(2)}) collective-permute-start(f32[8,40,128]{2,1,0:T(8,128)S(1)} %get-tuple-element.29), channel_id=1, source_target_pairs={{2,0},{4,2},{6,4},{0,6},{3,1},{5,3},{7,5},{1,7},{10,8},{12,10},{14... | collective-permute-start | bytes 491528 | tf_op jit(solution)/shard_map/ppermute | solution.py:412
  13.1 0.0 copy-done
  13.1 0.0 copy-done.1
  13.1 0.0 copy-done.2
  13.1 0.0 copy-done.5
  13.1 0.0 copy-start.7
  13.1 0.0 copy-start.9
  13.1 3.0 %shard_map.113.after_ref.base_ref = f32[7,128,128]{2,1,0:T(8,128)S(1)} custom-call(f32[128,128]{1,0:T(8,128)S(1)} %bitcast.8, f32[3,16384]{1,0:T(4,128)S(1)} %copy-done.1, f32[3,16384]{1,0:T(4,128)S(1)} %copy-done.2, s32[8,16384]{1,0:T(8,128)S(1)} %copy-done, f32[8,64,128]{2,1,0:T(8,128)S(1)} %get-tuple-element.24.after_ref.tile_ref), custom_call_target="tpu_custom_call" | custom-call | flops 4600000000 | bytes 4096 | tf_op jit(solution)/shard_map/pallas_call | solution.py:31
  16.1 0.0 collective-permute-done.got_ref
  16.1 1.5 %collective-permute-start.4 = (f32[2,40,128]{2,1,0:T(8,128)S(1)}, f32[2,40,128]{2,1,0:T(8,128)S(1)}, u32[]{:S(2)}, u32[]{:S(2)}) collective-permute-start(f32[2,40,128]{2,1,0:T(8,128)S(1)} %get-tuple-element.27), channel_id=1, source_target_pairs={{2,0},{4,2},{6,4},{0,6},{3,1},{5,3},{7,5},{1,7},{10,8},{12,10},{14... | collective-permute-start | bytes 122888 | tf_op jit(solution)/shard_map/ppermute | solution.py:412
  17.6 0.1 collective-permute-start.3
  17.6 0.0 collective-permute-done.5.low_ref.ylow_ref
  17.6 2.3 %collective-permute-done.6.high_ref.yhigh_ref = f32[8,40,128]{2,1,0:T(8,128)S(1)} collective-permute-done((f32[8,40,128]{2,1,0:T(8,128)S(1)}, f32[8,40,128]{2,1,0:T(8,128)S(1)}, u32[]{:S(2)}, u32[]{:S(2)}) %collective-permute-start.6) | collective-permute-done | bytes 163872 | tf_op jit(solution)/shard_map/ppermute | solution.py:412
  19.9 0.1 shard_map.115
  20.0 1.7 %collective-permute-start.10 = (f32[8,80,128]{2,1,0:T(8,128)S(1)}, f32[8,80,128]{2,1,0:T(8,128)S(1)}, u32[]{:S(2)}, u32[]{:S(2)}) collective-permute-start(f32[8,80,128]{2,1,0:T(8,128)S(1)} %get-tuple-element.34), channel_id=1, source_target_pairs={{8,0},{16,8},{24,16},{0,24},{9,1},{17,9},{25,17},{1,25},{10,2},{18... | collective-permute-start | bytes 983048 | tf_op jit(solution)/shard_map/ppermute | solution.py:412
  21.7 1.2 %collective-permute-start.9 = (f32[8,80,128]{2,1,0:T(8,128)S(1)}, f32[8,80,128]{2,1,0:T(8,128)S(1)}, u32[]{:S(2)}, u32[]{:S(2)}) collective-permute-start(f32[8,80,128]{2,1,0:T(8,128)S(1)} %get-tuple-element.30.after_ref), channel_id=1, source_target_pairs={{24,0},{0,8},{8,16},{16,24},{25,1},{1,9},{9,17},{17,25},{26,2},{2,... | collective-permute-start | bytes 983048 | tf_op jit(solution)/shard_map/ppermute | solution.py:412
  22.8 0.0 copy-done.7
  22.8 0.0 copy-done.9
  22.8 3.7 %shard_map.116 = (f32[8,32,128]{2,1,0:T(8,128)S(1)}, f32[128,128]{1,0:T(8,128)S(1)}, bf16[128,4096]{1,0:T(8,128)(2,1)S(1)}, bf16[128,4096]{1,0:T(8,128)(2,1)S(1)}) custom-call(s32[1]{0:T(128)} %bitcast.sec_ref, f32[7,128,128]{2,1,0:T(8,128)S(1)} %shard_map.113.after_ref.base_ref, s32[128,128]{1,0:T(8,128)S(1)} %bitcast.10, s32[4,1024]{1,0:T(4,128)S(1)} %copy-done.9, ...), custom_call_target="tpu_custom_call" | custom-call | flops 4600000000 | bytes 4096 | tf_op jit(solution)/shard_map/pallas_call | solution.py:31
  26.5 0.0 collective-permute-done.4.high_ref.yhigh_ref
  26.5 0.0 collective-permute-done.3.low_ref.ylow_ref
  26.6 0.5 collective-permute-start.7
  27.1 0.1 collective-permute-start.8
  27.1 4.2 %collective-permute-done.10.xhigh_ref = f32[8,80,128]{2,1,0:T(8,128)S(1)} collective-permute-done((f32[8,80,128]{2,1,0:T(8,128)S(1)}, f32[8,80,128]{2,1,0:T(8,128)S(1)}, u32[]{:S(2)}, u32[]{:S(2)}) %collective-permute-start.10) | collective-permute-done | bytes 327712 | tf_op jit(solution)/shard_map/ppermute | solution.py:412
  31.3 0.0 collective-permute-done.9.xlow_ref
  31.3 0.2 shard_map.118.flow_ref
  31.5 0.0 collective-permute-done.7.xlow_ref
  31.5 1.6 %collective-permute-done.8.xhigh_ref = f32[2,80,128]{2,1,0:T(8,128)S(1)} collective-permute-done((f32[2,80,128]{2,1,0:T(8,128)S(1)}, f32[2,80,128]{2,1,0:T(8,128)S(1)}, u32[]{:S(2)}, u32[]{:S(2)}) %collective-permute-start.8) | collective-permute-done | bytes 81952 | tf_op jit(solution)/shard_map/ppermute | solution.py:412
  33.1 3.0 %shard_map.119 = (f32[8,8,128]{2,1,0:T(8,128)}, f32[3,8,8,128]{3,2,1,0:T(8,128)}, bf16[512,256]{1,0:T(8,128)(2,1)S(1)}, f32[6,32,128]{2,1,0:T(8,128)S(1)}) custom-call(f32[2,64,128]{2,1,0:T(8,128)S(1)} %get-tuple-element.25.tile_ref, f32[2,40,128]{2,1,0:T(8,128)S(1)} %collective-permute-done.3.low_ref.ylow_ref, ...), custom_call_target="tpu_custom_call" | custom-call | flops 6899999744 | bytes 4096 | tf_op jit(solution)/shard_map/pallas_call | solution.py:31
  36.1 2.5 %collective-permute-start.14 = (f32[6,8,128]{2,1,0:T(8,128)S(1)}, f32[6,8,128]{2,1,0:T(8,128)S(1)}, u32[]{:S(2)}, u32[]{:S(2)}) collective-permute-start(f32[6,8,128]{2,1,0:T(8,128)S(1)} %get-tuple-element.44), channel_id=1, source_target_pairs={{2,0},{4,2},{6,4},{0,6},{3,1},{5,3},{7,5},{1,7},{10,8},{12,10},{14... | collective-permute-start | bytes 73736 | tf_op jit(solution)/shard_map/ppermute | solution.py:412
  38.6 0.0 collective-permute-start.13
  38.6 0.7 %collective-permute-start.12 = (f32[6,8,128]{2,1,0:T(8,128)S(1)}, f32[6,8,128]{2,1,0:T(8,128)S(1)}, u32[]{:S(2)}, u32[]{:S(2)}) collective-permute-start(f32[6,8,128]{2,1,0:T(8,128)S(1)} %get-tuple-element.46), channel_id=1, source_target_pairs={{8,0},{16,8},{24,16},{0,24},{9,1},{17,9},{25,17},{1,25},{10,2},{18... | collective-permute-start | bytes 73736 | tf_op jit(solution)/shard_map/ppermute | solution.py:412
  39.3 1.0 %collective-permute-start.11 = (f32[6,8,128]{2,1,0:T(8,128)S(1)}, f32[6,8,128]{2,1,0:T(8,128)S(1)}, u32[]{:S(2)}, u32[]{:S(2)}) collective-permute-start(f32[6,8,128]{2,1,0:T(8,128)S(1)} %get-tuple-element.47), channel_id=1, source_target_pairs={{24,0},{0,8},{8,16},{16,24},{25,1},{1,9},{9,17},{17,25},{26,2},{2,... | collective-permute-start | bytes 73736 | tf_op jit(solution)/shard_map/ppermute | solution.py:412
  40.4 5.2 %shard_map.120.moved_ref = f32[6,128,128]{2,1,0:T(8,128)S(1)} custom-call(s32[1]{0:T(128)} %bitcast.sec_ref, bf16[512,256]{1,0:T(8,128)(2,1)S(1)} %get-tuple-element.40.table_ref, s32[128,128]{1,0:T(8,128)S(1)} %bitcast.11, f32[7,128,128]{2,1,0:T(8,128)S(1)} %shard_map.113.after_ref.base_ref), custom_call_target="tpu_custom_call" | custom-call | flops 6899999744 | bytes 4096 | tf_op jit(solution)/shard_map/pallas_call | solution.py:31
  45.6 0.0 collective-permute-done.14.d_ref
  45.6 0.0 collective-permute-done.13.c_ref
  45.6 0.0 collective-permute-done.12.b_ref
  45.6 0.0 collective-permute-done.11.a_ref
  45.6 6.4 %shard_map.121 = (f32[3,16384]{1,0:T(4,128)}, f32[3,16384]{1,0:T(4,128)}) custom-call(bf16[128,4096]{1,0:T(8,128)(2,1)S(1)} %get-tuple-element.37.left_ref, bf16[128,4096]{1,0:T(8,128)(2,1)S(1)} %get-tuple-element.38.low_ref, f32[128,128]{1,0:T(8,128)S(1)} %get-tuple-element.39.mask_ref, f32[6,128,128]{2,1,0:T(8,128)S(1)} %shard_map.120.moved_ref, ...), custom_call_target="tpu_custom_call" | custom-call | flops 4600000000 | bytes 4096 | tf_op jit(solution)/shard_map/pallas_call | solution.py:31
  (3 shorter events, 0.1 us)
Async XLA Ops:
  0.6 8.9 %collective-permute-start.1 = (f32[64,128]{1,0:T(8,128)}, f32[64,128]{1,0:T(8,128)S(1)}, u32[]{:S(2)}, u32[]{:S(2)}) collective-permute-start(f32[64,128]{1,0:T(8,128)} %bitcast.12), channel_id=1, source_target_pairs={{1,0},{0,1},{3,2},{2,3},{5,4},{4,5},{7,6},{6,7},{9,8},{8,9},{11,10... | collective-permute-start | bytes 98312 | tf_op jit(solution)/shard_map/ppermute | solution.py:412
  2.8 6.8 %collective-permute-start.2 = (f32[192,128]{1,0:T(8,128)}, f32[192,128]{1,0:T(8,128)S(1)}, u32[]{:S(2)}, u32[]{:S(2)}) collective-permute-start(f32[192,128]{1,0:T(8,128)} %bitcast.5), channel_id=1, source_target_pairs={{1,0},{0,1},{3,2},{2,3},{5,4},{4,5},{7,6},{6,7},{9,8},{8,9},{11,10... | collective-permute-start | bytes 294920 | tf_op jit(solution)/shard_map/ppermute | solution.py:412
  2.8 0.8 %copy-start.4 = (f32[16384]{0:T(1024)S(1)}, f32[16384]{0:T(1024)}, u32[]{:S(2)}) copy-start(f32[16384]{0:T(1024)} %param.12) | copy-start | bytes 196612
  3.7 0.8 %copy-start.6 = (s32[16384]{0:T(1024)S(1)}, s32[16384]{0:T(1024)}, u32[]{:S(2)}) copy-start(s32[16384]{0:T(1024)} %param.13) | copy-start | bytes 196612
  4.5 5.0 %copy-start.3 = (f32[3,8,8,128]{3,2,1,0:T(8,128)S(1)}, f32[3,8,8,128]{3,2,1,0:T(8,128)}, u32[]{:S(2)}) copy-start(f32[3,8,8,128]{3,2,1,0:T(8,128)} %param.9) | copy-start | bytes 294916
  4.5 5.0 %copy-start.8 = (f32[8,8,128]{2,1,0:T(8,128)S(1)}, f32[8,8,128]{2,1,0:T(8,128)}, u32[]{:S(2)}) copy-start(f32[8,8,128]{2,1,0:T(8,128)} %param.8) | copy-start | bytes 98308
  4.5 8.5 %copy-start = (s32[8,16384]{1,0:T(8,128)S(1)}, s32[8,16384]{1,0:T(8,128)}, u32[]{:S(2)}) copy-start(s32[8,16384]{1,0:T(8,128)} %pair_ref.1) | copy-start | bytes 1572868
  4.5 8.5 %copy-start.1 = (f32[3,16384]{1,0:T(4,128)S(1)}, f32[3,16384]{1,0:T(4,128)}, u32[]{:S(2)}) copy-start(f32[3,16384]{1,0:T(4,128)} %pos_ref.1) | copy-start | bytes 589828
  4.5 8.5 %copy-start.2 = (f32[3,16384]{1,0:T(4,128)S(1)}, f32[3,16384]{1,0:T(4,128)}, u32[]{:S(2)}) copy-start(f32[3,16384]{1,0:T(4,128)} %vel_ref.1) | copy-start | bytes 589828
  4.5 8.5 %copy-start.5 = (f32[16384]{0:T(1024)S(1)}, f32[16384]{0:T(1024)}, u32[]{:S(2)}) copy-start(f32[16384]{0:T(1024)} %param.12) | copy-start | bytes 196612
  8.1 8.0 %collective-permute-start = (f32[128,128]{1,0:T(8,128)S(1)}, f32[128,128]{1,0:T(8,128)S(1)}, u32[]{:S(2)}, u32[]{:S(2)}) collective-permute-start(f32[128,128]{1,0:T(8,128)S(1)} %shard_map.111.mine_ref), channel_id=1, source_target_pairs={{1,0},{0,1},{3,2},{2,3},{5,4},{4,5},{7,6},{6,7},{9,8},{8,9},{11,10... | collective-permute-start | bytes 196616 | tf_op jit(solution)/shard_map/ppermute | solution.py:412
  9.6 8.0 %collective-permute-start.5 = (f32[8,40,128]{2,1,0:T(8,128)S(1)}, f32[8,40,128]{2,1,0:T(8,128)S(1)}, u32[]{:S(2)}, u32[]{:S(2)}) collective-permute-start(f32[8,40,128]{2,1,0:T(8,128)S(1)} %get-tuple-element.28), channel_id=1, source_target_pairs={{6,0},{0,2},{2,4},{4,6},{7,1},{1,3},{3,5},{5,7},{14,8},{8,10},{10,... | collective-permute-start | bytes 491528 | tf_op jit(solution)/shard_map/ppermute | solution.py:412
  11.0 8.9 %collective-permute-start.6 = (f32[8,40,128]{2,1,0:T(8,128)S(1)}, f32[8,40,128]{2,1,0:T(8,128)S(1)}, u32[]{:S(2)}, u32[]{:S(2)}) collective-permute-start(f32[8,40,128]{2,1,0:T(8,128)S(1)} %get-tuple-element.29), channel_id=1, source_target_pairs={{2,0},{4,2},{6,4},{0,6},{3,1},{5,3},{7,5},{1,7},{10,8},{12,10},{14... | collective-permute-start | bytes 491528 | tf_op jit(solution)/shard_map/ppermute | solution.py:412
  13.1 9.8 %copy-start.7 = (s32[16384]{0:T(1024)S(1)}, s32[16384]{0:T(1024)}, u32[]{:S(2)}) copy-start(s32[16384]{0:T(1024)} %param.13) | copy-start | bytes 196612
  13.1 9.7 %copy-start.9 = (s32[4,1024]{1,0:T(4,128)S(1)}, s32[4,1024]{1,0:T(4,128)}, u32[]{:S(2)}) copy-start(s32[4,1024]{1,0:T(4,128)} %dep_ref.1) | copy-start | bytes 49156
  16.1 10.4 %collective-permute-start.4 = (f32[2,40,128]{2,1,0:T(8,128)S(1)}, f32[2,40,128]{2,1,0:T(8,128)S(1)}, u32[]{:S(2)}, u32[]{:S(2)}) collective-permute-start(f32[2,40,128]{2,1,0:T(8,128)S(1)} %get-tuple-element.27), channel_id=1, source_target_pairs={{2,0},{4,2},{6,4},{0,6},{3,1},{5,3},{7,5},{1,7},{10,8},{12,10},{14... | collective-permute-start | bytes 122888 | tf_op jit(solution)/shard_map/ppermute | solution.py:412
  17.6 9.0 %collective-permute-start.3 = (f32[2,40,128]{2,1,0:T(8,128)S(1)}, f32[2,40,128]{2,1,0:T(8,128)S(1)}, u32[]{:S(2)}, u32[]{:S(2)}) collective-permute-start(f32[2,40,128]{2,1,0:T(8,128)S(1)} %get-tuple-element.26.after_ref), channel_id=1, source_target_pairs={{6,0},{0,2},{2,4},{4,6},{7,1},{1,3},{3,5},{5,7},{14,8},{8,10},{10,... | collective-permute-start | bytes 122888 | tf_op jit(solution)/shard_map/ppermute | solution.py:412
  20.0 11.3 %collective-permute-start.10 = (f32[8,80,128]{2,1,0:T(8,128)S(1)}, f32[8,80,128]{2,1,0:T(8,128)S(1)}, u32[]{:S(2)}, u32[]{:S(2)}) collective-permute-start(f32[8,80,128]{2,1,0:T(8,128)S(1)} %get-tuple-element.34), channel_id=1, source_target_pairs={{8,0},{16,8},{24,16},{0,24},{9,1},{17,9},{25,17},{1,25},{10,2},{18... | collective-permute-start | bytes 983048 | tf_op jit(solution)/shard_map/ppermute | solution.py:412
  21.7 9.7 %collective-permute-start.9 = (f32[8,80,128]{2,1,0:T(8,128)S(1)}, f32[8,80,128]{2,1,0:T(8,128)S(1)}, u32[]{:S(2)}, u32[]{:S(2)}) collective-permute-start(f32[8,80,128]{2,1,0:T(8,128)S(1)} %get-tuple-element.30.after_ref), channel_id=1, source_target_pairs={{24,0},{0,8},{8,16},{16,24},{25,1},{1,9},{9,17},{17,25},{26,2},{2,... | collective-permute-start | bytes 983048 | tf_op jit(solution)/shard_map/ppermute | solution.py:412
  26.6 4.9 %collective-permute-start.7 = (f32[2,80,128]{2,1,0:T(8,128)S(1)}, f32[2,80,128]{2,1,0:T(8,128)S(1)}, u32[]{:S(2)}, u32[]{:S(2)}) collective-permute-start(f32[2,80,128]{2,1,0:T(8,128)S(1)} %get-tuple-element.32), channel_id=1, source_target_pairs={{24,0},{0,8},{8,16},{16,24},{25,1},{1,9},{9,17},{17,25},{26,2},{2,... | collective-permute-start | bytes 245768 | tf_op jit(solution)/shard_map/ppermute | solution.py:412
  27.1 6.0 %collective-permute-start.8 = (f32[2,80,128]{2,1,0:T(8,128)S(1)}, f32[2,80,128]{2,1,0:T(8,128)S(1)}, u32[]{:S(2)}, u32[]{:S(2)}) collective-permute-start(f32[2,80,128]{2,1,0:T(8,128)S(1)} %get-tuple-element.33), channel_id=1, source_target_pairs={{8,0},{16,8},{24,16},{0,24},{9,1},{17,9},{25,17},{1,25},{10,2},{18... | collective-permute-start | bytes 245768 | tf_op jit(solution)/shard_map/ppermute | solution.py:412
  36.1 9.5 %collective-permute-start.14 = (f32[6,8,128]{2,1,0:T(8,128)S(1)}, f32[6,8,128]{2,1,0:T(8,128)S(1)}, u32[]{:S(2)}, u32[]{:S(2)}) collective-permute-start(f32[6,8,128]{2,1,0:T(8,128)S(1)} %get-tuple-element.44), channel_id=1, source_target_pairs={{2,0},{4,2},{6,4},{0,6},{3,1},{5,3},{7,5},{1,7},{10,8},{12,10},{14... | collective-permute-start | bytes 73736 | tf_op jit(solution)/shard_map/ppermute | solution.py:412
  38.6 7.0 %collective-permute-start.13 = (f32[6,8,128]{2,1,0:T(8,128)S(1)}, f32[6,8,128]{2,1,0:T(8,128)S(1)}, u32[]{:S(2)}, u32[]{:S(2)}) collective-permute-start(f32[6,8,128]{2,1,0:T(8,128)S(1)} %get-tuple-element.45), channel_id=1, source_target_pairs={{6,0},{0,2},{2,4},{4,6},{7,1},{1,3},{3,5},{5,7},{14,8},{8,10},{10,... | collective-permute-start | bytes 73736 | tf_op jit(solution)/shard_map/ppermute | solution.py:412
  38.6 7.0 %collective-permute-start.12 = (f32[6,8,128]{2,1,0:T(8,128)S(1)}, f32[6,8,128]{2,1,0:T(8,128)S(1)}, u32[]{:S(2)}, u32[]{:S(2)}) collective-permute-start(f32[6,8,128]{2,1,0:T(8,128)S(1)} %get-tuple-element.46), channel_id=1, source_target_pairs={{8,0},{16,8},{24,16},{0,24},{9,1},{17,9},{25,17},{1,25},{10,2},{18... | collective-permute-start | bytes 73736 | tf_op jit(solution)/shard_map/ppermute | solution.py:412
  39.3 6.3 %collective-permute-start.11 = (f32[6,8,128]{2,1,0:T(8,128)S(1)}, f32[6,8,128]{2,1,0:T(8,128)S(1)}, u32[]{:S(2)}, u32[]{:S(2)}) collective-permute-start(f32[6,8,128]{2,1,0:T(8,128)S(1)} %get-tuple-element.47), channel_id=1, source_target_pairs={{24,0},{0,8},{8,16},{16,24},{25,1},{1,9},{9,17},{17,25},{26,2},{2,... | collective-permute-start | bytes 73736 | tf_op jit(solution)/shard_map/ppermute | solution.py:412

commit v3 on v2

--- a/solution.py
+++ b/solution.py
@@ -1,3 +1,5 @@
+import functools
+
 import jax
 import jax.numpy as jnp
 from jax import lax
@@ -22,12 +24,16 @@
 NT = (((1,), (1,)), ((), ()))
 
 
-def call(kernel, outs, *args, scratch=(), busy_us=0.1, smem=(), loose=()):
+def call(kernel, outs, *args, scratch=(), busy_us=0.1, smem=(), loose=(), hbm=()):
     outs_list = [jax.ShapeDtypeStruct(shape, dtype) for shape, dtype in outs]
     vmem = pl.BlockSpec(memory_space=pltpu.VMEM)
     scalar = pl.BlockSpec(memory_space=pltpu.SMEM)
     anywhere = pl.BlockSpec(memory_space=pl.ANY)
-    specs = [scalar if i in smem else anywhere if i in loose else vmem for i in range(len(args))]
+    outside = pl.BlockSpec(memory_space=pltpu.HBM)
+    specs = [
+        scalar if i in smem else anywhere if i in loose else outside if i in hbm else vmem
+        for i in range(len(args))
+    ]
     return pl.pallas_call(
         kernel,
         out_shape=outs_list,
@@ -161,9 +167,27 @@
     return found
 
 
-def leave_kernel(
-    sec_ref, base_ref, cell_ref, dep_ref, after_ref, out_ref, mask_ref, left_ref, low_ref, hi_ref, lo_ref, table_ref
-):
+def marks_kernel(dep_ref, after_ref, mask_ref, left_ref, low_ref):
+    counts = counters()
+    per = dep_ref.shape[1] // LANES
+    for r in range(4):
+        for q in range(per):
+            row = dep_ref[r : r + 1, q * LANES : (q + 1) * LANES]
+            hi_row, lane = (row >> 7).astype(F32), row & (LANES - 1)
+            lanes = slice((r * per + q) * LANES, (r * per + q + 1) * LANES)
+            for h in range(2):
+                left_ref[h * LANES : (h + 1) * LANES, lanes] = one_hot(
+                    jnp.where((lane >> 6) == h, hi_row, -1.0), counts
+                )
+            low_ref[:, lanes] = one_hot((lane & 63).astype(F32), counts[:4])
+    mask_ref[...] = unfold(lax.dot_general(low_ref[...], left_ref[...], NT, preferred_element_type=F32))
+
+
+def unfold(halves):
+    return jnp.swapaxes(jnp.concatenate([halves[:, :LANES], halves[:, LANES:]], axis=0), 0, 1)
+
+
+def leave_kernel(sec_ref, base_ref, cell_ref, dep_ref, after_ref, out_ref, hi_ref, lo_ref, table_ref):
     sec = sec_ref[0]
     high, low = cell_split(cell_ref[...], sec)
     cell = (high * LANES + low).astype(F32)
@@ -174,11 +198,8 @@
         for q in range(per):
             row = dep_ref[r : r + 1, q * LANES : (q + 1) * LANES]
             k = r * per + q
-            hi_row, lo_row = (row >> 7).astype(F32), (row & (LANES - 1)).astype(F32)
-            hi_ref[k : k + 1, :] = hi_row
-            lo_ref[k : k + 1, :] = lo_row
-            left_ref[:, k * LANES : (k + 1) * LANES] = one_hot(hi_row, counts)
-            low_ref[:, k * LANES : (k + 1) * LANES] = one_hot(lo_row, counts)
+            hi_ref[k : k + 1, :] = (row >> 7).astype(F32)
+            lo_ref[k : k + 1, :] = (row & (LANES - 1)).astype(F32)
 
     def step(i, carry):
         ats = [pl.ds(2 * i + h, 1) for h in range(2)]
@@ -189,14 +210,41 @@
         return carry
 
     lax.fori_loop(0, 2 * per, step, 0, unroll=8)
-    mask_ref[...] = lax.dot_general(left_ref[...], low_ref[...], NT, preferred_element_type=F32)
-
-
-def slices_y(tile_ref, fields, up_ref, down_ref):
-    for g in range(fields):
-        for j in range(HALO):
-            up_ref[g, 8 * j : 8 * j + 8, :] = tile_ref[g, pl.ds(8 - HALO + j, 8, stride=8), :]
-            down_ref[g, 8 * j : 8 * j + 8, :] = tile_ref[g, pl.ds(j, 8, stride=8), :]
+
+
+STATE = ((HALO, HALO, HALO), (HALO - 1, HALO, HALO), (HALO, HALO - 1, HALO), (HALO - 1, HALO - 1, HALO - 1))
+VOID = ((HALO, HALO, HALO),)
+
+
+def y_starts(spec):
+    starts, at = [], 0
+    for depth, _, _ in spec:
+        for _ in range(2):
+            starts.append(at)
+            at += 8 * depth
+    return starts, at
+
+
+def x_starts(spec):
+    starts, at = [], 0
+    for _, depth, reach in spec:
+        for _ in range(2):
+            own = []
+            for away in range(1, depth + 1):
+                extra = min(HALO - 1, reach - away)
+                own.append((at, extra))
+                at += 8 + 2 * extra
+            starts.append(own)
+    return starts, at
+
+
+def slices_y(spec, tile_ref, up_ref, down_ref):
+    for g, start in enumerate(y_starts(spec)[0]):
+        depth = spec[g // 2][0]
+        for j in range(depth):
+            at = start + 8 * j
+            up_ref[at : at + 8, :] = tile_ref[g, pl.ds(8 - depth + j, 8, stride=8), :]
+            down_ref[at : at + 8, :] = tile_ref[g, pl.ds(j, 8, stride=8), :]
 
 
 def early_kernel(p_ref, v_ref, far_p_ref, far_v_ref, tile_ref, up_ref, down_ref):
@@ -205,7 +253,7 @@
     for d in range(3):
         tile_ref[2 + 2 * d] = v_ref[64 * d : 64 * d + 64, :]
         tile_ref[3 + 2 * d] = far_v_ref[64 * d : 64 * d + 64, :]
-    slices_y(tile_ref, 8, up_ref, down_ref)
+    slices_y(STATE, tile_ref, up_ref, down_ref)
 
 
 def tile_kernel(mine_ref, got_ref, after_ref, tile_ref, up_ref, down_ref):
@@ -213,48 +261,47 @@
     far = mine_ref[64:128, :] + got_ref[0:64, :]
     tile_ref[0] = 1.0 / (1.0 + own)
     tile_ref[1] = 1.0 / (1.0 + far)
-    slices_y(tile_ref, 2, up_ref, down_ref)
-
-
-def side_kernel(tile_ref, low_ref, high_ref, after_ref, up_ref, down_ref):
-    for g in range(tile_ref.shape[0]):
+    slices_y(VOID, tile_ref, up_ref, down_ref)
+
+
+def side_kernel(spec, tile_ref, low_ref, high_ref, after_ref, up_ref, down_ref):
+    starts = x_starts(spec)[0]
+    for g, y_start in enumerate(y_starts(spec)[0]):
+        depth = spec[g // 2][0]
+        for away, (start, extra) in enumerate(starts[g], 1):
+            for x, out_ref in ((8 - away, up_ref), (away - 1, down_ref)):
+                rows = [tile_ref[g, 8 * x : 8 * x + 8, :]]
+                if extra > 0:
+                    rows.insert(0, low_ref[pl.ds(y_start + 8 * (depth - extra) + x, extra, stride=8), :])
+                    rows.append(high_ref[pl.ds(y_start + x, extra, stride=8), :])
+                rows = jnp.concatenate(rows, axis=0) if extra > 0 else rows[0]
+                out_ref[start : start + 8 + 2 * extra, :] = rows
+
+
+def assemble(spec, tile_ref, ylow_ref, yhigh_ref, xlow_ref, xhigh_ref, grid_ref):
+    filler = jnp.ones((8, LANES), F32)
+    starts = x_starts(spec)[0]
+    for g, y_start in enumerate(y_starts(spec)[0]):
+        f, h = g // 2, g % 2
+        depth = spec[f][0]
+        lanes = slice(LANES * h, LANES * (h + 1))
+        for x in list(range(HALO)) + list(range(HALO + 8, 2 * HALO + 8)):
+            for m in range(3):
+                grid_ref[f, x, 8 * m : 8 * m + 8, lanes] = filler
+        for away, (start, extra) in enumerate(starts[g], 1):
+            for x, side_ref in ((HALO - away, xlow_ref), (HALO + 7 + away, xhigh_ref)):
+                grid_ref[f, x, 4 - extra : 12 + extra, lanes] = side_ref[start : start + 8 + 2 * extra, :]
         for x in range(8):
-            slab = jnp.concatenate(
-                [
-                    low_ref[g, pl.ds(8 + x, 4, stride=8), :],
-                    tile_ref[g, 8 * x : 8 * x + 8, :],
-                    high_ref[g, pl.ds(x, 4, stride=8), :],
-                ],
-                axis=0,
-            )
-            if x >= 8 - HALO:
-                at = x - (8 - HALO)
-                up_ref[g, 16 * at : 16 * at + 16, :] = slab
-            if x < HALO:
-                down_ref[g, 16 * x : 16 * x + 16, :] = slab
-
-
-def assemble(tile_ref, ylow_ref, yhigh_ref, xlow_ref, xhigh_ref, grid_ref):
-    filler = jnp.ones((8, LANES), F32)
-    for g in range(tile_ref.shape[0]):
-        f, h = g // 2, g % 2
-        lanes = slice(LANES * h, LANES * (h + 1))
-        for j in range(HALO):
-            grid_ref[f, j, 0:16, lanes] = xlow_ref[g, 16 * j : 16 * j + 16, :]
-            grid_ref[f, j, 16:24, lanes] = filler
-            grid_ref[f, 8 + HALO + j, 0:16, lanes] = xhigh_ref[g, 16 * j : 16 * j + 16, :]
-            grid_ref[f, 8 + HALO + j, 16:24, lanes] = filler
-        for x in range(8):
-            grid_ref[f, HALO + x, 0:24, lanes] = jnp.concatenate(
-                [
-                    ylow_ref[g, pl.ds(8 + x, 4, stride=8), :],
-                    tile_ref[g, 8 * x : 8 * x + 8, :],
-                    yhigh_ref[g, pl.ds(x, 5, stride=8), :],
-                    filler[:6],
-                    ylow_ref[g, x : x + 1, :],
-                ],
-                axis=0,
-            )
+            far = depth - 4
+            rows = [
+                ylow_ref[pl.ds(y_start + 8 * far + x, 4, stride=8), :],
+                tile_ref[g, 8 * x : 8 * x + 8, :],
+                yhigh_ref[pl.ds(y_start + x, depth, stride=8), :],
+                filler[: 8 - 2 * far],
+            ]
+            if far > 0:
+                rows.append(ylow_ref[y_start + x : y_start + x + 1, :])
+            grid_ref[f, HALO + x, 0:24, lanes] = jnp.concatenate(rows, axis=0)
 
 
 def y_sides(values):
@@ -271,7 +318,7 @@
     void_ref, even_ref, odd_ref, invd_ref, div_ref, face_ref,
 ):
     size = 8 + 2 * HALO
-    assemble(tile_ref, ylow_ref, yhigh_ref, xlow_ref, xhigh_ref, void_ref)
+    assemble(VOID, tile_ref, ylow_ref, yhigh_ref, xlow_ref, xhigh_ref, void_ref)
 
     for x in range(1, size - 1):
         void = void_ref[0, x]
@@ -348,7 +395,7 @@
 
 
 def flow_kernel(tile_ref, ylow_ref, yhigh_ref, xlow_ref, xhigh_ref, flow_ref):
-    assemble(tile_ref, ylow_ref, yhigh_ref, xlow_ref, xhigh_ref, flow_ref)
+    assemble(STATE, tile_ref, ylow_ref, yhigh_ref, xlow_ref, xhigh_ref, flow_ref)
 
 
 def main_kernel(sec_ref, table_ref, cell_ref, base_ref, out_ref, hi_ref, lo_ref):
@@ -389,13 +436,13 @@
                 part = value.astype(BF16).astype(F32)
                 lanes = slice((r * per + q) * LANES, (r * per + q + 1) * LANES)
                 for k, wide in enumerate((row16(part), row16(value - part))):
-                    for m in range(8):
-                        right_ref[f % 2, LANES * k + 16 * m : LANES * k + 16 * m + 16, lanes] = (
-                            low_ref[16 * m : 16 * m + 16, lanes] * wide
-                        )
-        placed = lax.dot_general(left_ref[...], right_ref[f % 2], NT, preferred_element_type=F32)
-        placed = placed[:, :LANES] + placed[:, LANES:]
-        keep_ref[f] = jnp.where(stays, moved_ref[f], placed)
+                    for m in range(4):
+                        at = LANES * f + 64 * k + 16 * m
+                        right_ref[at : at + 16, lanes] = low_ref[16 * m : 16 * m + 16, lanes] * wide
+    placed = lax.dot_general(right_ref[...], left_ref[...], NT, preferred_element_type=F32)
+    for f in range(6):
+        rows = unfold(placed[LANES * f : LANES * f + 64] + placed[LANES * f + 64 : LANES * f + 128])
+        keep_ref[f] = jnp.where(stays, moved_ref[f], rows)
 
     def spread(b, carry):
         at = pl.ds(pl.multiple_of(b * LANES, LANES), LANES)
@@ -430,11 +477,13 @@
     (mine,) = call(
         deposit_kernel, [((LANES, LANES), F32)], sec, vol2, cell2,
         scratch=[dense, pltpu.VMEM((rows, LANES), jnp.int32)] + [dense] * 4 + [pltpu.SemaphoreType.DMA((2,))],
-        smem=(0,), loose=(1, 2), busy_us=4,
+        smem=(0,), hbm=(1, 2), busy_us=4,
     )
     got = shifted(mine, "sec", 1)
+    state_y, state_x = y_starts(STATE)[1], x_starts(STATE)[1]
+    void_y, void_x = y_starts(VOID)[1], x_starts(VOID)[1]
     state, state_up, state_down = call(
-        early_kernel, [((8, 64, LANES), F32), ((8, 40, LANES), F32), ((8, 40, LANES), F32)],
+        early_kernel, [((8, 64, LANES), F32), ((state_y, LANES), F32), ((state_y, LANES), F32)],
         near_p, near_v, far_p, far_v,
     )
     state_ylow = shifted(state_up, "gy", 1)
@@ -444,37 +493,37 @@
         loose=(4,), busy_us=4,
     )
     tile, up, down = call(
-        tile_kernel, [((2, 64, LANES), F32), ((2, 40, LANES), F32), ((2, 40, LANES), F32)], mine, got, base,
+        tile_kernel, [((2, 64, LANES), F32), ((void_y, LANES), F32), ((void_y, LANES), F32)], mine, got, base,
         loose=(2,),
     )
     ylow = shifted(up, "gy", 1)
     yhigh = shifted(down, "gy", -1)
     state_xup, state_xdown = call(
-        side_kernel, [((8, 80, LANES), F32), ((8, 80, LANES), F32)], state, state_ylow, state_yhigh, up, loose=(3,),
+        functools.partial(side_kernel, STATE), [((state_x, LANES), F32), ((state_x, LANES), F32)],
+        state, state_ylow, state_yhigh, up, loose=(3,),
     )
     state_xlow = shifted(state_xup, "gx", 1)
     state_xhigh = shifted(state_xdown, "gx", -1)
-    leave, mask, left, low = call(
-        leave_kernel,
-        [
-            ((8, leavers, LANES), F32), ((LANES, LANES), F32), ((LANES, 4 * movers), BF16),
-            ((LANES, 4 * movers), BF16),
-        ],
-        sec, base, cell2, departures, state_xup,
+    mask, left, low = call(
+        marks_kernel, [((rows, LANES), F32), ((2 * LANES, 4 * movers), BF16), ((64, 4 * movers), BF16)],
+        departures, state_xup, loose=(1,), busy_us=2,
+    )
+    xup, xdown = call(
+        functools.partial(side_kernel, VOID), [((void_x, LANES), F32), ((void_x, LANES), F32)],
+        tile, ylow, yhigh, mask, loose=(3,),
+    )
+    xlow = shifted(xup, "gx", 1)
+    xhigh = shifted(xdown, "gx", -1)
+    (leave,) = call(
+        leave_kernel, [((8, leavers, LANES), F32)], sec, base, cell2, departures, xup,
         scratch=[
             pltpu.VMEM((leavers, LANES), F32), pltpu.VMEM((leavers, LANES), F32),
             pltpu.VMEM((8 * LANES, 2 * LANES), BF16),
         ],
-        smem=(0,), loose=(4,), busy_us=4,
-    )
-    xup, xdown = call(
-        side_kernel, [((2, 80, LANES), F32), ((2, 80, LANES), F32)], tile, ylow, yhigh, leave, loose=(3,),
-    )
-    xlow = shifted(xup, "gx", 1)
-    xhigh = shifted(xdown, "gx", -1)
+        smem=(0,), loose=(4,), busy_us=3,
+    )
     (flow,) = call(
-        flow_kernel, [((4, size, 24, 2 * LANES), F32)], state, state_ylow, state_yhigh, state_xlow, state_xhigh,
-        busy_us=1,
+        flow_kernel, [((4, size, 24, 2 * LANES), F32)], state, state_ylow, state_yhigh, state_xlow, state_xhigh, busy_us=1,
     )
     grid = pltpu.VMEM((size, 24, 2 * LANES), F32)
     p_out, v_out, table, sent = call(
@@ -502,7 +551,7 @@
     pos_out, vel_out = call(
         settle_kernel, [(positions.shape, F32), (velocities.shape, F32)],
         left, low, mask, moved, *arrived,
-        scratch=[pltpu.VMEM((2, 2 * LANES, 4 * movers), BF16), pltpu.VMEM((6, rows, LANES), F32)],
+        scratch=[pltpu.VMEM((6 * LANES, 4 * movers), BF16), pltpu.VMEM((6, rows, LANES), F32)],
         busy_us=4,
     )
     return p_out, v_out, pos_out, vel_out

time: 52.2 us -> 45.8 us (0.88)
  waiting for transfers between devices: 8.06 us -> 1.62 us
  Pallas kernels: 25.1 us -> 22.1 us
  starting transfers between devices: 16.3 us -> 19.3 us
    ppermute x15, waiting for transfers between devices: 8.06 us -> 1.62 us  [shifted(): lax.ppermute(block, axis, [((i - distance) % count, i) for i in range(cou...]
    pallas_call x11 -> x12, Pallas kernels: 25.1 us -> 22.1 us  [call(): pl.pallas_call(kernel, out_shape=outs_list, in_specs=specs, out_specs=[vm...]
    ppermute x15, starting transfers between devices: 16.3 us -> 19.3 us  [shifted(): lax.ppermute(block, axis, [((i - distance) % count, i) for i in range(cou...]
  transfers between devices with their start and end apart: 15 -> 15, of which waited for: 3 -> 1; matrix products, arithmetic and copies ran while one was open for 0% -> 0% of each run, Pallas kernels for 30% -> 35%
where the time goes in v3:
time: 45.8 us; the launch traced here: 45.6 us
  Pallas kernels  22.1 us (48%)
  starting transfers between devices  19.3 us (42%)
  local copies, waits for them, and re-layouts  1.72 us (4%)
  waiting for transfers between devices  1.62 us (4%)
  between operations  0.86 us (2%)
    pallas_call x12, Pallas kernels, call(): pl.pallas_call(kernel, out_shape=outs_list, in_specs=specs, out_specs=[vm...  22.1 us
    ppermute x15, starting transfers between devices, shifted(): lax.ppermute(block, axis, [((i - distance) % count, i) for i in range(cou...  19.3 us
    unnamed x20, local copies, waits for them, and re-layouts  1.71 us
    ppermute x15, waiting for transfers between devices, shifted(): lax.ppermute(block, axis, [((i - distance) % count, i) for i in range(cou...  1.62 us
  transfers between devices with their start and end apart: 15, of which 1 were waited for; matrix products, arithmetic and copies ran while one was open for 0% of the time, Pallas kernels for 35%

profile of v3, /device:TPU:1, one launch (start us, length us, event | category | flops | bytes accessed | tf_op | source)
XLA Modules:
  0.0 45.6 jit_solution(14053222466614348039)
XLA Ops:
  0.6 2.1 %collective-permute-start.1 = (f32[64,128]{1,0:T(8,128)}, f32[64,128]{1,0:T(8,128)S(1)}, u32[]{:S(2)}, u32[]{:S(2)}) collective-permute-start(f32[64,128]{1,0:T(8,128)} %bitcast.12), channel_id=1, source_target_pairs={{1,0},{0,1},{3,2},{2,3},{5,4},{4,5},{7,6},{6,7},{9,8},{8,9},{11,10... | collective-permute-start | bytes 98312 | tf_op jit(solution)/shard_map/ppermute | solution.py:459
  2.8 0.1 collective-permute-start.2
  2.8 0.0 copy-start.4
  2.8 0.8 %copy-done.4 = f32[16384]{0:T(1024)S(1)} copy-done((f32[16384]{0:T(1024)S(1)}, f32[16384]{0:T(1024)}, u32[]{:S(2)}) %copy-start.4) | copy-done | bytes 65560
  3.7 0.0 copy-start.6
  3.7 0.8 %copy-done.6 = s32[16384]{0:T(1024)S(1)} copy-done((s32[16384]{0:T(1024)S(1)}, s32[16384]{0:T(1024)}, u32[]{:S(2)}) %copy-start.6) | copy-done | bytes 65560
  4.5 0.0 copy-start.3
  4.5 0.0 copy-start.8
  4.5 0.0 copy-start
  4.5 0.0 copy-start.1
  4.5 0.0 copy-start.2
  4.5 0.0 copy-start.5
  4.6 3.5 %shard_map.111.mine_ref = f32[128,128]{1,0:T(8,128)S(1)} custom-call(s32[1]{0:T(128)} %bitcast.sec_ref, f32[128,128]{1,0:T(8,128)S(1)} %bitcast.7, s32[128,128]{1,0:T(8,128)S(1)} %bitcast.9), custom_call_target="tpu_custom_call" | custom-call | flops 4600000000 | bytes 4096 | tf_op jit(solution)/shard_map/pallas_call | solution.py:37
  8.1 1.4 %collective-permute-start = (f32[128,128]{1,0:T(8,128)S(1)}, f32[128,128]{1,0:T(8,128)S(1)}, u32[]{:S(2)}, u32[]{:S(2)}) collective-permute-start(f32[128,128]{1,0:T(8,128)S(1)} %shard_map.111.mine_ref), channel_id=1, source_target_pairs={{1,0},{0,1},{3,2},{2,3},{5,4},{4,5},{7,6},{6,7},{9,8},{8,9},{11,10... | collective-permute-start | bytes 196616 | tf_op jit(solution)/shard_map/ppermute | solution.py:459
  9.5 0.0 collective-permute-done.1.far_p_ref
  9.5 0.0 collective-permute-done.2.far_v_ref
  9.5 0.0 copy-done.3
  9.5 0.0 copy-done.8
  9.5 0.1 shard_map.112
  9.6 1.4 %collective-permute-start.5 = (f32[288,128]{1,0:T(8,128)S(1)}, f32[288,128]{1,0:T(8,128)S(1)}, u32[]{:S(2)}, u32[]{:S(2)}) collective-permute-start(f32[288,128]{1,0:T(8,128)S(1)} %get-tuple-element.27), channel_id=1, source_target_pairs={{6,0},{0,2},{2,4},{4,6},{7,1},{1,3},{3,5},{5,7},{14,8},{8,10},{10,... | collective-permute-start | bytes 442376 | tf_op jit(solution)/shard_map/ppermute | solution.py:459
  11.0 2.1 %collective-permute-start.6 = (f32[288,128]{1,0:T(8,128)S(1)}, f32[288,128]{1,0:T(8,128)S(1)}, u32[]{:S(2)}, u32[]{:S(2)}) collective-permute-start(f32[288,128]{1,0:T(8,128)S(1)} %get-tuple-element.28), channel_id=1, source_target_pairs={{2,0},{4,2},{6,4},{0,6},{3,1},{5,3},{7,5},{1,7},{10,8},{12,10},{14... | collective-permute-start | bytes 442376 | tf_op jit(solution)/shard_map/ppermute | solution.py:459
  13.1 0.0 copy-done
  13.1 0.0 copy-done.1
  13.1 0.0 copy-done.2
  13.1 0.0 copy-done.5
  13.1 0.0 copy-start.9
  13.1 3.0 %shard_map.113.after_ref.base_ref = f32[7,128,128]{2,1,0:T(8,128)S(1)} custom-call(f32[128,128]{1,0:T(8,128)S(1)} %bitcast.8, f32[3,16384]{1,0:T(4,128)S(1)} %copy-done.1, f32[3,16384]{1,0:T(4,128)S(1)} %copy-done.2, s32[8,16384]{1,0:T(8,128)S(1)} %copy-done, f32[8,64,128]{2,1,0:T(8,128)S(1)} %get-tuple-element.23.after_ref.tile_ref), custom_call_target="tpu_custom_call" | custom-call | flops 4600000000 | bytes 4096 | tf_op jit(solution)/shard_map/pallas_call | solution.py:37
  16.1 0.0 collective-permute-done.got_ref
  16.1 1.5 %collective-permute-start.4 = (f32[80,128]{1,0:T(8,128)S(1)}, f32[80,128]{1,0:T(8,128)S(1)}, u32[]{:S(2)}, u32[]{:S(2)}) collective-permute-start(f32[80,128]{1,0:T(8,128)S(1)} %get-tuple-element.26), channel_id=1, source_target_pairs={{2,0},{4,2},{6,4},{0,6},{3,1},{5,3},{7,5},{1,7},{10,8},{12,10},{14... | collective-permute-start | bytes 122888 | tf_op jit(solution)/shard_map/ppermute | solution.py:459
  17.6 0.1 collective-permute-start.3
  17.6 0.0 collective-permute-done.5.low_ref.ylow_ref
  17.6 1.6 %collective-permute-done.6.high_ref.yhigh_ref = f32[288,128]{1,0:T(8,128)S(1)} collective-permute-done((f32[288,128]{1,0:T(8,128)S(1)}, f32[288,128]{1,0:T(8,128)S(1)}, u32[]{:S(2)}, u32[]{:S(2)}) %collective-permute-start.6) | collective-permute-done | bytes 147488 | tf_op jit(solution)/shard_map/ppermute | solution.py:459
  19.2 0.1 shard_map.115
  19.3 1.7 %collective-permute-start.10 = (f32[432,128]{1,0:T(8,128)S(1)}, f32[432,128]{1,0:T(8,128)S(1)}, u32[]{:S(2)}, u32[]{:S(2)}) collective-permute-start(f32[432,128]{1,0:T(8,128)S(1)} %get-tuple-element.33), channel_id=1, source_target_pairs={{8,0},{16,8},{24,16},{0,24},{9,1},{17,9},{25,17},{1,25},{10,2},{18... | collective-permute-start | bytes 663560 | tf_op jit(solution)/shard_map/ppermute | solution.py:459
  21.0 0.0 copy-start.7
  21.0 1.2 %collective-permute-start.9 = (f32[432,128]{1,0:T(8,128)S(1)}, f32[432,128]{1,0:T(8,128)S(1)}, u32[]{:S(2)}, u32[]{:S(2)}) collective-permute-start(f32[432,128]{1,0:T(8,128)S(1)} %get-tuple-element.29.after_ref), channel_id=1, source_target_pairs={{24,0},{0,8},{8,16},{16,24},{25,1},{1,9},{9,17},{17,25},{26,2},{2,... | collective-permute-start | bytes 663560 | tf_op jit(solution)/shard_map/ppermute | solution.py:459
  22.1 0.0 copy-done.9
  22.1 1.0 %shard_map.116 = (f32[128,128]{1,0:T(8,128)S(1)}, bf16[256,4096]{1,0:T(8,128)(2,1)S(1)}, bf16[64,4096]{1,0:T(8,128)(2,1)S(1)}) custom-call(s32[4,1024]{1,0:T(4,128)S(1)} %copy-done.9, f32[432,128]{1,0:T(8,128)S(1)} %get-tuple-element.29.after_ref), custom_call_target="tpu_custom_call" | custom-call | flops 2300000000 | bytes 4096 | tf_op jit(solution)/shard_map/pallas_call | solution.py:37
  23.1 0.0 collective-permute-done.4.high_ref.yhigh_ref
  23.1 0.0 collective-permute-done.3.low_ref.ylow_ref
  23.2 2.6 %collective-permute-start.8 = (f32[120,128]{1,0:T(8,128)S(1)}, f32[120,128]{1,0:T(8,128)S(1)}, u32[]{:S(2)}, u32[]{:S(2)}) collective-permute-start(f32[120,128]{1,0:T(8,128)S(1)} %get-tuple-element.32), channel_id=1, source_target_pairs={{8,0},{16,8},{24,16},{0,24},{9,1},{17,9},{25,17},{1,25},{10,2},{18... | collective-permute-start | bytes 184328 | tf_op jit(solution)/shard_map/ppermute | solution.py:459
  25.8 1.2 %collective-permute-start.7 = (f32[120,128]{1,0:T(8,128)S(1)}, f32[120,128]{1,0:T(8,128)S(1)}, u32[]{:S(2)}, u32[]{:S(2)}) collective-permute-start(f32[120,128]{1,0:T(8,128)S(1)} %get-tuple-element.31.after_ref), channel_id=1, source_target_pairs={{24,0},{0,8},{8,16},{16,24},{25,1},{1,9},{9,17},{17,25},{26,2},{2,... | collective-permute-start | bytes 184328 | tf_op jit(solution)/shard_map/ppermute | solution.py:459
  26.9 0.0 copy-done.7
  27.0 2.8 %shard_map.119.leave_ref = f32[8,32,128]{2,1,0:T(8,128)S(1)} custom-call(s32[1]{0:T(128)} %bitcast.sec_ref, f32[7,128,128]{2,1,0:T(8,128)S(1)} %shard_map.113.after_ref.base_ref, s32[128,128]{1,0:T(8,128)S(1)} %bitcast.10, s32[4,1024]{1,0:T(4,128)S(1)} %copy-done.9, f32[120,128]{1,0:T(8,128)S(1)} %get-tuple-element.31.after_ref), custom_call_target="tpu_custom_call" | custom-call | flops 3449999872 | bytes 4096 | tf_op jit(solution)/shard_map/pallas_call | solution.py:37
  29.7 0.0 collective-permute-done.10.xhigh_ref
  29.7 0.0 collective-permute-done.9.xlow_ref
  29.7 0.2 shard_map.118.flow_ref
  29.9 0.0 collective-permute-done.8.xhigh_ref
  30.0 0.0 collective-permute-done.7.xlow_ref
  30.0 3.0 %shard_map.120 = (f32[8,8,128]{2,1,0:T(8,128)}, f32[3,8,8,128]{3,2,1,0:T(8,128)}, bf16[512,256]{1,0:T(8,128)(2,1)S(1)}, f32[6,32,128]{2,1,0:T(8,128)S(1)}) custom-call(f32[2,64,128]{2,1,0:T(8,128)S(1)} %get-tuple-element.24.tile_ref, f32[80,128]{1,0:T(8,128)S(1)} %collective-permute-done.3.low_ref.ylow_ref, ...), custom_call_target="tpu_custom_call" | custom-call | flops 6899999744 | bytes 4096 | tf_op jit(solution)/shard_map/pallas_call | solution.py:37
  33.0 2.3 %collective-permute-start.14 = (f32[6,8,128]{2,1,0:T(8,128)S(1)}, f32[6,8,128]{2,1,0:T(8,128)S(1)}, u32[]{:S(2)}, u32[]{:S(2)}) collective-permute-start(f32[6,8,128]{2,1,0:T(8,128)S(1)} %get-tuple-element.42), channel_id=1, source_target_pairs={{2,0},{4,2},{6,4},{0,6},{3,1},{5,3},{7,5},{1,7},{10,8},{12,10},{14... | collective-permute-start | bytes 73736 | tf_op jit(solution)/shard_map/ppermute | solution.py:459
  35.4 0.0 collective-permute-start.13
  35.4 0.7 %collective-permute-start.12 = (f32[6,8,128]{2,1,0:T(8,128)S(1)}, f32[6,8,128]{2,1,0:T(8,128)S(1)}, u32[]{:S(2)}, u32[]{:S(2)}) collective-permute-start(f32[6,8,128]{2,1,0:T(8,128)S(1)} %get-tuple-element.44), channel_id=1, source_target_pairs={{8,0},{16,8},{24,16},{0,24},{9,1},{17,9},{25,17},{1,25},{10,2},{18... | collective-permute-start | bytes 73736 | tf_op jit(solution)/shard_map/ppermute | solution.py:459
  36.1 1.0 %collective-permute-start.11 = (f32[6,8,128]{2,1,0:T(8,128)S(1)}, f32[6,8,128]{2,1,0:T(8,128)S(1)}, u32[]{:S(2)}, u32[]{:S(2)}) collective-permute-start(f32[6,8,128]{2,1,0:T(8,128)S(1)} %get-tuple-element.45), channel_id=1, source_target_pairs={{24,0},{0,8},{8,16},{16,24},{25,1},{1,9},{9,17},{17,25},{26,2},{2,... | collective-permute-start | bytes 73736 | tf_op jit(solution)/shard_map/ppermute | solution.py:459
  37.1 5.2 %shard_map.121.moved_ref = f32[6,128,128]{2,1,0:T(8,128)S(1)} custom-call(s32[1]{0:T(128)} %bitcast.sec_ref, bf16[512,256]{1,0:T(8,128)(2,1)S(1)} %get-tuple-element.38.table_ref, s32[128,128]{1,0:T(8,128)S(1)} %bitcast.11, f32[7,128,128]{2,1,0:T(8,128)S(1)} %shard_map.113.after_ref.base_ref), custom_call_target="tpu_custom_call" | custom-call | flops 6899999744 | bytes 4096 | tf_op jit(solution)/shard_map/pallas_call | solution.py:37
  42.3 0.0 collective-permute-done.14.d_ref
  42.3 0.0 collective-permute-done.13.c_ref
  42.3 0.0 collective-permute-done.12.b_ref
  42.4 0.0 collective-permute-done.11.a_ref
  42.4 3.2 %shard_map.122 = (f32[3,16384]{1,0:T(4,128)}, f32[3,16384]{1,0:T(4,128)}) custom-call(bf16[256,4096]{1,0:T(8,128)(2,1)S(1)} %get-tuple-element.36.left_ref, bf16[64,4096]{1,0:T(8,128)(2,1)S(1)} %get-tuple-element.37.low_ref, f32[128,128]{1,0:T(8,128)S(1)} %get-tuple-element.30.after_ref.mask_ref, f32[6,128,128]{2,1,0:T(8,128)S(1)} %shard_map.121.moved_ref, ...), custom_call_target="tpu_custom_call" | custom-call | flops 4600000000 | bytes 4096 | tf_op jit(solution)/shard_map/pallas_call | solution.py:37
  (3 shorter events, 0.1 us)
Async XLA Ops:
  0.6 8.9 %collective-permute-start.1 = (f32[64,128]{1,0:T(8,128)}, f32[64,128]{1,0:T(8,128)S(1)}, u32[]{:S(2)}, u32[]{:S(2)}) collective-permute-start(f32[64,128]{1,0:T(8,128)} %bitcast.12), channel_id=1, source_target_pairs={{1,0},{0,1},{3,2},{2,3},{5,4},{4,5},{7,6},{6,7},{9,8},{8,9},{11,10... | collective-permute-start | bytes 98312 | tf_op jit(solution)/shard_map/ppermute | solution.py:459
  2.8 6.8 %collective-permute-start.2 = (f32[192,128]{1,0:T(8,128)}, f32[192,128]{1,0:T(8,128)S(1)}, u32[]{:S(2)}, u32[]{:S(2)}) collective-permute-start(f32[192,128]{1,0:T(8,128)} %bitcast.5), channel_id=1, source_target_pairs={{1,0},{0,1},{3,2},{2,3},{5,4},{4,5},{7,6},{6,7},{9,8},{8,9},{11,10... | collective-permute-start | bytes 294920 | tf_op jit(solution)/shard_map/ppermute | solution.py:459
  2.8 0.8 %copy-start.4 = (f32[16384]{0:T(1024)S(1)}, f32[16384]{0:T(1024)}, u32[]{:S(2)}) copy-start(f32[16384]{0:T(1024)} %param.12) | copy-start | bytes 196612
  3.7 0.8 %copy-start.6 = (s32[16384]{0:T(1024)S(1)}, s32[16384]{0:T(1024)}, u32[]{:S(2)}) copy-start(s32[16384]{0:T(1024)} %param.13) | copy-start | bytes 196612
  4.5 5.0 %copy-start.3 = (f32[3,8,8,128]{3,2,1,0:T(8,128)S(1)}, f32[3,8,8,128]{3,2,1,0:T(8,128)}, u32[]{:S(2)}) copy-start(f32[3,8,8,128]{3,2,1,0:T(8,128)} %param.9) | copy-start | bytes 294916
  4.5 5.0 %copy-start.8 = (f32[8,8,128]{2,1,0:T(8,128)S(1)}, f32[8,8,128]{2,1,0:T(8,128)}, u32[]{:S(2)}) copy-start(f32[8,8,128]{2,1,0:T(8,128)} %param.8) | copy-start | bytes 98308
  4.5 8.5 %copy-start = (s32[8,16384]{1,0:T(8,128)S(1)}, s32[8,16384]{1,0:T(8,128)}, u32[]{:S(2)}) copy-start(s32[8,16384]{1,0:T(8,128)} %pair_ref.1) | copy-start | bytes 1572868
  4.5 8.5 %copy-start.1 = (f32[3,16384]{1,0:T(4,128)S(1)}, f32[3,16384]{1,0:T(4,128)}, u32[]{:S(2)}) copy-start(f32[3,16384]{1,0:T(4,128)} %pos_ref.1) | copy-start | bytes 589828
  4.5 8.5 %copy-start.2 = (f32[3,16384]{1,0:T(4,128)S(1)}, f32[3,16384]{1,0:T(4,128)}, u32[]{:S(2)}) copy-start(f32[3,16384]{1,0:T(4,128)} %vel_ref.1) | copy-start | bytes 589828
  4.5 8.5 %copy-start.5 = (f32[16384]{0:T(1024)S(1)}, f32[16384]{0:T(1024)}, u32[]{:S(2)}) copy-start(f32[16384]{0:T(1024)} %param.12) | copy-start | bytes 196612
  8.1 8.0 %collective-permute-start = (f32[128,128]{1,0:T(8,128)S(1)}, f32[128,128]{1,0:T(8,128)S(1)}, u32[]{:S(2)}, u32[]{:S(2)}) collective-permute-start(f32[128,128]{1,0:T(8,128)S(1)} %shard_map.111.mine_ref), channel_id=1, source_target_pairs={{1,0},{0,1},{3,2},{2,3},{5,4},{4,5},{7,6},{6,7},{9,8},{8,9},{11,10... | collective-permute-start | bytes 196616 | tf_op jit(solution)/shard_map/ppermute | solution.py:459
  9.6 8.0 %collective-permute-start.5 = (f32[288,128]{1,0:T(8,128)S(1)}, f32[288,128]{1,0:T(8,128)S(1)}, u32[]{:S(2)}, u32[]{:S(2)}) collective-permute-start(f32[288,128]{1,0:T(8,128)S(1)} %get-tuple-element.27), channel_id=1, source_target_pairs={{6,0},{0,2},{2,4},{4,6},{7,1},{1,3},{3,5},{5,7},{14,8},{8,10},{10,... | collective-permute-start | bytes 442376 | tf_op jit(solution)/shard_map/ppermute | solution.py:459
  11.0 8.2 %collective-permute-start.6 = (f32[288,128]{1,0:T(8,128)S(1)}, f32[288,128]{1,0:T(8,128)S(1)}, u32[]{:S(2)}, u32[]{:S(2)}) collective-permute-start(f32[288,128]{1,0:T(8,128)S(1)} %get-tuple-element.28), channel_id=1, source_target_pairs={{2,0},{4,2},{6,4},{0,6},{3,1},{5,3},{7,5},{1,7},{10,8},{12,10},{14... | collective-permute-start | bytes 442376 | tf_op jit(solution)/shard_map/ppermute | solution.py:459
  13.1 9.1 %copy-start.9 = (s32[4,1024]{1,0:T(4,128)S(1)}, s32[4,1024]{1,0:T(4,128)}, u32[]{:S(2)}) copy-start(s32[4,1024]{1,0:T(4,128)} %dep_ref.3) | copy-start | bytes 49156
  16.1 7.0 %collective-permute-start.4 = (f32[80,128]{1,0:T(8,128)S(1)}, f32[80,128]{1,0:T(8,128)S(1)}, u32[]{:S(2)}, u32[]{:S(2)}) collective-permute-start(f32[80,128]{1,0:T(8,128)S(1)} %get-tuple-element.26), channel_id=1, source_target_pairs={{2,0},{4,2},{6,4},{0,6},{3,1},{5,3},{7,5},{1,7},{10,8},{12,10},{14... | collective-permute-start | bytes 122888 | tf_op jit(solution)/shard_map/ppermute | solution.py:459
  17.6 5.6 %collective-permute-start.3 = (f32[80,128]{1,0:T(8,128)S(1)}, f32[80,128]{1,0:T(8,128)S(1)}, u32[]{:S(2)}, u32[]{:S(2)}) collective-permute-start(f32[80,128]{1,0:T(8,128)S(1)} %get-tuple-element.25.after_ref), channel_id=1, source_target_pairs={{6,0},{0,2},{2,4},{4,6},{7,1},{1,3},{3,5},{5,7},{14,8},{8,10},{10,... | collective-permute-start | bytes 122888 | tf_op jit(solution)/shard_map/ppermute | solution.py:459
  19.3 10.4 %collective-permute-start.10 = (f32[432,128]{1,0:T(8,128)S(1)}, f32[432,128]{1,0:T(8,128)S(1)}, u32[]{:S(2)}, u32[]{:S(2)}) collective-permute-start(f32[432,128]{1,0:T(8,128)S(1)} %get-tuple-element.33), channel_id=1, source_target_pairs={{8,0},{16,8},{24,16},{0,24},{9,1},{17,9},{25,17},{1,25},{10,2},{18... | collective-permute-start | bytes 663560 | tf_op jit(solution)/shard_map/ppermute | solution.py:459
  21.0 6.0 %copy-start.7 = (s32[16384]{0:T(1024)S(1)}, s32[16384]{0:T(1024)}, u32[]{:S(2)}) copy-start(s32[16384]{0:T(1024)} %param.13) | copy-start | bytes 196612
  21.0 8.8 %collective-permute-start.9 = (f32[432,128]{1,0:T(8,128)S(1)}, f32[432,128]{1,0:T(8,128)S(1)}, u32[]{:S(2)}, u32[]{:S(2)}) collective-permute-start(f32[432,128]{1,0:T(8,128)S(1)} %get-tuple-element.29.after_ref), channel_id=1, source_target_pairs={{24,0},{0,8},{8,16},{16,24},{25,1},{1,9},{9,17},{17,25},{26,2},{2,... | collective-permute-start | bytes 663560 | tf_op jit(solution)/shard_map/ppermute | solution.py:459
  23.2 6.8 %collective-permute-start.8 = (f32[120,128]{1,0:T(8,128)S(1)}, f32[120,128]{1,0:T(8,128)S(1)}, u32[]{:S(2)}, u32[]{:S(2)}) collective-permute-start(f32[120,128]{1,0:T(8,128)S(1)} %get-tuple-element.32), channel_id=1, source_target_pairs={{8,0},{16,8},{24,16},{0,24},{9,1},{17,9},{25,17},{1,25},{10,2},{18... | collective-permute-start | bytes 184328 | tf_op jit(solution)/shard_map/ppermute | solution.py:459
  25.8 4.2 %collective-permute-start.7 = (f32[120,128]{1,0:T(8,128)S(1)}, f32[120,128]{1,0:T(8,128)S(1)}, u32[]{:S(2)}, u32[]{:S(2)}) collective-permute-start(f32[120,128]{1,0:T(8,128)S(1)} %get-tuple-element.31.after_ref), channel_id=1, source_target_pairs={{24,0},{0,8},{8,16},{16,24},{25,1},{1,9},{9,17},{17,25},{26,2},{2,... | collective-permute-start | bytes 184328 | tf_op jit(solution)/shard_map/ppermute | solution.py:459
  33.0 9.3 %collective-permute-start.14 = (f32[6,8,128]{2,1,0:T(8,128)S(1)}, f32[6,8,128]{2,1,0:T(8,128)S(1)}, u32[]{:S(2)}, u32[]{:S(2)}) collective-permute-start(f32[6,8,128]{2,1,0:T(8,128)S(1)} %get-tuple-element.42), channel_id=1, source_target_pairs={{2,0},{4,2},{6,4},{0,6},{3,1},{5,3},{7,5},{1,7},{10,8},{12,10},{14... | collective-permute-start | bytes 73736 | tf_op jit(solution)/shard_map/ppermute | solution.py:459
  35.4 7.0 %collective-permute-start.13 = (f32[6,8,128]{2,1,0:T(8,128)S(1)}, f32[6,8,128]{2,1,0:T(8,128)S(1)}, u32[]{:S(2)}, u32[]{:S(2)}) collective-permute-start(f32[6,8,128]{2,1,0:T(8,128)S(1)} %get-tuple-element.43), channel_id=1, source_target_pairs={{6,0},{0,2},{2,4},{4,6},{7,1},{1,3},{3,5},{5,7},{14,8},{8,10},{10,... | collective-permute-start | bytes 73736 | tf_op jit(solution)/shard_map/ppermute | solution.py:459
  35.4 7.0 %collective-permute-start.12 = (f32[6,8,128]{2,1,0:T(8,128)S(1)}, f32[6,8,128]{2,1,0:T(8,128)S(1)}, u32[]{:S(2)}, u32[]{:S(2)}) collective-permute-start(f32[6,8,128]{2,1,0:T(8,128)S(1)} %get-tuple-element.44), channel_id=1, source_target_pairs={{8,0},{16,8},{24,16},{0,24},{9,1},{17,9},{25,17},{1,25},{10,2},{18... | collective-permute-start | bytes 73736 | tf_op jit(solution)/shard_map/ppermute | solution.py:459
  36.1 6.3 %collective-permute-start.11 = (f32[6,8,128]{2,1,0:T(8,128)S(1)}, f32[6,8,128]{2,1,0:T(8,128)S(1)}, u32[]{:S(2)}, u32[]{:S(2)}) collective-permute-start(f32[6,8,128]{2,1,0:T(8,128)S(1)} %get-tuple-element.45), channel_id=1, source_target_pairs={{24,0},{0,8},{8,16},{16,24},{25,1},{1,9},{9,17},{17,25},{26,2},{2,... | collective-permute-start | bytes 73736 | tf_op jit(solution)/shard_map/ppermute | solution.py:459

commit v4 on v3

--- a/solution.py
+++ b/solution.py
@@ -24,16 +24,12 @@
 NT = (((1,), (1,)), ((), ()))
 
 
-def call(kernel, outs, *args, scratch=(), busy_us=0.1, smem=(), loose=(), hbm=()):
+def call(kernel, outs, *args, scratch=(), busy_us=0.1, smem=(), loose=()):
     outs_list = [jax.ShapeDtypeStruct(shape, dtype) for shape, dtype in outs]
     vmem = pl.BlockSpec(memory_space=pltpu.VMEM)
     scalar = pl.BlockSpec(memory_space=pltpu.SMEM)
     anywhere = pl.BlockSpec(memory_space=pl.ANY)
-    outside = pl.BlockSpec(memory_space=pltpu.HBM)
-    specs = [
-        scalar if i in smem else anywhere if i in loose else outside if i in hbm else vmem
-        for i in range(len(args))
-    ]
+    specs = [scalar if i in smem else anywhere if i in loose else vmem for i in range(len(args))]
     return pl.pallas_call(
         kernel,
         out_shape=outs_list,
@@ -72,17 +68,11 @@
     return high, cells & (LANES - 1)
 
 
-def deposit_kernel(
-    sec_ref, vol_in, cell_in, out_ref, vol_ref, cell_ref, hi_ref, lo_ref, va_ref, vb_ref, sems,
-):
-    copies = [
-        pltpu.make_async_copy(vol_in, vol_ref, sems.at[0]),
-        pltpu.make_async_copy(cell_in, cell_ref, sems.at[1]),
-    ]
-    for copy in copies:
-        copy.start()
-    for copy in copies:
-        copy.wait()
+def ahead_kernel(out_ref):
+    out_ref[...] = jnp.zeros(out_ref.shape, F32)
+
+
+def deposit_kernel(sec_ref, vol_ref, cell_ref, after_ref, out_ref, hi_ref, lo_ref, va_ref, vb_ref):
     sec = sec_ref[0]
     high, low = cell_split(cell_ref[...], sec)
     hi_ref[...] = high.astype(F32)
@@ -114,7 +104,7 @@
         right = jnp.concatenate(rights, axis=1)
         return acc + lax.dot_general(left, right, NT, preferred_element_type=F32)
 
-    acc = lax.fori_loop(0, steps, step, jnp.zeros((LANES, 2 * LANES), F32), unroll=2)
+    acc = lax.fori_loop(0, steps, step, jnp.zeros((LANES, 2 * LANES), F32), unroll=4)
     out_ref[...] = acc[:, :LANES] + acc[:, LANES:]
 
 
@@ -140,7 +130,7 @@
             base_ref[3 + d, pl.ds(b, 1), :] = mine[3 + d] + TIME_STEP * force
         return carry
 
-    lax.fori_loop(0, blocks, step, 0, unroll=8)
+    lax.fori_loop(0, blocks, step, 0, unroll=32)
 
 
 def table_of(fields, table_ref):
@@ -209,7 +199,7 @@
                 out_ref[f, ats[h], :] = found[f][h]
         return carry
 
-    lax.fori_loop(0, 2 * per, step, 0, unroll=8)
+    lax.fori_loop(0, 2 * per, step, 0, unroll=16)
 
 
 STATE = ((HALO, HALO, HALO), (HALO - 1, HALO, HALO), (HALO, HALO - 1, HALO), (HALO - 1, HALO - 1, HALO - 1))
@@ -385,7 +375,7 @@
                 sent_ref[f, pl.ds(2 * i + h, 1), :] = found[f][h]
         return carry
 
-    lax.fori_loop(0, count // 2, step, 0, unroll=8)
+    lax.fori_loop(0, count // 2, step, 0, unroll=16)
     drag = TIME_STEP * sent_ref[0] * leave_ref[6]
     scale = 1.0 / (1.0 + drag)
     speeds = [(leave_ref[3 + d] + drag * sent_ref[1 + d]) * scale for d in range(3)]
@@ -414,7 +404,7 @@
                 out_ref[f, ats[h], :] = found[f][h]
         return carry
 
-    lax.fori_loop(0, rows // 2, step, 0, unroll=16)
+    lax.fori_loop(0, rows // 2, step, 0, unroll=32)
     drag = TIME_STEP * out_ref[0] * base_ref[6]
     scale = 1.0 / (1.0 + drag)
     speeds = [(base_ref[3 + d] + drag * out_ref[1 + d]) * scale for d in range(3)]
@@ -474,10 +464,10 @@
 
     far_p = shifted(near_p, "sec", 1)
     far_v = shifted(near_v, "sec", 1)
+    (ahead,) = call(ahead_kernel, [((8, LANES), F32)], busy_us=3)
     (mine,) = call(
-        deposit_kernel, [((LANES, LANES), F32)], sec, vol2, cell2,
-        scratch=[dense, pltpu.VMEM((rows, LANES), jnp.int32)] + [dense] * 4 + [pltpu.SemaphoreType.DMA((2,))],
-        smem=(0,), hbm=(1, 2), busy_us=4,
+        deposit_kernel, [((LANES, LANES), F32)], sec, vol2, cell2, ahead,
+        scratch=[dense] * 4, smem=(0,), loose=(3,), busy_us=4,
     )
     got = shifted(mine, "sec", 1)
     state_y, state_x = y_starts(STATE)[1], x_starts(STATE)[1]

time: 45.8 us -> 44.1 us (0.963)
  Pallas kernels: 22.1 us -> 19.4 us
  waiting for transfers between devices: 1.62 us -> 4.04 us
  local copies, waits for them, and re-layouts: 1.72 us -> 0.9 us
  starting transfers between devices: 19.3 us -> 18.7 us
    pallas_call x12 -> x13, Pallas kernels: 22.1 us -> 19.4 us  [call(): pl.pallas_call(kernel, out_shape=outs_list, in_specs=specs, out_specs=[vm...]
    ppermute x15, waiting for transfers between devices: 1.62 us -> 4.04 us  [shifted(): lax.ppermute(block, axis, [((i - distance) % count, i) for i in range(cou...]
    unnamed x20 -> x16, local copies, waits for them, and re-layouts: 1.71 us -> 0.89 us
    ppermute x15, starting transfers between devices: 19.3 us -> 18.7 us  [shifted(): lax.ppermute(block, axis, [((i - distance) % count, i) for i in range(cou...]
  transfers between devices with their start and end apart: 15 -> 15, of which waited for: 1 -> 3; matrix products, arithmetic and copies ran while one was open for 0% -> 0% of each run, Pallas kernels for 35% -> 30%
where the time goes in v4:
time: 44.1 us; the launch traced here: 43.9 us
  Pallas kernels  19.4 us (44%)
  starting transfers between devices  18.7 us (42%)
  waiting for transfers between devices  4.04 us (9%)
  local copies, waits for them, and re-layouts  0.9 us (2%)
  between operations  0.81 us (2%)
    pallas_call x13, Pallas kernels, call(): pl.pallas_call(kernel, out_shape=outs_list, in_specs=specs, out_specs=[vm...  19.4 us
    ppermute x15, starting transfers between devices, shifted(): lax.ppermute(block, axis, [((i - distance) % count, i) for i in range(cou...  18.7 us
    ppermute x15, waiting for transfers between devices, shifted(): lax.ppermute(block, axis, [((i - distance) % count, i) for i in range(cou...  4.04 us
    unnamed x16, local copies, waits for them, and re-layouts  0.89 us
  transfers between devices with their start and end apart: 15, of which 3 were waited for; matrix products, arithmetic and copies ran while one was open for 0% of the time, Pallas kernels for 30%

profile of v4, /device:TPU:1, one launch (start us, length us, event | category | flops | bytes accessed | tf_op | source)
XLA Modules:
  0.0 43.9 jit_solution(13701246538896674156)
XLA Ops:
  0.6 2.1 %collective-permute-start.1 = (f32[64,128]{1,0:T(8,128)}, f32[64,128]{1,0:T(8,128)S(1)}, u32[]{:S(2)}, u32[]{:S(2)}) collective-permute-start(f32[64,128]{1,0:T(8,128)} %bitcast.12), channel_id=1, source_target_pairs={{1,0},{0,1},{3,2},{2,3},{5,4},{4,5},{7,6},{6,7},{9,8},{8,9},{11,10... | collective-permute-start | bytes 98312 | tf_op jit(solution)/shard_map/ppermute | solution.py:449
  2.8 0.1 collective-permute-start.2
  2.8 0.0 copy-start.4
  2.8 0.0 copy-start.5
  2.9 0.8 %copy-done.4 = f32[16384]{0:T(1024)S(1)} copy-done((f32[16384]{0:T(1024)S(1)}, f32[16384]{0:T(1024)}, u32[]{:S(2)}) %copy-start.4) | copy-done | bytes 65560
  3.7 0.0 copy-done.5
  3.7 0.0 copy-start.3
  3.7 0.0 copy-start.6
  3.7 0.0 copy-start
  3.7 0.0 copy-start.1
  3.7 0.0 copy-start.2
  3.7 3.0 %shard_map.112.mine_ref = f32[128,128]{1,0:T(8,128)S(1)} custom-call(s32[1]{0:T(128)} %bitcast.sec_ref, f32[128,128]{1,0:T(8,128)S(1)} %bitcast.7, s32[128,128]{1,0:T(8,128)S(1)} %bitcast.9, f32[8,128]{1,0:T(8,128)S(1)} %shard_map.111.after_ref), custom_call_target="tpu_custom_call" | custom-call | flops 4600000000 | bytes 4096 | tf_op jit(solution)/shard_map/pallas_call | solution.py:33
  6.8 1.4 %collective-permute-start = (f32[128,128]{1,0:T(8,128)S(1)}, f32[128,128]{1,0:T(8,128)S(1)}, u32[]{:S(2)}, u32[]{:S(2)}) collective-permute-start(f32[128,128]{1,0:T(8,128)S(1)} %shard_map.112.mine_ref), channel_id=1, source_target_pairs={{1,0},{0,1},{3,2},{2,3},{5,4},{4,5},{7,6},{6,7},{9,8},{8,9},{11,10... | collective-permute-start | bytes 196616 | tf_op jit(solution)/shard_map/ppermute | solution.py:449
  8.2 0.0 collective-permute-done.1.far_p_ref
  8.2 0.0 collective-permute-done.2.far_v_ref
  8.2 0.0 copy-done.3
  8.2 0.0 copy-done.6
  8.2 0.1 shard_map.113
  8.3 1.4 %collective-permute-start.5 = (f32[288,128]{1,0:T(8,128)S(1)}, f32[288,128]{1,0:T(8,128)S(1)}, u32[]{:S(2)}, u32[]{:S(2)}) collective-permute-start(f32[288,128]{1,0:T(8,128)S(1)} %get-tuple-element.27), channel_id=1, source_target_pairs={{6,0},{0,2},{2,4},{4,6},{7,1},{1,3},{3,5},{5,7},{14,8},{8,10},{10,... | collective-permute-start | bytes 442376 | tf_op jit(solution)/shard_map/ppermute | solution.py:449
  9.7 2.1 %collective-permute-start.6 = (f32[288,128]{1,0:T(8,128)S(1)}, f32[288,128]{1,0:T(8,128)S(1)}, u32[]{:S(2)}, u32[]{:S(2)}) collective-permute-start(f32[288,128]{1,0:T(8,128)S(1)} %get-tuple-element.28), channel_id=1, source_target_pairs={{2,0},{4,2},{6,4},{0,6},{3,1},{5,3},{7,5},{1,7},{10,8},{12,10},{14... | collective-permute-start | bytes 442376 | tf_op jit(solution)/shard_map/ppermute | solution.py:449
  11.8 0.0 copy-done
  11.8 0.0 copy-done.1
  11.8 0.0 copy-done.2
  11.8 0.0 copy-start.7
  11.8 1.7 %shard_map.114.after_ref.base_ref = f32[7,128,128]{2,1,0:T(8,128)S(1)} custom-call(f32[128,128]{1,0:T(8,128)S(1)} %bitcast.8, f32[3,16384]{1,0:T(4,128)S(1)} %copy-done.1, f32[3,16384]{1,0:T(4,128)S(1)} %copy-done.2, s32[8,16384]{1,0:T(8,128)S(1)} %copy-done, f32[8,64,128]{2,1,0:T(8,128)S(1)} %get-tuple-element.23.after_ref.tile_ref), custom_call_target="tpu_custom_call" | custom-call | flops 4600000000 | bytes 4096 | tf_op jit(solution)/shard_map/pallas_call | solution.py:33
  13.5 0.0 collective-permute-done.got_ref
  13.5 1.5 %collective-permute-start.4 = (f32[80,128]{1,0:T(8,128)S(1)}, f32[80,128]{1,0:T(8,128)S(1)}, u32[]{:S(2)}, u32[]{:S(2)}) collective-permute-start(f32[80,128]{1,0:T(8,128)S(1)} %get-tuple-element.26), channel_id=1, source_target_pairs={{2,0},{4,2},{6,4},{0,6},{3,1},{5,3},{7,5},{1,7},{10,8},{12,10},{14... | collective-permute-start | bytes 122888 | tf_op jit(solution)/shard_map/ppermute | solution.py:449
  15.0 0.1 collective-permute-start.3
  15.0 0.0 collective-permute-done.5.low_ref.ylow_ref
  15.0 2.7 %collective-permute-done.6.high_ref.yhigh_ref = f32[288,128]{1,0:T(8,128)S(1)} collective-permute-done((f32[288,128]{1,0:T(8,128)S(1)}, f32[288,128]{1,0:T(8,128)S(1)}, u32[]{:S(2)}, u32[]{:S(2)}) %collective-permute-start.6) | collective-permute-done | bytes 147488 | tf_op jit(solution)/shard_map/ppermute | solution.py:449
  17.7 0.1 shard_map.116
  17.8 1.8 %collective-permute-start.10 = (f32[432,128]{1,0:T(8,128)S(1)}, f32[432,128]{1,0:T(8,128)S(1)}, u32[]{:S(2)}, u32[]{:S(2)}) collective-permute-start(f32[432,128]{1,0:T(8,128)S(1)} %get-tuple-element.33), channel_id=1, source_target_pairs={{8,0},{16,8},{24,16},{0,24},{9,1},{17,9},{25,17},{1,25},{10,2},{18... | collective-permute-start | bytes 663560 | tf_op jit(solution)/shard_map/ppermute | solution.py:449
  19.7 1.2 %collective-permute-start.9 = (f32[432,128]{1,0:T(8,128)S(1)}, f32[432,128]{1,0:T(8,128)S(1)}, u32[]{:S(2)}, u32[]{:S(2)}) collective-permute-start(f32[432,128]{1,0:T(8,128)S(1)} %get-tuple-element.29.after_ref), channel_id=1, source_target_pairs={{24,0},{0,8},{8,16},{16,24},{25,1},{1,9},{9,17},{17,25},{26,2},{2,... | collective-permute-start | bytes 663560 | tf_op jit(solution)/shard_map/ppermute | solution.py:449
  20.8 0.0 copy-done.7
  20.8 1.0 %shard_map.117 = (f32[128,128]{1,0:T(8,128)S(1)}, bf16[256,4096]{1,0:T(8,128)(2,1)S(1)}, bf16[64,4096]{1,0:T(8,128)(2,1)S(1)}) custom-call(s32[4,1024]{1,0:T(4,128)S(1)} %copy-done.7, f32[432,128]{1,0:T(8,128)S(1)} %get-tuple-element.29.after_ref), custom_call_target="tpu_custom_call" | custom-call | flops 2300000000 | bytes 4096 | tf_op jit(solution)/shard_map/pallas_call | solution.py:33
  21.8 0.0 collective-permute-done.4.high_ref.yhigh_ref
  21.8 0.0 collective-permute-done.3.low_ref.ylow_ref
  21.9 1.3 %collective-permute-start.8 = (f32[120,128]{1,0:T(8,128)S(1)}, f32[120,128]{1,0:T(8,128)S(1)}, u32[]{:S(2)}, u32[]{:S(2)}) collective-permute-start(f32[120,128]{1,0:T(8,128)S(1)} %get-tuple-element.32), channel_id=1, source_target_pairs={{8,0},{16,8},{24,16},{0,24},{9,1},{17,9},{25,17},{1,25},{10,2},{18... | collective-permute-start | bytes 184328 | tf_op jit(solution)/shard_map/ppermute | solution.py:449
  23.2 1.2 %collective-permute-start.7 = (f32[120,128]{1,0:T(8,128)S(1)}, f32[120,128]{1,0:T(8,128)S(1)}, u32[]{:S(2)}, u32[]{:S(2)}) collective-permute-start(f32[120,128]{1,0:T(8,128)S(1)} %get-tuple-element.31.after_ref), channel_id=1, source_target_pairs={{24,0},{0,8},{8,16},{16,24},{25,1},{1,9},{9,17},{17,25},{26,2},{2,... | collective-permute-start | bytes 184328 | tf_op jit(solution)/shard_map/ppermute | solution.py:449
  24.4 2.4 %shard_map.120.leave_ref = f32[8,32,128]{2,1,0:T(8,128)S(1)} custom-call(s32[1]{0:T(128)} %bitcast.sec_ref, f32[7,128,128]{2,1,0:T(8,128)S(1)} %shard_map.114.after_ref.base_ref, s32[128,128]{1,0:T(8,128)S(1)} %bitcast.10, s32[4,1024]{1,0:T(4,128)S(1)} %copy-done.7, f32[120,128]{1,0:T(8,128)S(1)} %get-tuple-element.31.after_ref), custom_call_target="tpu_custom_call" | custom-call | flops 3449999872 | bytes 4096 | tf_op jit(solution)/shard_map/pallas_call | solution.py:33
  26.8 0.2 collective-permute-done.10.xhigh_ref
  27.0 0.0 collective-permute-done.9.xlow_ref
  27.0 0.2 shard_map.119.flow_ref
  27.2 1.1 %collective-permute-done.8.xhigh_ref = f32[120,128]{1,0:T(8,128)S(1)} collective-permute-done((f32[120,128]{1,0:T(8,128)S(1)}, f32[120,128]{1,0:T(8,128)S(1)}, u32[]{:S(2)}, u32[]{:S(2)}) %collective-permute-start.8) | collective-permute-done | bytes 61472 | tf_op jit(solution)/shard_map/ppermute | solution.py:449
  28.3 0.0 collective-permute-done.7.xlow_ref
  28.3 2.9 %shard_map.121 = (f32[8,8,128]{2,1,0:T(8,128)}, f32[3,8,8,128]{3,2,1,0:T(8,128)}, bf16[512,256]{1,0:T(8,128)(2,1)S(1)}, f32[6,32,128]{2,1,0:T(8,128)S(1)}) custom-call(f32[2,64,128]{2,1,0:T(8,128)S(1)} %get-tuple-element.24.tile_ref, f32[80,128]{1,0:T(8,128)S(1)} %collective-permute-done.3.low_ref.ylow_ref, ...), custom_call_target="tpu_custom_call" | custom-call | flops 6899999744 | bytes 4096 | tf_op jit(solution)/shard_map/pallas_call | solution.py:33
  31.2 2.9 %collective-permute-start.14 = (f32[6,8,128]{2,1,0:T(8,128)S(1)}, f32[6,8,128]{2,1,0:T(8,128)S(1)}, u32[]{:S(2)}, u32[]{:S(2)}) collective-permute-start(f32[6,8,128]{2,1,0:T(8,128)S(1)} %get-tuple-element.42), channel_id=1, source_target_pairs={{2,0},{4,2},{6,4},{0,6},{3,1},{5,3},{7,5},{1,7},{10,8},{12,10},{14... | collective-permute-start | bytes 73736 | tf_op jit(solution)/shard_map/ppermute | solution.py:449
  34.1 0.0 collective-permute-start.13
  34.1 0.7 %collective-permute-start.12 = (f32[6,8,128]{2,1,0:T(8,128)S(1)}, f32[6,8,128]{2,1,0:T(8,128)S(1)}, u32[]{:S(2)}, u32[]{:S(2)}) collective-permute-start(f32[6,8,128]{2,1,0:T(8,128)S(1)} %get-tuple-element.44), channel_id=1, source_target_pairs={{8,0},{16,8},{24,16},{0,24},{9,1},{17,9},{25,17},{1,25},{10,2},{18... | collective-permute-start | bytes 73736 | tf_op jit(solution)/shard_map/ppermute | solution.py:449
  34.8 1.1 %collective-permute-start.11 = (f32[6,8,128]{2,1,0:T(8,128)S(1)}, f32[6,8,128]{2,1,0:T(8,128)S(1)}, u32[]{:S(2)}, u32[]{:S(2)}) collective-permute-start(f32[6,8,128]{2,1,0:T(8,128)S(1)} %get-tuple-element.45), channel_id=1, source_target_pairs={{24,0},{0,8},{8,16},{16,24},{25,1},{1,9},{9,17},{17,25},{26,2},{2,... | collective-permute-start | bytes 73736 | tf_op jit(solution)/shard_map/ppermute | solution.py:449
  35.8 4.8 %shard_map.122.moved_ref = f32[6,128,128]{2,1,0:T(8,128)S(1)} custom-call(s32[1]{0:T(128)} %bitcast.sec_ref, bf16[512,256]{1,0:T(8,128)(2,1)S(1)} %get-tuple-element.38.table_ref, s32[128,128]{1,0:T(8,128)S(1)} %bitcast.11, f32[7,128,128]{2,1,0:T(8,128)S(1)} %shard_map.114.after_ref.base_ref), custom_call_target="tpu_custom_call" | custom-call | flops 6899999744 | bytes 4096 | tf_op jit(solution)/shard_map/pallas_call | solution.py:33
  40.7 0.0 collective-permute-done.14.d_ref
  40.7 0.0 collective-permute-done.13.c_ref
  40.7 0.0 collective-permute-done.12.b_ref
  40.7 0.0 collective-permute-done.11.a_ref
  40.7 3.2 %shard_map.123 = (f32[3,16384]{1,0:T(4,128)}, f32[3,16384]{1,0:T(4,128)}) custom-call(bf16[256,4096]{1,0:T(8,128)(2,1)S(1)} %get-tuple-element.36.left_ref, bf16[64,4096]{1,0:T(8,128)(2,1)S(1)} %get-tuple-element.37.low_ref, f32[128,128]{1,0:T(8,128)S(1)} %get-tuple-element.30.after_ref.mask_ref, f32[6,128,128]{2,1,0:T(8,128)S(1)} %shard_map.122.moved_ref, ...), custom_call_target="tpu_custom_call" | custom-call | flops 4600000000 | bytes 4096 | tf_op jit(solution)/shard_map/pallas_call | solution.py:33
  (4 shorter events, 0.1 us)
Async XLA Ops:
  0.6 7.6 %collective-permute-start.1 = (f32[64,128]{1,0:T(8,128)}, f32[64,128]{1,0:T(8,128)S(1)}, u32[]{:S(2)}, u32[]{:S(2)}) collective-permute-start(f32[64,128]{1,0:T(8,128)} %bitcast.12), channel_id=1, source_target_pairs={{1,0},{0,1},{3,2},{2,3},{5,4},{4,5},{7,6},{6,7},{9,8},{8,9},{11,10... | collective-permute-start | bytes 98312 | tf_op jit(solution)/shard_map/ppermute | solution.py:449
  2.8 5.5 %collective-permute-start.2 = (f32[192,128]{1,0:T(8,128)}, f32[192,128]{1,0:T(8,128)S(1)}, u32[]{:S(2)}, u32[]{:S(2)}) collective-permute-start(f32[192,128]{1,0:T(8,128)} %bitcast.5), channel_id=1, source_target_pairs={{1,0},{0,1},{3,2},{2,3},{5,4},{4,5},{7,6},{6,7},{9,8},{8,9},{11,10... | collective-permute-start | bytes 294920 | tf_op jit(solution)/shard_map/ppermute | solution.py:449
  2.8 0.8 %copy-start.4 = (f32[16384]{0:T(1024)S(1)}, f32[16384]{0:T(1024)}, u32[]{:S(2)}) copy-start(f32[16384]{0:T(1024)} %param.12) | copy-start | bytes 196612
  2.8 0.9 %copy-start.5 = (s32[16384]{0:T(1024)S(1)}, s32[16384]{0:T(1024)}, u32[]{:S(2)}) copy-start(s32[16384]{0:T(1024)} %param.13) | copy-start | bytes 196612
  3.7 4.5 %copy-start.3 = (f32[3,8,8,128]{3,2,1,0:T(8,128)S(1)}, f32[3,8,8,128]{3,2,1,0:T(8,128)}, u32[]{:S(2)}) copy-start(f32[3,8,8,128]{3,2,1,0:T(8,128)} %param.9) | copy-start | bytes 294916
  3.7 4.5 %copy-start.6 = (f32[8,8,128]{2,1,0:T(8,128)S(1)}, f32[8,8,128]{2,1,0:T(8,128)}, u32[]{:S(2)}) copy-start(f32[8,8,128]{2,1,0:T(8,128)} %param.8) | copy-start | bytes 98308
  3.7 8.0 %copy-start = (s32[8,16384]{1,0:T(8,128)S(1)}, s32[8,16384]{1,0:T(8,128)}, u32[]{:S(2)}) copy-start(s32[8,16384]{1,0:T(8,128)} %pair_ref.1) | copy-start | bytes 1572868
  3.7 8.0 %copy-start.1 = (f32[3,16384]{1,0:T(4,128)S(1)}, f32[3,16384]{1,0:T(4,128)}, u32[]{:S(2)}) copy-start(f32[3,16384]{1,0:T(4,128)} %pos_ref.1) | copy-start | bytes 589828
  3.7 8.0 %copy-start.2 = (f32[3,16384]{1,0:T(4,128)S(1)}, f32[3,16384]{1,0:T(4,128)}, u32[]{:S(2)}) copy-start(f32[3,16384]{1,0:T(4,128)} %vel_ref.1) | copy-start | bytes 589828
  6.8 6.7 %collective-permute-start = (f32[128,128]{1,0:T(8,128)S(1)}, f32[128,128]{1,0:T(8,128)S(1)}, u32[]{:S(2)}, u32[]{:S(2)}) collective-permute-start(f32[128,128]{1,0:T(8,128)S(1)} %shard_map.112.mine_ref), channel_id=1, source_target_pairs={{1,0},{0,1},{3,2},{2,3},{5,4},{4,5},{7,6},{6,7},{9,8},{8,9},{11,10... | collective-permute-start | bytes 196616 | tf_op jit(solution)/shard_map/ppermute | solution.py:449
  8.3 6.7 %collective-permute-start.5 = (f32[288,128]{1,0:T(8,128)S(1)}, f32[288,128]{1,0:T(8,128)S(1)}, u32[]{:S(2)}, u32[]{:S(2)}) collective-permute-start(f32[288,128]{1,0:T(8,128)S(1)} %get-tuple-element.27), channel_id=1, source_target_pairs={{6,0},{0,2},{2,4},{4,6},{7,1},{1,3},{3,5},{5,7},{14,8},{8,10},{10,... | collective-permute-start | bytes 442376 | tf_op jit(solution)/shard_map/ppermute | solution.py:449
  9.7 8.1 %collective-permute-start.6 = (f32[288,128]{1,0:T(8,128)S(1)}, f32[288,128]{1,0:T(8,128)S(1)}, u32[]{:S(2)}, u32[]{:S(2)}) collective-permute-start(f32[288,128]{1,0:T(8,128)S(1)} %get-tuple-element.28), channel_id=1, source_target_pairs={{2,0},{4,2},{6,4},{0,6},{3,1},{5,3},{7,5},{1,7},{10,8},{12,10},{14... | collective-permute-start | bytes 442376 | tf_op jit(solution)/shard_map/ppermute | solution.py:449
  11.8 9.0 %copy-start.7 = (s32[4,1024]{1,0:T(4,128)S(1)}, s32[4,1024]{1,0:T(4,128)}, u32[]{:S(2)}) copy-start(s32[4,1024]{1,0:T(4,128)} %dep_ref.3) | copy-start | bytes 49156
  13.5 8.3 %collective-permute-start.4 = (f32[80,128]{1,0:T(8,128)S(1)}, f32[80,128]{1,0:T(8,128)S(1)}, u32[]{:S(2)}, u32[]{:S(2)}) collective-permute-start(f32[80,128]{1,0:T(8,128)S(1)} %get-tuple-element.26), channel_id=1, source_target_pairs={{2,0},{4,2},{6,4},{0,6},{3,1},{5,3},{7,5},{1,7},{10,8},{12,10},{14... | collective-permute-start | bytes 122888 | tf_op jit(solution)/shard_map/ppermute | solution.py:449
  15.0 6.9 %collective-permute-start.3 = (f32[80,128]{1,0:T(8,128)S(1)}, f32[80,128]{1,0:T(8,128)S(1)}, u32[]{:S(2)}, u32[]{:S(2)}) collective-permute-start(f32[80,128]{1,0:T(8,128)S(1)} %get-tuple-element.25.after_ref), channel_id=1, source_target_pairs={{6,0},{0,2},{2,4},{4,6},{7,1},{1,3},{3,5},{5,7},{14,8},{8,10},{10,... | collective-permute-start | bytes 122888 | tf_op jit(solution)/shard_map/ppermute | solution.py:449
  17.8 9.2 %collective-permute-start.10 = (f32[432,128]{1,0:T(8,128)S(1)}, f32[432,128]{1,0:T(8,128)S(1)}, u32[]{:S(2)}, u32[]{:S(2)}) collective-permute-start(f32[432,128]{1,0:T(8,128)S(1)} %get-tuple-element.33), channel_id=1, source_target_pairs={{8,0},{16,8},{24,16},{0,24},{9,1},{17,9},{25,17},{1,25},{10,2},{18... | collective-permute-start | bytes 663560 | tf_op jit(solution)/shard_map/ppermute | solution.py:449
  19.7 7.4 %collective-permute-start.9 = (f32[432,128]{1,0:T(8,128)S(1)}, f32[432,128]{1,0:T(8,128)S(1)}, u32[]{:S(2)}, u32[]{:S(2)}) collective-permute-start(f32[432,128]{1,0:T(8,128)S(1)} %get-tuple-element.29.after_ref), channel_id=1, source_target_pairs={{24,0},{0,8},{8,16},{16,24},{25,1},{1,9},{9,17},{17,25},{26,2},{2,... | collective-permute-start | bytes 663560 | tf_op jit(solution)/shard_map/ppermute | solution.py:449
  21.9 6.5 %collective-permute-start.8 = (f32[120,128]{1,0:T(8,128)S(1)}, f32[120,128]{1,0:T(8,128)S(1)}, u32[]{:S(2)}, u32[]{:S(2)}) collective-permute-start(f32[120,128]{1,0:T(8,128)S(1)} %get-tuple-element.32), channel_id=1, source_target_pairs={{8,0},{16,8},{24,16},{0,24},{9,1},{17,9},{25,17},{1,25},{10,2},{18... | collective-permute-start | bytes 184328 | tf_op jit(solution)/shard_map/ppermute | solution.py:449
  23.2 5.1 %collective-permute-start.7 = (f32[120,128]{1,0:T(8,128)S(1)}, f32[120,128]{1,0:T(8,128)S(1)}, u32[]{:S(2)}, u32[]{:S(2)}) collective-permute-start(f32[120,128]{1,0:T(8,128)S(1)} %get-tuple-element.31.after_ref), channel_id=1, source_target_pairs={{24,0},{0,8},{8,16},{16,24},{25,1},{1,9},{9,17},{17,25},{26,2},{2,... | collective-permute-start | bytes 184328 | tf_op jit(solution)/shard_map/ppermute | solution.py:449
  31.2 9.4 %collective-permute-start.14 = (f32[6,8,128]{2,1,0:T(8,128)S(1)}, f32[6,8,128]{2,1,0:T(8,128)S(1)}, u32[]{:S(2)}, u32[]{:S(2)}) collective-permute-start(f32[6,8,128]{2,1,0:T(8,128)S(1)} %get-tuple-element.42), channel_id=1, source_target_pairs={{2,0},{4,2},{6,4},{0,6},{3,1},{5,3},{7,5},{1,7},{10,8},{12,10},{14... | collective-permute-start | bytes 73736 | tf_op jit(solution)/shard_map/ppermute | solution.py:449
  34.1 6.6 %collective-permute-start.13 = (f32[6,8,128]{2,1,0:T(8,128)S(1)}, f32[6,8,128]{2,1,0:T(8,128)S(1)}, u32[]{:S(2)}, u32[]{:S(2)}) collective-permute-start(f32[6,8,128]{2,1,0:T(8,128)S(1)} %get-tuple-element.43), channel_id=1, source_target_pairs={{6,0},{0,2},{2,4},{4,6},{7,1},{1,3},{3,5},{5,7},{14,8},{8,10},{10,... | collective-permute-start | bytes 73736 | tf_op jit(solution)/shard_map/ppermute | solution.py:449
  34.1 6.6 %collective-permute-start.12 = (f32[6,8,128]{2,1,0:T(8,128)S(1)}, f32[6,8,128]{2,1,0:T(8,128)S(1)}, u32[]{:S(2)}, u32[]{:S(2)}) collective-permute-start(f32[6,8,128]{2,1,0:T(8,128)S(1)} %get-tuple-element.44), channel_id=1, source_target_pairs={{8,0},{16,8},{24,16},{0,24},{9,1},{17,9},{25,17},{1,25},{10,2},{18... | collective-permute-start | bytes 73736 | tf_op jit(solution)/shard_map/ppermute | solution.py:449
  34.8 5.9 %collective-permute-start.11 = (f32[6,8,128]{2,1,0:T(8,128)S(1)}, f32[6,8,128]{2,1,0:T(8,128)S(1)}, u32[]{:S(2)}, u32[]{:S(2)}) collective-permute-start(f32[6,8,128]{2,1,0:T(8,128)S(1)} %get-tuple-element.45), channel_id=1, source_target_pairs={{24,0},{0,8},{8,16},{16,24},{25,1},{1,9},{9,17},{17,25},{26,2},{2,... | collective-permute-start | bytes 73736 | tf_op jit(solution)/shard_map/ppermute | solution.py:449

commit v5 on v4

--- a/solution.py
+++ b/solution.py
@@ -237,12 +237,15 @@
             down_ref[at : at + 8, :] = tile_ref[g, pl.ds(j, 8, stride=8), :]
 
 
-def early_kernel(p_ref, v_ref, far_p_ref, far_v_ref, tile_ref, up_ref, down_ref):
-    tile_ref[0] = p_ref[...]
-    tile_ref[1] = far_p_ref[...]
-    for d in range(3):
-        tile_ref[2 + 2 * d] = v_ref[64 * d : 64 * d + 64, :]
-        tile_ref[3 + 2 * d] = far_v_ref[64 * d : 64 * d + 64, :]
+def pack_kernel(p_ref, v_ref, after_ref, out_ref):
+    out_ref[0:64, :] = p_ref[...]
+    out_ref[64:256, :] = v_ref[...]
+
+
+def early_kernel(near_ref, far_ref, tile_ref, up_ref, down_ref):
+    for f in range(4):
+        tile_ref[2 * f] = near_ref[64 * f : 64 * f + 64, :]
+        tile_ref[2 * f + 1] = far_ref[64 * f : 64 * f + 64, :]
     slices_y(STATE, tile_ref, up_ref, down_ref)
 
 
@@ -462,11 +465,11 @@
     size = 8 + 2 * HALO
     leavers = 4 * movers // LANES
 
-    far_p = shifted(near_p, "sec", 1)
-    far_v = shifted(near_v, "sec", 1)
     (ahead,) = call(ahead_kernel, [((8, LANES), F32)], busy_us=3)
+    (near,) = call(pack_kernel, [((256, LANES), F32)], near_p, near_v, ahead, loose=(2,), busy_us=3)
+    far = shifted(near, "sec", 1)
     (mine,) = call(
-        deposit_kernel, [((LANES, LANES), F32)], sec, vol2, cell2, ahead,
+        deposit_kernel, [((LANES, LANES), F32)], sec, vol2, cell2, near,
         scratch=[dense] * 4, smem=(0,), loose=(3,), busy_us=4,
     )
     got = shifted(mine, "sec", 1)
@@ -474,7 +477,7 @@
     void_y, void_x = y_starts(VOID)[1], x_starts(VOID)[1]
     state, state_up, state_down = call(
         early_kernel, [((8, 64, LANES), F32), ((state_y, LANES), F32), ((state_y, LANES), F32)],
-        near_p, near_v, far_p, far_v,
+        near, far,
     )
     state_ylow = shifted(state_up, "gy", 1)
     state_yhigh = shifted(state_down, "gy", -1)

time: 44.1 us -> 43.5 us (0.986)
  starting transfers between devices: 18.7 us -> 17.4 us
  waiting for transfers between devices: 4.04 us -> 4.82 us
    ppermute x15 -> x14, starting transfers between devices: 18.7 us -> 17.4 us  [shifted(): lax.ppermute(block, axis, [((i - distance) % count, i) for i in range(cou...]
    ppermute x15 -> x14, waiting for transfers between devices: 4.04 us -> 4.82 us  [shifted(): lax.ppermute(block, axis, [((i - distance) % count, i) for i in range(cou...]
    pallas_call x13 -> x14, Pallas kernels: 19.4 us -> 19.4 us  [call(): pl.pallas_call(kernel, out_shape=outs_list, in_specs=specs, out_specs=[vm...]
  transfers between devices with their start and end apart: 15 -> 14, of which waited for: 3 -> 3; matrix products, arithmetic and copies ran while one was open for 0% -> 0% of each run, Pallas kernels for 30% -> 31%
where the time goes in v5:
time: 43.5 us; the launch traced here: 43.3 us
  Pallas kernels  19.4 us (45%)
  starting transfers between devices  17.4 us (40%)
  waiting for transfers between devices  4.82 us (11%)
  local copies, waits for them, and re-layouts  0.9 us (2%)
  between operations  0.82 us (2%)
    pallas_call x14, Pallas kernels, call(): pl.pallas_call(kernel, out_shape=outs_list, in_specs=specs, out_specs=[vm...  19.4 us
    ppermute x14, starting transfers between devices, shifted(): lax.ppermute(block, axis, [((i - distance) % count, i) for i in range(cou...  17.4 us
    ppermute x14, waiting for transfers between devices, shifted(): lax.ppermute(block, axis, [((i - distance) % count, i) for i in range(cou...  4.82 us
    unnamed x16, local copies, waits for them, and re-layouts  0.89 us
  transfers between devices with their start and end apart: 14, of which 3 were waited for; matrix products, arithmetic and copies ran while one was open for 0% of the time, Pallas kernels for 31%

profile of v5, /device:TPU:1, one launch (start us, length us, event | category | flops | bytes accessed | tf_op | source)
XLA Modules:
  0.0 43.3 jit_solution(338316508848958542)
XLA Ops:
  0.6 0.0 copy-start.3
  0.6 0.0 copy-start.6
  0.7 0.9 %copy-done.3 = f32[3,8,8,128]{3,2,1,0:T(8,128)S(1)} copy-done((f32[3,8,8,128]{3,2,1,0:T(8,128)S(1)}, f32[3,8,8,128]{3,2,1,0:T(8,128)}, u32[]{:S(2)}) %copy-start.3) | copy-done | bytes 98328
  1.5 0.0 copy-done.6
  1.5 0.0 copy-start.4
  1.5 0.0 copy-start.5
  1.5 2.1 %collective-permute-start.1 = (f32[256,128]{1,0:T(8,128)S(1)}, f32[256,128]{1,0:T(8,128)S(1)}, u32[]{:S(2)}, u32[]{:S(2)}) collective-permute-start(f32[256,128]{1,0:T(8,128)S(1)} %shard_map.112.after_ref.near_ref), channel_id=1, source_target_pairs={{1,0},{0,1},{3,2},{2,3},{5,4},{4,5},{7,6},{6,7},{9,8},{8,9},{11,10... | collective-permute-start | bytes 393224 | tf_op jit(solution)/shard_map/ppermute | solution.py:452
  3.7 0.0 copy-done.4
  3.7 0.0 copy-done.5
  3.7 0.0 copy-start
  3.7 0.0 copy-start.1
  3.7 0.0 copy-start.2
  3.7 3.0 %shard_map.113.mine_ref = f32[128,128]{1,0:T(8,128)S(1)} custom-call(s32[1]{0:T(128)} %bitcast.sec_ref, f32[128,128]{1,0:T(8,128)S(1)} %bitcast.6, s32[128,128]{1,0:T(8,128)S(1)} %bitcast.8, f32[256,128]{1,0:T(8,128)S(1)} %shard_map.112.after_ref.near_ref), custom_call_target="tpu_custom_call" | custom-call | flops 4600000000 | bytes 4096 | tf_op jit(solution)/shard_map/pallas_call | solution.py:33
  6.7 0.8 %collective-permute-start = (f32[128,128]{1,0:T(8,128)S(1)}, f32[128,128]{1,0:T(8,128)S(1)}, u32[]{:S(2)}, u32[]{:S(2)}) collective-permute-start(f32[128,128]{1,0:T(8,128)S(1)} %shard_map.113.mine_ref), channel_id=1, source_target_pairs={{1,0},{0,1},{3,2},{2,3},{5,4},{4,5},{7,6},{6,7},{9,8},{8,9},{11,10... | collective-permute-start | bytes 196616 | tf_op jit(solution)/shard_map/ppermute | solution.py:452
  7.6 0.0 collective-permute-done.1.far_ref
  7.6 0.1 shard_map.114
  7.6 1.4 %collective-permute-start.4 = (f32[288,128]{1,0:T(8,128)S(1)}, f32[288,128]{1,0:T(8,128)S(1)}, u32[]{:S(2)}, u32[]{:S(2)}) collective-permute-start(f32[288,128]{1,0:T(8,128)S(1)} %get-tuple-element.27), channel_id=1, source_target_pairs={{6,0},{0,2},{2,4},{4,6},{7,1},{1,3},{3,5},{5,7},{14,8},{8,10},{10,... | collective-permute-start | bytes 442376 | tf_op jit(solution)/shard_map/ppermute | solution.py:452
  9.0 2.1 %collective-permute-start.5 = (f32[288,128]{1,0:T(8,128)S(1)}, f32[288,128]{1,0:T(8,128)S(1)}, u32[]{:S(2)}, u32[]{:S(2)}) collective-permute-start(f32[288,128]{1,0:T(8,128)S(1)} %get-tuple-element.28), channel_id=1, source_target_pairs={{2,0},{4,2},{6,4},{0,6},{3,1},{5,3},{7,5},{1,7},{10,8},{12,10},{14... | collective-permute-start | bytes 442376 | tf_op jit(solution)/shard_map/ppermute | solution.py:452
  11.1 0.0 copy-done
  11.1 0.0 copy-done.1
  11.1 0.0 copy-done.2
  11.1 0.0 copy-start.7
  11.1 1.7 %shard_map.115.after_ref.base_ref = f32[7,128,128]{2,1,0:T(8,128)S(1)} custom-call(f32[128,128]{1,0:T(8,128)S(1)} %bitcast.7, f32[3,16384]{1,0:T(4,128)S(1)} %copy-done.1, f32[3,16384]{1,0:T(4,128)S(1)} %copy-done.2, s32[8,16384]{1,0:T(8,128)S(1)} %copy-done, f32[8,64,128]{2,1,0:T(8,128)S(1)} %get-tuple-element.23.after_ref.tile_ref), custom_call_target="tpu_custom_call" | custom-call | flops 4600000000 | bytes 4096 | tf_op jit(solution)/shard_map/pallas_call | solution.py:33
  12.8 0.0 collective-permute-done.got_ref
  12.8 1.5 %collective-permute-start.3 = (f32[80,128]{1,0:T(8,128)S(1)}, f32[80,128]{1,0:T(8,128)S(1)}, u32[]{:S(2)}, u32[]{:S(2)}) collective-permute-start(f32[80,128]{1,0:T(8,128)S(1)} %get-tuple-element.26), channel_id=1, source_target_pairs={{2,0},{4,2},{6,4},{0,6},{3,1},{5,3},{7,5},{1,7},{10,8},{12,10},{14... | collective-permute-start | bytes 122888 | tf_op jit(solution)/shard_map/ppermute | solution.py:452
  14.3 0.1 collective-permute-start.2
  14.3 0.0 collective-permute-done.4.low_ref.ylow_ref
  14.4 2.9 %collective-permute-done.5.high_ref.yhigh_ref = f32[288,128]{1,0:T(8,128)S(1)} collective-permute-done((f32[288,128]{1,0:T(8,128)S(1)}, f32[288,128]{1,0:T(8,128)S(1)}, u32[]{:S(2)}, u32[]{:S(2)}) %collective-permute-start.5) | collective-permute-done | bytes 147488 | tf_op jit(solution)/shard_map/ppermute | solution.py:452
  17.3 0.1 shard_map.117
  17.3 1.6 %collective-permute-start.9 = (f32[432,128]{1,0:T(8,128)S(1)}, f32[432,128]{1,0:T(8,128)S(1)}, u32[]{:S(2)}, u32[]{:S(2)}) collective-permute-start(f32[432,128]{1,0:T(8,128)S(1)} %get-tuple-element.33), channel_id=1, source_target_pairs={{8,0},{16,8},{24,16},{0,24},{9,1},{17,9},{25,17},{1,25},{10,2},{18... | collective-permute-start | bytes 663560 | tf_op jit(solution)/shard_map/ppermute | solution.py:452
  19.0 1.2 %collective-permute-start.8 = (f32[432,128]{1,0:T(8,128)S(1)}, f32[432,128]{1,0:T(8,128)S(1)}, u32[]{:S(2)}, u32[]{:S(2)}) collective-permute-start(f32[432,128]{1,0:T(8,128)S(1)} %get-tuple-element.29.after_ref), channel_id=1, source_target_pairs={{24,0},{0,8},{8,16},{16,24},{25,1},{1,9},{9,17},{17,25},{26,2},{2,... | collective-permute-start | bytes 663560 | tf_op jit(solution)/shard_map/ppermute | solution.py:452
  20.1 0.0 copy-done.7
  20.1 1.0 %shard_map.118 = (f32[128,128]{1,0:T(8,128)S(1)}, bf16[256,4096]{1,0:T(8,128)(2,1)S(1)}, bf16[64,4096]{1,0:T(8,128)(2,1)S(1)}) custom-call(s32[4,1024]{1,0:T(4,128)S(1)} %copy-done.7, f32[432,128]{1,0:T(8,128)S(1)} %get-tuple-element.29.after_ref), custom_call_target="tpu_custom_call" | custom-call | flops 2300000000 | bytes 4096 | tf_op jit(solution)/shard_map/pallas_call | solution.py:33
  21.1 0.0 collective-permute-done.3.high_ref.yhigh_ref
  21.1 0.0 collective-permute-done.2.low_ref.ylow_ref
  21.2 0.8 %collective-permute-start.7 = (f32[120,128]{1,0:T(8,128)S(1)}, f32[120,128]{1,0:T(8,128)S(1)}, u32[]{:S(2)}, u32[]{:S(2)}) collective-permute-start(f32[120,128]{1,0:T(8,128)S(1)} %get-tuple-element.32), channel_id=1, source_target_pairs={{8,0},{16,8},{24,16},{0,24},{9,1},{17,9},{25,17},{1,25},{10,2},{18... | collective-permute-start | bytes 184328 | tf_op jit(solution)/shard_map/ppermute | solution.py:452
  22.0 1.2 %collective-permute-start.6 = (f32[120,128]{1,0:T(8,128)S(1)}, f32[120,128]{1,0:T(8,128)S(1)}, u32[]{:S(2)}, u32[]{:S(2)}) collective-permute-start(f32[120,128]{1,0:T(8,128)S(1)} %get-tuple-element.31.after_ref), channel_id=1, source_target_pairs={{24,0},{0,8},{8,16},{16,24},{25,1},{1,9},{9,17},{17,25},{26,2},{2,... | collective-permute-start | bytes 184328 | tf_op jit(solution)/shard_map/ppermute | solution.py:452
  23.1 2.4 %shard_map.121.leave_ref = f32[8,32,128]{2,1,0:T(8,128)S(1)} custom-call(s32[1]{0:T(128)} %bitcast.sec_ref, f32[7,128,128]{2,1,0:T(8,128)S(1)} %shard_map.115.after_ref.base_ref, s32[128,128]{1,0:T(8,128)S(1)} %bitcast.9, s32[4,1024]{1,0:T(4,128)S(1)} %copy-done.7, f32[120,128]{1,0:T(8,128)S(1)} %get-tuple-element.31.after_ref), custom_call_target="tpu_custom_call" | custom-call | flops 3449999872 | bytes 4096 | tf_op jit(solution)/shard_map/pallas_call | solution.py:33
  25.6 0.8 %collective-permute-done.9.xhigh_ref = f32[432,128]{1,0:T(8,128)S(1)} collective-permute-done((f32[432,128]{1,0:T(8,128)S(1)}, f32[432,128]{1,0:T(8,128)S(1)}, u32[]{:S(2)}, u32[]{:S(2)}) %collective-permute-start.9) | collective-permute-done | bytes 221216 | tf_op jit(solution)/shard_map/ppermute | solution.py:452
  26.3 0.0 collective-permute-done.8.xlow_ref
  26.3 0.2 shard_map.120.flow_ref
  26.5 1.1 %collective-permute-done.7.xhigh_ref = f32[120,128]{1,0:T(8,128)S(1)} collective-permute-done((f32[120,128]{1,0:T(8,128)S(1)}, f32[120,128]{1,0:T(8,128)S(1)}, u32[]{:S(2)}, u32[]{:S(2)}) %collective-permute-start.7) | collective-permute-done | bytes 61472 | tf_op jit(solution)/shard_map/ppermute | solution.py:452
  27.6 0.0 collective-permute-done.6.xlow_ref
  27.6 2.9 %shard_map.122 = (f32[8,8,128]{2,1,0:T(8,128)}, f32[3,8,8,128]{3,2,1,0:T(8,128)}, bf16[512,256]{1,0:T(8,128)(2,1)S(1)}, f32[6,32,128]{2,1,0:T(8,128)S(1)}) custom-call(f32[2,64,128]{2,1,0:T(8,128)S(1)} %get-tuple-element.24.tile_ref, f32[80,128]{1,0:T(8,128)S(1)} %collective-permute-done.2.low_ref.ylow_ref, ...), custom_call_target="tpu_custom_call" | custom-call | flops 6899999744 | bytes 4096 | tf_op jit(solution)/shard_map/pallas_call | solution.py:33
  30.5 3.0 %collective-permute-start.13 = (f32[6,8,128]{2,1,0:T(8,128)S(1)}, f32[6,8,128]{2,1,0:T(8,128)S(1)}, u32[]{:S(2)}, u32[]{:S(2)}) collective-permute-start(f32[6,8,128]{2,1,0:T(8,128)S(1)} %get-tuple-element.42), channel_id=1, source_target_pairs={{2,0},{4,2},{6,4},{0,6},{3,1},{5,3},{7,5},{1,7},{10,8},{12,10},{14... | collective-permute-start | bytes 73736 | tf_op jit(solution)/shard_map/ppermute | solution.py:452
  33.5 0.0 collective-permute-start.12
  33.5 0.7 %collective-permute-start.11 = (f32[6,8,128]{2,1,0:T(8,128)S(1)}, f32[6,8,128]{2,1,0:T(8,128)S(1)}, u32[]{:S(2)}, u32[]{:S(2)}) collective-permute-start(f32[6,8,128]{2,1,0:T(8,128)S(1)} %get-tuple-element.44), channel_id=1, source_target_pairs={{8,0},{16,8},{24,16},{0,24},{9,1},{17,9},{25,17},{1,25},{10,2},{18... | collective-permute-start | bytes 73736 | tf_op jit(solution)/shard_map/ppermute | solution.py:452
  34.2 1.0 %collective-permute-start.10 = (f32[6,8,128]{2,1,0:T(8,128)S(1)}, f32[6,8,128]{2,1,0:T(8,128)S(1)}, u32[]{:S(2)}, u32[]{:S(2)}) collective-permute-start(f32[6,8,128]{2,1,0:T(8,128)S(1)} %get-tuple-element.45), channel_id=1, source_target_pairs={{24,0},{0,8},{8,16},{16,24},{25,1},{1,9},{9,17},{17,25},{26,2},{2,... | collective-permute-start | bytes 73736 | tf_op jit(solution)/shard_map/ppermute | solution.py:452
  35.2 4.8 %shard_map.123.moved_ref = f32[6,128,128]{2,1,0:T(8,128)S(1)} custom-call(s32[1]{0:T(128)} %bitcast.sec_ref, bf16[512,256]{1,0:T(8,128)(2,1)S(1)} %get-tuple-element.38.table_ref, s32[128,128]{1,0:T(8,128)S(1)} %bitcast.10, f32[7,128,128]{2,1,0:T(8,128)S(1)} %shard_map.115.after_ref.base_ref), custom_call_target="tpu_custom_call" | custom-call | flops 6899999744 | bytes 4096 | tf_op jit(solution)/shard_map/pallas_call | solution.py:33
  40.1 0.0 collective-permute-done.13.d_ref
  40.1 0.0 collective-permute-done.12.c_ref
  40.1 0.0 collective-permute-done.11.b_ref
  40.1 0.0 collective-permute-done.10.a_ref
  40.1 3.2 %shard_map.124 = (f32[3,16384]{1,0:T(4,128)}, f32[3,16384]{1,0:T(4,128)}) custom-call(bf16[256,4096]{1,0:T(8,128)(2,1)S(1)} %get-tuple-element.36.left_ref, bf16[64,4096]{1,0:T(8,128)(2,1)S(1)} %get-tuple-element.37.low_ref, f32[128,128]{1,0:T(8,128)S(1)} %get-tuple-element.30.after_ref.mask_ref, f32[6,128,128]{2,1,0:T(8,128)S(1)} %shard_map.123.moved_ref, ...), custom_call_target="tpu_custom_call" | custom-call | flops 4600000000 | bytes 4096 | tf_op jit(solution)/shard_map/pallas_call | solution.py:33
  (5 shorter events, 0.1 us)
Async XLA Ops:
  0.6 0.9 %copy-start.3 = (f32[3,8,8,128]{3,2,1,0:T(8,128)S(1)}, f32[3,8,8,128]{3,2,1,0:T(8,128)}, u32[]{:S(2)}) copy-start(f32[3,8,8,128]{3,2,1,0:T(8,128)} %param.9) | copy-start | bytes 294916
  0.6 0.9 %copy-start.6 = (f32[8,8,128]{2,1,0:T(8,128)S(1)}, f32[8,8,128]{2,1,0:T(8,128)}, u32[]{:S(2)}) copy-start(f32[8,8,128]{2,1,0:T(8,128)} %param.8) | copy-start | bytes 98308
  1.5 2.2 %copy-start.4 = (f32[16384]{0:T(1024)S(1)}, f32[16384]{0:T(1024)}, u32[]{:S(2)}) copy-start(f32[16384]{0:T(1024)} %param.12) | copy-start | bytes 196612
  1.5 2.2 %copy-start.5 = (s32[16384]{0:T(1024)S(1)}, s32[16384]{0:T(1024)}, u32[]{:S(2)}) copy-start(s32[16384]{0:T(1024)} %param.13) | copy-start | bytes 196612
  1.5 6.0 %collective-permute-start.1 = (f32[256,128]{1,0:T(8,128)S(1)}, f32[256,128]{1,0:T(8,128)S(1)}, u32[]{:S(2)}, u32[]{:S(2)}) collective-permute-start(f32[256,128]{1,0:T(8,128)S(1)} %shard_map.112.after_ref.near_ref), channel_id=1, source_target_pairs={{1,0},{0,1},{3,2},{2,3},{5,4},{4,5},{7,6},{6,7},{9,8},{8,9},{11,10... | collective-permute-start | bytes 393224 | tf_op jit(solution)/shard_map/ppermute | solution.py:452
  3.7 7.4 %copy-start = (s32[8,16384]{1,0:T(8,128)S(1)}, s32[8,16384]{1,0:T(8,128)}, u32[]{:S(2)}) copy-start(s32[8,16384]{1,0:T(8,128)} %pair_ref.1) | copy-start | bytes 1572868
  3.7 7.4 %copy-start.1 = (f32[3,16384]{1,0:T(4,128)S(1)}, f32[3,16384]{1,0:T(4,128)}, u32[]{:S(2)}) copy-start(f32[3,16384]{1,0:T(4,128)} %pos_ref.1) | copy-start | bytes 589828
  3.7 7.4 %copy-start.2 = (f32[3,16384]{1,0:T(4,128)S(1)}, f32[3,16384]{1,0:T(4,128)}, u32[]{:S(2)}) copy-start(f32[3,16384]{1,0:T(4,128)} %vel_ref.1) | copy-start | bytes 589828
  6.7 6.1 %collective-permute-start = (f32[128,128]{1,0:T(8,128)S(1)}, f32[128,128]{1,0:T(8,128)S(1)}, u32[]{:S(2)}, u32[]{:S(2)}) collective-permute-start(f32[128,128]{1,0:T(8,128)S(1)} %shard_map.113.mine_ref), channel_id=1, source_target_pairs={{1,0},{0,1},{3,2},{2,3},{5,4},{4,5},{7,6},{6,7},{9,8},{8,9},{11,10... | collective-permute-start | bytes 196616 | tf_op jit(solution)/shard_map/ppermute | solution.py:452
  7.6 6.7 %collective-permute-start.4 = (f32[288,128]{1,0:T(8,128)S(1)}, f32[288,128]{1,0:T(8,128)S(1)}, u32[]{:S(2)}, u32[]{:S(2)}) collective-permute-start(f32[288,128]{1,0:T(8,128)S(1)} %get-tuple-element.27), channel_id=1, source_target_pairs={{6,0},{0,2},{2,4},{4,6},{7,1},{1,3},{3,5},{5,7},{14,8},{8,10},{10,... | collective-permute-start | bytes 442376 | tf_op jit(solution)/shard_map/ppermute | solution.py:452
  9.0 8.3 %collective-permute-start.5 = (f32[288,128]{1,0:T(8,128)S(1)}, f32[288,128]{1,0:T(8,128)S(1)}, u32[]{:S(2)}, u32[]{:S(2)}) collective-permute-start(f32[288,128]{1,0:T(8,128)S(1)} %get-tuple-element.28), channel_id=1, source_target_pairs={{2,0},{4,2},{6,4},{0,6},{3,1},{5,3},{7,5},{1,7},{10,8},{12,10},{14... | collective-permute-start | bytes 442376 | tf_op jit(solution)/shard_map/ppermute | solution.py:452
  11.1 9.0 %copy-start.7 = (s32[4,1024]{1,0:T(4,128)S(1)}, s32[4,1024]{1,0:T(4,128)}, u32[]{:S(2)}) copy-start(s32[4,1024]{1,0:T(4,128)} %dep_ref.3) | copy-start | bytes 49156
  12.8 8.3 %collective-permute-start.3 = (f32[80,128]{1,0:T(8,128)S(1)}, f32[80,128]{1,0:T(8,128)S(1)}, u32[]{:S(2)}, u32[]{:S(2)}) collective-permute-start(f32[80,128]{1,0:T(8,128)S(1)} %get-tuple-element.26), channel_id=1, source_target_pairs={{2,0},{4,2},{6,4},{0,6},{3,1},{5,3},{7,5},{1,7},{10,8},{12,10},{14... | collective-permute-start | bytes 122888 | tf_op jit(solution)/shard_map/ppermute | solution.py:452
  14.3 6.8 %collective-permute-start.2 = (f32[80,128]{1,0:T(8,128)S(1)}, f32[80,128]{1,0:T(8,128)S(1)}, u32[]{:S(2)}, u32[]{:S(2)}) collective-permute-start(f32[80,128]{1,0:T(8,128)S(1)} %get-tuple-element.25.after_ref), channel_id=1, source_target_pairs={{6,0},{0,2},{2,4},{4,6},{7,1},{1,3},{3,5},{5,7},{14,8},{8,10},{10,... | collective-permute-start | bytes 122888 | tf_op jit(solution)/shard_map/ppermute | solution.py:452
  17.3 9.0 %collective-permute-start.9 = (f32[432,128]{1,0:T(8,128)S(1)}, f32[432,128]{1,0:T(8,128)S(1)}, u32[]{:S(2)}, u32[]{:S(2)}) collective-permute-start(f32[432,128]{1,0:T(8,128)S(1)} %get-tuple-element.33), channel_id=1, source_target_pairs={{8,0},{16,8},{24,16},{0,24},{9,1},{17,9},{25,17},{1,25},{10,2},{18... | collective-permute-start | bytes 663560 | tf_op jit(solution)/shard_map/ppermute | solution.py:452
  19.0 7.4 %collective-permute-start.8 = (f32[432,128]{1,0:T(8,128)S(1)}, f32[432,128]{1,0:T(8,128)S(1)}, u32[]{:S(2)}, u32[]{:S(2)}) collective-permute-start(f32[432,128]{1,0:T(8,128)S(1)} %get-tuple-element.29.after_ref), channel_id=1, source_target_pairs={{24,0},{0,8},{8,16},{16,24},{25,1},{1,9},{9,17},{17,25},{26,2},{2,... | collective-permute-start | bytes 663560 | tf_op jit(solution)/shard_map/ppermute | solution.py:452
  21.2 6.5 %collective-permute-start.7 = (f32[120,128]{1,0:T(8,128)S(1)}, f32[120,128]{1,0:T(8,128)S(1)}, u32[]{:S(2)}, u32[]{:S(2)}) collective-permute-start(f32[120,128]{1,0:T(8,128)S(1)} %get-tuple-element.32), channel_id=1, source_target_pairs={{8,0},{16,8},{24,16},{0,24},{9,1},{17,9},{25,17},{1,25},{10,2},{18... | collective-permute-start | bytes 184328 | tf_op jit(solution)/shard_map/ppermute | solution.py:452
  22.0 5.7 %collective-permute-start.6 = (f32[120,128]{1,0:T(8,128)S(1)}, f32[120,128]{1,0:T(8,128)S(1)}, u32[]{:S(2)}, u32[]{:S(2)}) collective-permute-start(f32[120,128]{1,0:T(8,128)S(1)} %get-tuple-element.31.after_ref), channel_id=1, source_target_pairs={{24,0},{0,8},{8,16},{16,24},{25,1},{1,9},{9,17},{17,25},{26,2},{2,... | collective-permute-start | bytes 184328 | tf_op jit(solution)/shard_map/ppermute | solution.py:452
  30.5 9.5 %collective-permute-start.13 = (f32[6,8,128]{2,1,0:T(8,128)S(1)}, f32[6,8,128]{2,1,0:T(8,128)S(1)}, u32[]{:S(2)}, u32[]{:S(2)}) collective-permute-start(f32[6,8,128]{2,1,0:T(8,128)S(1)} %get-tuple-element.42), channel_id=1, source_target_pairs={{2,0},{4,2},{6,4},{0,6},{3,1},{5,3},{7,5},{1,7},{10,8},{12,10},{14... | collective-permute-start | bytes 73736 | tf_op jit(solution)/shard_map/ppermute | solution.py:452
  33.5 6.6 %collective-permute-start.12 = (f32[6,8,128]{2,1,0:T(8,128)S(1)}, f32[6,8,128]{2,1,0:T(8,128)S(1)}, u32[]{:S(2)}, u32[]{:S(2)}) collective-permute-start(f32[6,8,128]{2,1,0:T(8,128)S(1)} %get-tuple-element.43), channel_id=1, source_target_pairs={{6,0},{0,2},{2,4},{4,6},{7,1},{1,3},{3,5},{5,7},{14,8},{8,10},{10,... | collective-permute-start | bytes 73736 | tf_op jit(solution)/shard_map/ppermute | solution.py:452
  33.5 6.6 %collective-permute-start.11 = (f32[6,8,128]{2,1,0:T(8,128)S(1)}, f32[6,8,128]{2,1,0:T(8,128)S(1)}, u32[]{:S(2)}, u32[]{:S(2)}) collective-permute-start(f32[6,8,128]{2,1,0:T(8,128)S(1)} %get-tuple-element.44), channel_id=1, source_target_pairs={{8,0},{16,8},{24,16},{0,24},{9,1},{17,9},{25,17},{1,25},{10,2},{18... | collective-permute-start | bytes 73736 | tf_op jit(solution)/shard_map/ppermute | solution.py:452
  34.2 5.9 %collective-permute-start.10 = (f32[6,8,128]{2,1,0:T(8,128)S(1)}, f32[6,8,128]{2,1,0:T(8,128)S(1)}, u32[]{:S(2)}, u32[]{:S(2)}) collective-permute-start(f32[6,8,128]{2,1,0:T(8,128)S(1)} %get-tuple-element.45), channel_id=1, source_target_pairs={{24,0},{0,8},{8,16},{16,24},{25,1},{1,9},{9,17},{17,25},{26,2},{2,... | collective-permute-start | bytes 73736 | tf_op jit(solution)/shard_map/ppermute | solution.py:452

commit v6 on v5

--- a/solution.py
+++ b/solution.py
@@ -104,7 +104,7 @@
         right = jnp.concatenate(rights, axis=1)
         return acc + lax.dot_general(left, right, NT, preferred_element_type=F32)
 
-    acc = lax.fori_loop(0, steps, step, jnp.zeros((LANES, 2 * LANES), F32), unroll=4)
+    acc = lax.fori_loop(0, steps, step, jnp.zeros((LANES, 2 * LANES), F32), unroll=8)
     out_ref[...] = acc[:, :LANES] + acc[:, LANES:]
 
 
@@ -130,7 +130,7 @@
             base_ref[3 + d, pl.ds(b, 1), :] = mine[3 + d] + TIME_STEP * force
         return carry
 
-    lax.fori_loop(0, blocks, step, 0, unroll=32)
+    lax.fori_loop(0, blocks, step, 0, unroll=64)
 
 
 def table_of(fields, table_ref):
@@ -202,8 +202,8 @@
     lax.fori_loop(0, 2 * per, step, 0, unroll=16)
 
 
-STATE = ((HALO, HALO, HALO), (HALO - 1, HALO, HALO), (HALO, HALO - 1, HALO), (HALO - 1, HALO - 1, HALO - 1))
-VOID = ((HALO, HALO, HALO),)
+STATE = ((HALO - 1, HALO, HALO), (HALO, HALO - 1, HALO), (HALO - 1, HALO - 1, HALO - 1))
+VOID = ((HALO, HALO, HALO), (HALO, HALO, HALO))
 
 
 def y_starts(spec):
@@ -243,17 +243,19 @@
 
 
 def early_kernel(near_ref, far_ref, tile_ref, up_ref, down_ref):
-    for f in range(4):
-        tile_ref[2 * f] = near_ref[64 * f : 64 * f + 64, :]
-        tile_ref[2 * f + 1] = far_ref[64 * f : 64 * f + 64, :]
+    for d in range(3):
+        tile_ref[2 * d] = near_ref[64 * d + 64 : 64 * d + 128, :]
+        tile_ref[2 * d + 1] = far_ref[64 * d + 64 : 64 * d + 128, :]
     slices_y(STATE, tile_ref, up_ref, down_ref)
 
 
-def tile_kernel(mine_ref, got_ref, after_ref, tile_ref, up_ref, down_ref):
+def tile_kernel(mine_ref, got_ref, near_ref, far_ref, after_ref, tile_ref, up_ref, down_ref):
     own = mine_ref[0:64, :] + got_ref[64:128, :]
     far = mine_ref[64:128, :] + got_ref[0:64, :]
     tile_ref[0] = 1.0 / (1.0 + own)
     tile_ref[1] = 1.0 / (1.0 + far)
+    tile_ref[2] = near_ref[0:64, :]
+    tile_ref[3] = far_ref[0:64, :]
     slices_y(VOID, tile_ref, up_ref, down_ref)
 
 
@@ -322,14 +324,14 @@
             total = total + sides[k]
             face_ref[k, x] = void + sides[k]
         invd_ref[x] = 1.0 / total
-        ys = y_sides(void * flow_ref[2, x])
-        zs = z_sides(void * flow_ref[3, x])
+        ys = y_sides(void * flow_ref[1, x])
+        zs = z_sides(void * flow_ref[2, x])
         div_ref[x] = (
-            above * flow_ref[1, x + 1] - below * flow_ref[1, x - 1] + (ys[0] - ys[1]) + (zs[0] - zs[1])
+            above * flow_ref[0, x + 1] - below * flow_ref[0, x - 1] + (ys[0] - ys[1]) + (zs[0] - zs[1])
         )
 
     for t in range(SWEEPS):
-        source = flow_ref.at[0] if t == 0 else even_ref if t % 2 == 0 else odd_ref
+        source = void_ref.at[1] if t == 0 else even_ref if t % 2 == 0 else odd_ref
         target = odd_ref if t % 2 == 0 else even_ref
         for x in range(1 + t, size - 1 - t):
             void = void_ref[0, x]
@@ -347,9 +349,9 @@
         values = final[HALO + x]
         ys, zs = y_sides(values), z_sides(values)
         flows = (
-            flow_ref[1, HALO + x] - 0.5 * (final[HALO + x + 1] - final[HALO + x - 1]),
-            flow_ref[2, HALO + x] - 0.5 * (ys[0] - ys[1]),
-            flow_ref[3, HALO + x] - 0.5 * (zs[0] - zs[1]),
+            flow_ref[0, HALO + x] - 0.5 * (final[HALO + x + 1] - final[HALO + x - 1]),
+            flow_ref[1, HALO + x] - 0.5 * (ys[0] - ys[1]),
+            flow_ref[2, HALO + x] - 0.5 * (zs[0] - zs[1]),
         )
         p_out_ref[x] = values[4:12, :LANES]
         tables[0].append(jnp.exp(-2.65 * jnp.log(void_ref[0, HALO + x][4:12])))
@@ -407,7 +409,7 @@
                 out_ref[f, ats[h], :] = found[f][h]
         return carry
 
-    lax.fori_loop(0, rows // 2, step, 0, unroll=32)
+    lax.fori_loop(0, rows // 2, step, 0, unroll=64)
     drag = TIME_STEP * out_ref[0] * base_ref[6]
     scale = 1.0 / (1.0 + drag)
     speeds = [(base_ref[3 + d] + drag * out_ref[1 + d]) * scale for d in range(3)]
@@ -444,7 +446,7 @@
             vel_ref[d : d + 1, at] = keep_ref[3 + d, pl.ds(b, 1), :]
         return carry
 
-    lax.fori_loop(0, moved_ref.shape[1], spread, 0, unroll=16)
+    lax.fori_loop(0, moved_ref.shape[1], spread, 0, unroll=64)
 
 
 def shifted(block, axis, distance):
@@ -476,7 +478,7 @@
     state_y, state_x = y_starts(STATE)[1], x_starts(STATE)[1]
     void_y, void_x = y_starts(VOID)[1], x_starts(VOID)[1]
     state, state_up, state_down = call(
-        early_kernel, [((8, 64, LANES), F32), ((state_y, LANES), F32), ((state_y, LANES), F32)],
+        early_kernel, [((6, 64, LANES), F32), ((state_y, LANES), F32), ((state_y, LANES), F32)],
         near, far,
     )
     state_ylow = shifted(state_up, "gy", 1)
@@ -486,8 +488,8 @@
         loose=(4,), busy_us=4,
     )
     tile, up, down = call(
-        tile_kernel, [((2, 64, LANES), F32), ((void_y, LANES), F32), ((void_y, LANES), F32)], mine, got, base,
-        loose=(2,),
+        tile_kernel, [((4, 64, LANES), F32), ((void_y, LANES), F32), ((void_y, LANES), F32)], mine, got, near, far, base,
+        loose=(4,),
     )
     ylow = shifted(up, "gy", 1)
     yhigh = shifted(down, "gy", -1)
@@ -516,7 +518,7 @@
         smem=(0,), loose=(4,), busy_us=3,
     )
     (flow,) = call(
-        flow_kernel, [((4, size, 24, 2 * LANES), F32)], state, state_ylow, state_yhigh, state_xlow, state_xhigh, busy_us=1,
+        flow_kernel, [((3, size, 24, 2 * LANES), F32)], state, state_ylow, state_yhigh, state_xlow, state_xhigh, busy_us=1,
     )
     grid = pltpu.VMEM((size, 24, 2 * LANES), F32)
     p_out, v_out, table, sent = call(
@@ -527,7 +529,7 @@
         ],
         tile, ylow, yhigh, xlow, xhigh, flow, leave,
         scratch=[
-            pltpu.VMEM((1, size, 24, 2 * LANES), F32), grid, grid, grid, grid,
+            pltpu.VMEM((2, size, 24, 2 * LANES), F32), grid, grid, grid, grid,
             pltpu.VMEM((4, size, 24, 2 * LANES), F32),
         ],
         busy_us=6,

time: 43.5 us -> 41.7 us (0.959)
  waiting for transfers between devices: 4.82 us -> 2.6 us
  starting transfers between devices: 17.4 us -> 18.2 us
    ppermute x14, waiting for transfers between devices: 4.82 us -> 2.6 us  [shifted(): lax.ppermute(block, axis, [((i - distance) % count, i) for i in range(cou...]
    ppermute x14, starting transfers between devices: 17.4 us -> 18.2 us  [shifted(): lax.ppermute(block, axis, [((i - distance) % count, i) for i in range(cou...]
  transfers between devices with their start and end apart: 14 -> 14, of which waited for: 3 -> 2; matrix products, arithmetic and copies ran while one was open for 0% -> 0% of each run, Pallas kernels for 31% -> 30%
where the time goes in v6:
time: 41.7 us; the launch traced here: 41.6 us
  Pallas kernels  19 us (46%)
  starting transfers between devices  18.2 us (44%)
  waiting for transfers between devices  2.6 us (6%)
  local copies, waits for them, and re-layouts  0.9 us (2%)
  between operations  0.83 us (2%)
    pallas_call x14, Pallas kernels, call(): pl.pallas_call(kernel, out_shape=outs_list, in_specs=specs, out_specs=[vm...  19 us
    ppermute x14, starting transfers between devices, shifted(): lax.ppermute(block, axis, [((i - distance) % count, i) for i in range(cou...  18.2 us
    ppermute x14, waiting for transfers between devices, shifted(): lax.ppermute(block, axis, [((i - distance) % count, i) for i in range(cou...  2.6 us
    unnamed x16, local copies, waits for them, and re-layouts  0.89 us
  transfers between devices with their start and end apart: 14, of which 2 were waited for; matrix products, arithmetic and copies ran while one was open for 0% of the time, Pallas kernels for 30%

profile of v6, /device:TPU:1, one launch (start us, length us, event | category | flops | bytes accessed | tf_op | source)
XLA Modules:
  0.0 41.6 jit_solution(4766976130100086562)
XLA Ops:
  0.6 0.0 copy-start.3
  0.6 0.0 copy-start.6
  0.7 0.9 %copy-done.3 = f32[3,8,8,128]{3,2,1,0:T(8,128)S(1)} copy-done((f32[3,8,8,128]{3,2,1,0:T(8,128)S(1)}, f32[3,8,8,128]{3,2,1,0:T(8,128)}, u32[]{:S(2)}) %copy-start.3) | copy-done | bytes 98328
  1.5 0.0 copy-done.6
  1.5 0.0 copy-start.4
  1.5 0.0 copy-start.5
  1.5 2.1 %collective-permute-start.1 = (f32[256,128]{1,0:T(8,128)S(1)}, f32[256,128]{1,0:T(8,128)S(1)}, u32[]{:S(2)}, u32[]{:S(2)}) collective-permute-start(f32[256,128]{1,0:T(8,128)S(1)} %shard_map.112.after_ref.near_ref), channel_id=1, source_target_pairs={{1,0},{0,1},{3,2},{2,3},{5,4},{4,5},{7,6},{6,7},{9,8},{8,9},{11,10... | collective-permute-start | bytes 393224 | tf_op jit(solution)/shard_map/ppermute | solution.py:454
  3.7 0.0 copy-done.4
  3.7 0.0 copy-done.5
  3.7 0.0 copy-start
  3.7 0.0 copy-start.1
  3.7 0.0 copy-start.2
  3.7 2.9 %shard_map.113.mine_ref = f32[128,128]{1,0:T(8,128)S(1)} custom-call(s32[1]{0:T(128)} %bitcast.sec_ref, f32[128,128]{1,0:T(8,128)S(1)} %bitcast.6, s32[128,128]{1,0:T(8,128)S(1)} %bitcast.8, f32[256,128]{1,0:T(8,128)S(1)} %shard_map.112.after_ref.near_ref), custom_call_target="tpu_custom_call" | custom-call | flops 4600000000 | bytes 4096 | tf_op jit(solution)/shard_map/pallas_call | solution.py:33
  6.6 0.8 %collective-permute-start = (f32[128,128]{1,0:T(8,128)S(1)}, f32[128,128]{1,0:T(8,128)S(1)}, u32[]{:S(2)}, u32[]{:S(2)}) collective-permute-start(f32[128,128]{1,0:T(8,128)S(1)} %shard_map.113.mine_ref), channel_id=1, source_target_pairs={{1,0},{0,1},{3,2},{2,3},{5,4},{4,5},{7,6},{6,7},{9,8},{8,9},{11,10... | collective-permute-start | bytes 196616 | tf_op jit(solution)/shard_map/ppermute | solution.py:454
  7.4 0.0 collective-permute-done.1.far_ref
  7.4 0.1 shard_map.114
  7.5 1.4 %collective-permute-start.4 = (f32[208,128]{1,0:T(8,128)S(1)}, f32[208,128]{1,0:T(8,128)S(1)}, u32[]{:S(2)}, u32[]{:S(2)}) collective-permute-start(f32[208,128]{1,0:T(8,128)S(1)} %get-tuple-element.27), channel_id=1, source_target_pairs={{6,0},{0,2},{2,4},{4,6},{7,1},{1,3},{3,5},{5,7},{14,8},{8,10},{10,... | collective-permute-start | bytes 319496 | tf_op jit(solution)/shard_map/ppermute | solution.py:454
  8.8 2.1 %collective-permute-start.5 = (f32[208,128]{1,0:T(8,128)S(1)}, f32[208,128]{1,0:T(8,128)S(1)}, u32[]{:S(2)}, u32[]{:S(2)}) collective-permute-start(f32[208,128]{1,0:T(8,128)S(1)} %get-tuple-element.28), channel_id=1, source_target_pairs={{2,0},{4,2},{6,4},{0,6},{3,1},{5,3},{7,5},{1,7},{10,8},{12,10},{14... | collective-permute-start | bytes 319496 | tf_op jit(solution)/shard_map/ppermute | solution.py:454
  10.9 0.0 copy-done
  10.9 0.0 copy-done.1
  10.9 0.0 copy-done.2
  10.9 0.0 copy-start.7
  10.9 1.5 %shard_map.115.after_ref.base_ref = f32[7,128,128]{2,1,0:T(8,128)S(1)} custom-call(f32[128,128]{1,0:T(8,128)S(1)} %bitcast.7, f32[3,16384]{1,0:T(4,128)S(1)} %copy-done.1, f32[3,16384]{1,0:T(4,128)S(1)} %copy-done.2, s32[8,16384]{1,0:T(8,128)S(1)} %copy-done, f32[6,64,128]{2,1,0:T(8,128)S(1)} %get-tuple-element.23.after_ref.tile_ref), custom_call_target="tpu_custom_call" | custom-call | flops 4600000000 | bytes 4096 | tf_op jit(solution)/shard_map/pallas_call | solution.py:33
  12.4 0.0 collective-permute-done.got_ref
  12.4 1.5 %collective-permute-start.3 = (f32[160,128]{1,0:T(8,128)S(1)}, f32[160,128]{1,0:T(8,128)S(1)}, u32[]{:S(2)}, u32[]{:S(2)}) collective-permute-start(f32[160,128]{1,0:T(8,128)S(1)} %get-tuple-element.26), channel_id=1, source_target_pairs={{2,0},{4,2},{6,4},{0,6},{3,1},{5,3},{7,5},{1,7},{10,8},{12,10},{14... | collective-permute-start | bytes 245768 | tf_op jit(solution)/shard_map/ppermute | solution.py:454
  13.9 0.1 collective-permute-start.2
  14.0 0.0 collective-permute-done.4.low_ref.ylow_ref
  14.0 1.1 %collective-permute-done.5.high_ref.yhigh_ref = f32[208,128]{1,0:T(8,128)S(1)} collective-permute-done((f32[208,128]{1,0:T(8,128)S(1)}, f32[208,128]{1,0:T(8,128)S(1)}, u32[]{:S(2)}, u32[]{:S(2)}) %collective-permute-start.5) | collective-permute-done | bytes 106528 | tf_op jit(solution)/shard_map/ppermute | solution.py:454
  15.1 0.1 shard_map.117
  15.1 2.1 %collective-permute-start.9 = (f32[312,128]{1,0:T(8,128)S(1)}, f32[312,128]{1,0:T(8,128)S(1)}, u32[]{:S(2)}, u32[]{:S(2)}) collective-permute-start(f32[312,128]{1,0:T(8,128)S(1)} %get-tuple-element.33), channel_id=1, source_target_pairs={{8,0},{16,8},{24,16},{0,24},{9,1},{17,9},{25,17},{1,25},{10,2},{18... | collective-permute-start | bytes 479240 | tf_op jit(solution)/shard_map/ppermute | solution.py:454
  17.2 1.2 %collective-permute-start.8 = (f32[312,128]{1,0:T(8,128)S(1)}, f32[312,128]{1,0:T(8,128)S(1)}, u32[]{:S(2)}, u32[]{:S(2)}) collective-permute-start(f32[312,128]{1,0:T(8,128)S(1)} %get-tuple-element.29.after_ref), channel_id=1, source_target_pairs={{24,0},{0,8},{8,16},{16,24},{25,1},{1,9},{9,17},{17,25},{26,2},{2,... | collective-permute-start | bytes 479240 | tf_op jit(solution)/shard_map/ppermute | solution.py:454
  18.4 0.0 copy-done.7
  18.4 0.9 %shard_map.118 = (f32[128,128]{1,0:T(8,128)S(1)}, bf16[256,4096]{1,0:T(8,128)(2,1)S(1)}, bf16[64,4096]{1,0:T(8,128)(2,1)S(1)}) custom-call(s32[4,1024]{1,0:T(4,128)S(1)} %copy-done.7, f32[312,128]{1,0:T(8,128)S(1)} %get-tuple-element.29.after_ref), custom_call_target="tpu_custom_call" | custom-call | flops 2300000000 | bytes 4096 | tf_op jit(solution)/shard_map/pallas_call | solution.py:33
  19.3 0.0 collective-permute-done.3.high_ref.yhigh_ref
  19.3 0.0 collective-permute-done.2.low_ref.ylow_ref
  19.4 2.6 %collective-permute-start.7 = (f32[240,128]{1,0:T(8,128)S(1)}, f32[240,128]{1,0:T(8,128)S(1)}, u32[]{:S(2)}, u32[]{:S(2)}) collective-permute-start(f32[240,128]{1,0:T(8,128)S(1)} %get-tuple-element.32), channel_id=1, source_target_pairs={{8,0},{16,8},{24,16},{0,24},{9,1},{17,9},{25,17},{1,25},{10,2},{18... | collective-permute-start | bytes 368648 | tf_op jit(solution)/shard_map/ppermute | solution.py:454
  22.0 1.2 %collective-permute-start.6 = (f32[240,128]{1,0:T(8,128)S(1)}, f32[240,128]{1,0:T(8,128)S(1)}, u32[]{:S(2)}, u32[]{:S(2)}) collective-permute-start(f32[240,128]{1,0:T(8,128)S(1)} %get-tuple-element.31.after_ref), channel_id=1, source_target_pairs={{24,0},{0,8},{8,16},{16,24},{25,1},{1,9},{9,17},{17,25},{26,2},{2,... | collective-permute-start | bytes 368648 | tf_op jit(solution)/shard_map/ppermute | solution.py:454
  23.2 2.5 %shard_map.121.leave_ref = f32[8,32,128]{2,1,0:T(8,128)S(1)} custom-call(s32[1]{0:T(128)} %bitcast.sec_ref, f32[7,128,128]{2,1,0:T(8,128)S(1)} %shard_map.115.after_ref.base_ref, s32[128,128]{1,0:T(8,128)S(1)} %bitcast.9, s32[4,1024]{1,0:T(4,128)S(1)} %copy-done.7, f32[240,128]{1,0:T(8,128)S(1)} %get-tuple-element.31.after_ref), custom_call_target="tpu_custom_call" | custom-call | flops 3449999872 | bytes 4096 | tf_op jit(solution)/shard_map/pallas_call | solution.py:33
  25.6 0.0 collective-permute-done.9.xhigh_ref
  25.7 0.0 collective-permute-done.8.xlow_ref
  25.7 0.1 shard_map.120.flow_ref
  25.8 1.5 %collective-permute-done.7.xhigh_ref = f32[240,128]{1,0:T(8,128)S(1)} collective-permute-done((f32[240,128]{1,0:T(8,128)S(1)}, f32[240,128]{1,0:T(8,128)S(1)}, u32[]{:S(2)}, u32[]{:S(2)}) %collective-permute-start.7) | collective-permute-done | bytes 122912 | tf_op jit(solution)/shard_map/ppermute | solution.py:454
  27.3 0.0 collective-permute-done.6.xlow_ref
  27.3 2.9 %shard_map.122 = (f32[8,8,128]{2,1,0:T(8,128)}, f32[3,8,8,128]{3,2,1,0:T(8,128)}, bf16[512,256]{1,0:T(8,128)(2,1)S(1)}, f32[6,32,128]{2,1,0:T(8,128)S(1)}) custom-call(f32[4,64,128]{2,1,0:T(8,128)S(1)} %get-tuple-element.24.tile_ref, f32[160,128]{1,0:T(8,128)S(1)} %collective-permute-done.2.low_ref.ylow_ref, ...), custom_call_target="tpu_custom_call" | custom-call | flops 6899999744 | bytes 4096 | tf_op jit(solution)/shard_map/pallas_call | solution.py:33
  30.2 1.2 %collective-permute-start.13 = (f32[6,8,128]{2,1,0:T(8,128)S(1)}, f32[6,8,128]{2,1,0:T(8,128)S(1)}, u32[]{:S(2)}, u32[]{:S(2)}) collective-permute-start(f32[6,8,128]{2,1,0:T(8,128)S(1)} %get-tuple-element.42), channel_id=1, source_target_pairs={{2,0},{4,2},{6,4},{0,6},{3,1},{5,3},{7,5},{1,7},{10,8},{12,10},{14... | collective-permute-start | bytes 73736 | tf_op jit(solution)/shard_map/ppermute | solution.py:454
  31.4 0.3 collective-permute-start.12
  31.8 1.0 %collective-permute-start.11 = (f32[6,8,128]{2,1,0:T(8,128)S(1)}, f32[6,8,128]{2,1,0:T(8,128)S(1)}, u32[]{:S(2)}, u32[]{:S(2)}) collective-permute-start(f32[6,8,128]{2,1,0:T(8,128)S(1)} %get-tuple-element.44), channel_id=1, source_target_pairs={{8,0},{16,8},{24,16},{0,24},{9,1},{17,9},{25,17},{1,25},{10,2},{18... | collective-permute-start | bytes 73736 | tf_op jit(solution)/shard_map/ppermute | solution.py:454
  32.7 0.8 %collective-permute-start.10 = (f32[6,8,128]{2,1,0:T(8,128)S(1)}, f32[6,8,128]{2,1,0:T(8,128)S(1)}, u32[]{:S(2)}, u32[]{:S(2)}) collective-permute-start(f32[6,8,128]{2,1,0:T(8,128)S(1)} %get-tuple-element.45), channel_id=1, source_target_pairs={{24,0},{0,8},{8,16},{16,24},{25,1},{1,9},{9,17},{17,25},{26,2},{2,... | collective-permute-start | bytes 73736 | tf_op jit(solution)/shard_map/ppermute | solution.py:454
  33.5 4.6 %shard_map.123.moved_ref = f32[6,128,128]{2,1,0:T(8,128)S(1)} custom-call(s32[1]{0:T(128)} %bitcast.sec_ref, bf16[512,256]{1,0:T(8,128)(2,1)S(1)} %get-tuple-element.38.table_ref, s32[128,128]{1,0:T(8,128)S(1)} %bitcast.10, f32[7,128,128]{2,1,0:T(8,128)S(1)} %shard_map.115.after_ref.base_ref), custom_call_target="tpu_custom_call" | custom-call | flops 6899999744 | bytes 4096 | tf_op jit(solution)/shard_map/pallas_call | solution.py:33
  38.1 0.0 collective-permute-done.13.d_ref
  38.2 0.0 collective-permute-done.12.c_ref
  38.2 0.0 collective-permute-done.11.b_ref
  38.2 0.0 collective-permute-done.10.a_ref
  38.2 3.4 %shard_map.124 = (f32[3,16384]{1,0:T(4,128)}, f32[3,16384]{1,0:T(4,128)}) custom-call(bf16[256,4096]{1,0:T(8,128)(2,1)S(1)} %get-tuple-element.36.left_ref, bf16[64,4096]{1,0:T(8,128)(2,1)S(1)} %get-tuple-element.37.low_ref, f32[128,128]{1,0:T(8,128)S(1)} %get-tuple-element.30.after_ref.mask_ref, f32[6,128,128]{2,1,0:T(8,128)S(1)} %shard_map.123.moved_ref, ...), custom_call_target="tpu_custom_call" | custom-call | flops 4600000000 | bytes 4096 | tf_op jit(solution)/shard_map/pallas_call | solution.py:33
  (5 shorter events, 0.1 us)
Async XLA Ops:
  0.6 0.9 %copy-start.3 = (f32[3,8,8,128]{3,2,1,0:T(8,128)S(1)}, f32[3,8,8,128]{3,2,1,0:T(8,128)}, u32[]{:S(2)}) copy-start(f32[3,8,8,128]{3,2,1,0:T(8,128)} %param.9) | copy-start | bytes 294916
  0.6 0.9 %copy-start.6 = (f32[8,8,128]{2,1,0:T(8,128)S(1)}, f32[8,8,128]{2,1,0:T(8,128)}, u32[]{:S(2)}) copy-start(f32[8,8,128]{2,1,0:T(8,128)} %param.8) | copy-start | bytes 98308
  1.5 2.2 %copy-start.4 = (f32[16384]{0:T(1024)S(1)}, f32[16384]{0:T(1024)}, u32[]{:S(2)}) copy-start(f32[16384]{0:T(1024)} %param.12) | copy-start | bytes 196612
  1.5 2.2 %copy-start.5 = (s32[16384]{0:T(1024)S(1)}, s32[16384]{0:T(1024)}, u32[]{:S(2)}) copy-start(s32[16384]{0:T(1024)} %param.13) | copy-start | bytes 196612
  1.5 5.9 %collective-permute-start.1 = (f32[256,128]{1,0:T(8,128)S(1)}, f32[256,128]{1,0:T(8,128)S(1)}, u32[]{:S(2)}, u32[]{:S(2)}) collective-permute-start(f32[256,128]{1,0:T(8,128)S(1)} %shard_map.112.after_ref.near_ref), channel_id=1, source_target_pairs={{1,0},{0,1},{3,2},{2,3},{5,4},{4,5},{7,6},{6,7},{9,8},{8,9},{11,10... | collective-permute-start | bytes 393224 | tf_op jit(solution)/shard_map/ppermute | solution.py:454
  3.7 7.2 %copy-start = (s32[8,16384]{1,0:T(8,128)S(1)}, s32[8,16384]{1,0:T(8,128)}, u32[]{:S(2)}) copy-start(s32[8,16384]{1,0:T(8,128)} %pair_ref.1) | copy-start | bytes 1572868
  3.7 7.2 %copy-start.1 = (f32[3,16384]{1,0:T(4,128)S(1)}, f32[3,16384]{1,0:T(4,128)}, u32[]{:S(2)}) copy-start(f32[3,16384]{1,0:T(4,128)} %pos_ref.1) | copy-start | bytes 589828
  3.7 7.2 %copy-start.2 = (f32[3,16384]{1,0:T(4,128)S(1)}, f32[3,16384]{1,0:T(4,128)}, u32[]{:S(2)}) copy-start(f32[3,16384]{1,0:T(4,128)} %vel_ref.1) | copy-start | bytes 589828
  6.6 5.8 %collective-permute-start = (f32[128,128]{1,0:T(8,128)S(1)}, f32[128,128]{1,0:T(8,128)S(1)}, u32[]{:S(2)}, u32[]{:S(2)}) collective-permute-start(f32[128,128]{1,0:T(8,128)S(1)} %shard_map.113.mine_ref), channel_id=1, source_target_pairs={{1,0},{0,1},{3,2},{2,3},{5,4},{4,5},{7,6},{6,7},{9,8},{8,9},{11,10... | collective-permute-start | bytes 196616 | tf_op jit(solution)/shard_map/ppermute | solution.py:454
  7.5 6.5 %collective-permute-start.4 = (f32[208,128]{1,0:T(8,128)S(1)}, f32[208,128]{1,0:T(8,128)S(1)}, u32[]{:S(2)}, u32[]{:S(2)}) collective-permute-start(f32[208,128]{1,0:T(8,128)S(1)} %get-tuple-element.27), channel_id=1, source_target_pairs={{6,0},{0,2},{2,4},{4,6},{7,1},{1,3},{3,5},{5,7},{14,8},{8,10},{10,... | collective-permute-start | bytes 319496 | tf_op jit(solution)/shard_map/ppermute | solution.py:454
  8.8 6.3 %collective-permute-start.5 = (f32[208,128]{1,0:T(8,128)S(1)}, f32[208,128]{1,0:T(8,128)S(1)}, u32[]{:S(2)}, u32[]{:S(2)}) collective-permute-start(f32[208,128]{1,0:T(8,128)S(1)} %get-tuple-element.28), channel_id=1, source_target_pairs={{2,0},{4,2},{6,4},{0,6},{3,1},{5,3},{7,5},{1,7},{10,8},{12,10},{14... | collective-permute-start | bytes 319496 | tf_op jit(solution)/shard_map/ppermute | solution.py:454
  10.9 7.5 %copy-start.7 = (s32[4,1024]{1,0:T(4,128)S(1)}, s32[4,1024]{1,0:T(4,128)}, u32[]{:S(2)}) copy-start(s32[4,1024]{1,0:T(4,128)} %dep_ref.3) | copy-start | bytes 49156
  12.4 6.9 %collective-permute-start.3 = (f32[160,128]{1,0:T(8,128)S(1)}, f32[160,128]{1,0:T(8,128)S(1)}, u32[]{:S(2)}, u32[]{:S(2)}) collective-permute-start(f32[160,128]{1,0:T(8,128)S(1)} %get-tuple-element.26), channel_id=1, source_target_pairs={{2,0},{4,2},{6,4},{0,6},{3,1},{5,3},{7,5},{1,7},{10,8},{12,10},{14... | collective-permute-start | bytes 245768 | tf_op jit(solution)/shard_map/ppermute | solution.py:454
  13.9 5.4 %collective-permute-start.2 = (f32[160,128]{1,0:T(8,128)S(1)}, f32[160,128]{1,0:T(8,128)S(1)}, u32[]{:S(2)}, u32[]{:S(2)}) collective-permute-start(f32[160,128]{1,0:T(8,128)S(1)} %get-tuple-element.25.after_ref), channel_id=1, source_target_pairs={{6,0},{0,2},{2,4},{4,6},{7,1},{1,3},{3,5},{5,7},{14,8},{8,10},{10,... | collective-permute-start | bytes 245768 | tf_op jit(solution)/shard_map/ppermute | solution.py:454
  15.1 10.5 %collective-permute-start.9 = (f32[312,128]{1,0:T(8,128)S(1)}, f32[312,128]{1,0:T(8,128)S(1)}, u32[]{:S(2)}, u32[]{:S(2)}) collective-permute-start(f32[312,128]{1,0:T(8,128)S(1)} %get-tuple-element.33), channel_id=1, source_target_pairs={{8,0},{16,8},{24,16},{0,24},{9,1},{17,9},{25,17},{1,25},{10,2},{18... | collective-permute-start | bytes 479240 | tf_op jit(solution)/shard_map/ppermute | solution.py:454
  17.2 8.4 %collective-permute-start.8 = (f32[312,128]{1,0:T(8,128)S(1)}, f32[312,128]{1,0:T(8,128)S(1)}, u32[]{:S(2)}, u32[]{:S(2)}) collective-permute-start(f32[312,128]{1,0:T(8,128)S(1)} %get-tuple-element.29.after_ref), channel_id=1, source_target_pairs={{24,0},{0,8},{8,16},{16,24},{25,1},{1,9},{9,17},{17,25},{26,2},{2,... | collective-permute-start | bytes 479240 | tf_op jit(solution)/shard_map/ppermute | solution.py:454
  19.4 7.9 %collective-permute-start.7 = (f32[240,128]{1,0:T(8,128)S(1)}, f32[240,128]{1,0:T(8,128)S(1)}, u32[]{:S(2)}, u32[]{:S(2)}) collective-permute-start(f32[240,128]{1,0:T(8,128)S(1)} %get-tuple-element.32), channel_id=1, source_target_pairs={{8,0},{16,8},{24,16},{0,24},{9,1},{17,9},{25,17},{1,25},{10,2},{18... | collective-permute-start | bytes 368648 | tf_op jit(solution)/shard_map/ppermute | solution.py:454
  22.0 5.3 %collective-permute-start.6 = (f32[240,128]{1,0:T(8,128)S(1)}, f32[240,128]{1,0:T(8,128)S(1)}, u32[]{:S(2)}, u32[]{:S(2)}) collective-permute-start(f32[240,128]{1,0:T(8,128)S(1)} %get-tuple-element.31.after_ref), channel_id=1, source_target_pairs={{24,0},{0,8},{8,16},{16,24},{25,1},{1,9},{9,17},{17,25},{26,2},{2,... | collective-permute-start | bytes 368648 | tf_op jit(solution)/shard_map/ppermute | solution.py:454
  30.2 7.9 %collective-permute-start.13 = (f32[6,8,128]{2,1,0:T(8,128)S(1)}, f32[6,8,128]{2,1,0:T(8,128)S(1)}, u32[]{:S(2)}, u32[]{:S(2)}) collective-permute-start(f32[6,8,128]{2,1,0:T(8,128)S(1)} %get-tuple-element.42), channel_id=1, source_target_pairs={{2,0},{4,2},{6,4},{0,6},{3,1},{5,3},{7,5},{1,7},{10,8},{12,10},{14... | collective-permute-start | bytes 73736 | tf_op jit(solution)/shard_map/ppermute | solution.py:454
  31.4 6.7 %collective-permute-start.12 = (f32[6,8,128]{2,1,0:T(8,128)S(1)}, f32[6,8,128]{2,1,0:T(8,128)S(1)}, u32[]{:S(2)}, u32[]{:S(2)}) collective-permute-start(f32[6,8,128]{2,1,0:T(8,128)S(1)} %get-tuple-element.43), channel_id=1, source_target_pairs={{6,0},{0,2},{2,4},{4,6},{7,1},{1,3},{3,5},{5,7},{14,8},{8,10},{10,... | collective-permute-start | bytes 73736 | tf_op jit(solution)/shard_map/ppermute | solution.py:454
  31.8 6.4 %collective-permute-start.11 = (f32[6,8,128]{2,1,0:T(8,128)S(1)}, f32[6,8,128]{2,1,0:T(8,128)S(1)}, u32[]{:S(2)}, u32[]{:S(2)}) collective-permute-start(f32[6,8,128]{2,1,0:T(8,128)S(1)} %get-tuple-element.44), channel_id=1, source_target_pairs={{8,0},{16,8},{24,16},{0,24},{9,1},{17,9},{25,17},{1,25},{10,2},{18... | collective-permute-start | bytes 73736 | tf_op jit(solution)/shard_map/ppermute | solution.py:454
  32.7 5.4 %collective-permute-start.10 = (f32[6,8,128]{2,1,0:T(8,128)S(1)}, f32[6,8,128]{2,1,0:T(8,128)S(1)}, u32[]{:S(2)}, u32[]{:S(2)}) collective-permute-start(f32[6,8,128]{2,1,0:T(8,128)S(1)} %get-tuple-element.45), channel_id=1, source_target_pairs={{24,0},{0,8},{8,16},{16,24},{25,1},{1,9},{9,17},{17,25},{26,2},{2,... | collective-permute-start | bytes 73736 | tf_op jit(solution)/shard_map/ppermute | solution.py:454

commit v7 on v6

--- a/solution.py
+++ b/solution.py
@@ -273,12 +273,11 @@
                 out_ref[start : start + 8 + 2 * extra, :] = rows
 
 
-def assemble(spec, tile_ref, ylow_ref, yhigh_ref, xlow_ref, xhigh_ref, grid_ref):
+def assemble_sides(spec, xlow_ref, xhigh_ref, grid_ref):
     filler = jnp.ones((8, LANES), F32)
     starts = x_starts(spec)[0]
-    for g, y_start in enumerate(y_starts(spec)[0]):
+    for g in range(2 * len(spec)):
         f, h = g // 2, g % 2
-        depth = spec[f][0]
         lanes = slice(LANES * h, LANES * (h + 1))
         for x in list(range(HALO)) + list(range(HALO + 8, 2 * HALO + 8)):
             for m in range(3):
@@ -286,6 +285,14 @@
         for away, (start, extra) in enumerate(starts[g], 1):
             for x, side_ref in ((HALO - away, xlow_ref), (HALO + 7 + away, xhigh_ref)):
                 grid_ref[f, x, 4 - extra : 12 + extra, lanes] = side_ref[start : start + 8 + 2 * extra, :]
+
+
+def assemble_middle(spec, tile_ref, ylow_ref, yhigh_ref, grid_ref, first):
+    filler = jnp.ones((8, LANES), F32)
+    for g, y_start in enumerate(y_starts(spec)[0]):
+        f, h = g // 2, g % 2
+        depth = spec[f][0]
+        lanes = slice(LANES * h, LANES * (h + 1))
         for x in range(8):
             far = depth - 4
             rows = [
@@ -296,7 +303,7 @@
             ]
             if far > 0:
                 rows.append(ylow_ref[y_start + x : y_start + x + 1, :])
-            grid_ref[f, HALO + x, 0:24, lanes] = jnp.concatenate(rows, axis=0)
+            grid_ref[f, first + x, 0:24, lanes] = jnp.concatenate(rows, axis=0)
 
 
 def y_sides(values):
@@ -307,41 +314,63 @@
     return pltpu.roll(values, 2 * LANES - 1, 1), pltpu.roll(values, 1, 1)
 
 
+def set_up(void, flow_ref, x):
+    middle, above, below = void(x), void(x + 1), void(x - 1)
+    sides = y_sides(middle) + z_sides(middle)
+    total = 6.0 * middle + above + below
+    for k in range(4):
+        total = total + sides[k]
+    ys = y_sides(middle * flow_ref[1, x])
+    zs = z_sides(middle * flow_ref[2, x])
+    source = above * flow_ref[0, x + 1] - below * flow_ref[0, x - 1] + (ys[0] - ys[1]) + (zs[0] - zs[1])
+    return [middle + side for side in sides], 1.0 / total, source
+
+
+def swept(void, press, faces, inverse, source, x):
+    values = press(x)
+    sides = y_sides(values) + z_sides(values)
+    total = (void(x) + void(x + 1)) * press(x + 1) - source
+    total = total + (void(x) + void(x - 1)) * press(x - 1)
+    for k in range(4):
+        total = total + faces[k] * sides[k]
+    return total * inverse
+
+
+FIRST, LAST = HALO + 1, HALO + 7
+
+
 def fluid_kernel(
-    tile_ref, ylow_ref, yhigh_ref, xlow_ref, xhigh_ref, flow_ref, leave_ref,
+    xlow_ref, xhigh_ref, flow_ref, own_ref, inner_ref, leave_ref,
     p_out_ref, v_out_ref, table_ref, sent_ref,
-    void_ref, even_ref, odd_ref, invd_ref, div_ref, face_ref,
+    void_ref, even_ref, odd_ref, set_ref,
 ):
     size = 8 + 2 * HALO
-    assemble(VOID, tile_ref, ylow_ref, yhigh_ref, xlow_ref, xhigh_ref, void_ref)
+    assemble_sides(VOID, xlow_ref, xhigh_ref, void_ref)
+
+    def field(f):
+        return lambda x: own_ref[f, x - HALO] if HALO <= x < HALO + 8 else void_ref[f, x]
+
+    void = field(0)
+
+    def setting(k, x):
+        return inner_ref[k, x - FIRST] if FIRST <= x < LAST else set_ref[k, x]
 
     for x in range(1, size - 1):
-        void = void_ref[0, x]
-        above, below = void_ref[0, x + 1], void_ref[0, x - 1]
-        sides = y_sides(void) + z_sides(void)
-        total = 6.0 * void + above + below
-        for k in range(4):
-            total = total + sides[k]
-            face_ref[k, x] = void + sides[k]
-        invd_ref[x] = 1.0 / total
-        ys = y_sides(void * flow_ref[1, x])
-        zs = z_sides(void * flow_ref[2, x])
-        div_ref[x] = (
-            above * flow_ref[0, x + 1] - below * flow_ref[0, x - 1] + (ys[0] - ys[1]) + (zs[0] - zs[1])
-        )
+        if not FIRST <= x < LAST:
+            faces, inverse, source = set_up(void, flow_ref, x)
+            for k, values in enumerate(faces + [inverse, source]):
+                set_ref[k, x] = values
+
+    def first_sweep(x):
+        return inner_ref[6, x - FIRST] if FIRST <= x < LAST else odd_ref[x]
 
     for t in range(SWEEPS):
-        source = void_ref.at[1] if t == 0 else even_ref if t % 2 == 0 else odd_ref
+        before = field(1) if t == 0 else first_sweep if t == 1 else (lambda x, ref=even_ref if t % 2 == 0 else odd_ref: ref[x])
         target = odd_ref if t % 2 == 0 else even_ref
         for x in range(1 + t, size - 1 - t):
-            void = void_ref[0, x]
-            values = source[x]
-            sides = y_sides(values) + z_sides(values)
-            total = (void + void_ref[0, x + 1]) * source[x + 1] - div_ref[x]
-            total = total + (void + void_ref[0, x - 1]) * source[x - 1]
-            for k in range(4):
-                total = total + face_ref[k, x] * sides[k]
-            target[x] = total * invd_ref[x]
+            if t > 0 or not FIRST <= x < LAST:
+                faces = [setting(k, x) for k in range(4)]
+                target[x] = swept(void, before, faces, setting(4, x), setting(5, x), x)
 
     final = even_ref if SWEEPS % 2 == 0 else odd_ref
     tables = [[], [], [], []]
@@ -354,7 +383,7 @@
             flow_ref[2, HALO + x] - 0.5 * (zs[0] - zs[1]),
         )
         p_out_ref[x] = values[4:12, :LANES]
-        tables[0].append(jnp.exp(-2.65 * jnp.log(void_ref[0, HALO + x][4:12])))
+        tables[0].append(jnp.exp(-2.65 * jnp.log(own_ref[0, x][4:12])))
         for d in range(3):
             kept = flows[d][4:12]
             v_out_ref[d, x] = kept[:, :LANES]
@@ -389,8 +418,19 @@
         sent_ref[d] = leave_ref[d] + TIME_STEP * speeds[d]
 
 
-def flow_kernel(tile_ref, ylow_ref, yhigh_ref, xlow_ref, xhigh_ref, flow_ref):
-    assemble(STATE, tile_ref, ylow_ref, yhigh_ref, xlow_ref, xhigh_ref, flow_ref)
+def flow_kernel(
+    tile_ref, ylow_ref, yhigh_ref, xlow_ref, xhigh_ref, void_tile_ref, void_low_ref, void_high_ref,
+    flow_ref, own_ref, inner_ref,
+):
+    assemble_sides(STATE, xlow_ref, xhigh_ref, flow_ref)
+    assemble_middle(STATE, tile_ref, ylow_ref, yhigh_ref, flow_ref, HALO)
+    assemble_middle(VOID, void_tile_ref, void_low_ref, void_high_ref, own_ref, 0)
+    void, press = (lambda x: own_ref[0, x - HALO]), (lambda x: own_ref[1, x - HALO])
+    for x in range(FIRST, LAST):
+        faces, inverse, source = set_up(void, flow_ref, x)
+        result = swept(void, press, faces, inverse, source, x)
+        for k, values in enumerate(faces + [inverse, source, result]):
+            inner_ref[k, x - FIRST] = values
 
 
 def main_kernel(sec_ref, table_ref, cell_ref, base_ref, out_ref, hi_ref, lo_ref):
@@ -517,8 +557,12 @@
         ],
         smem=(0,), loose=(4,), busy_us=3,
     )
-    (flow,) = call(
-        flow_kernel, [((3, size, 24, 2 * LANES), F32)], state, state_ylow, state_yhigh, state_xlow, state_xhigh, busy_us=1,
+    flow, own, inner = call(
+        flow_kernel,
+        [
+            ((3, size, 24, 2 * LANES), F32), ((2, 8, 24, 2 * LANES), F32), ((7, LAST - FIRST, 24, 2 * LANES), F32),
+        ],
+        state, state_ylow, state_yhigh, state_xlow, state_xhigh, tile, ylow, yhigh, busy_us=1,
     )
     grid = pltpu.VMEM((size, 24, 2 * LANES), F32)
     p_out, v_out, table, sent = call(
@@ -527,10 +571,9 @@
             (pressure.shape, F32), (fluid_velocity.shape, F32), ((4 * LANES, 2 * LANES), BF16),
             ((6, leavers, LANES), F32),
         ],
-        tile, ylow, yhigh, xlow, xhigh, flow, leave,
+        xlow, xhigh, flow, own, inner, leave,
         scratch=[
-            pltpu.VMEM((2, size, 24, 2 * LANES), F32), grid, grid, grid, grid,
-            pltpu.VMEM((4, size, 24, 2 * LANES), F32),
+            pltpu.VMEM((2, size, 24, 2 * LANES), F32), grid, grid, pltpu.VMEM((6, size, 24, 2 * LANES), F32),
         ],
         busy_us=6,
     )

time: 41.7 us -> 41.2 us (0.988)
  transfers between devices with their start and end apart: 14 -> 14, of which waited for: 2 -> 2; matrix products, arithmetic and copies ran while one was open for 0% -> 0% of each run, Pallas kernels for 30% -> 32%
where the time goes in v7:
time: 41.2 us; the launch traced here: 41 us
  Pallas kernels  18.9 us (46%)
  starting transfers between devices  18.2 us (44%)
  waiting for transfers between devices  2.27 us (6%)
  local copies, waits for them, and re-layouts  0.9 us (2%)
  between operations  0.83 us (2%)
    pallas_call x14, Pallas kernels, call(): pl.pallas_call(kernel, out_shape=outs_list, in_specs=specs, out_specs=[vm...  18.9 us
    ppermute x14, starting transfers between devices, shifted(): lax.ppermute(block, axis, [((i - distance) % count, i) for i in range(cou...  18.2 us
    ppermute x14, waiting for transfers between devices, shifted(): lax.ppermute(block, axis, [((i - distance) % count, i) for i in range(cou...  2.27 us
    unnamed x16, local copies, waits for them, and re-layouts  0.89 us
  transfers between devices with their start and end apart: 14, of which 2 were waited for; matrix products, arithmetic and copies ran while one was open for 0% of the time, Pallas kernels for 32%

profile of v7, /device:TPU:1, one launch (start us, length us, event | category | flops | bytes accessed | tf_op | source)
XLA Modules:
  0.0 41.0 jit_solution(17719623340549998362)
XLA Ops:
  0.6 0.0 copy-start.3
  0.6 0.0 copy-start.6
  0.7 0.9 %copy-done.3 = f32[3,8,8,128]{3,2,1,0:T(8,128)S(1)} copy-done((f32[3,8,8,128]{3,2,1,0:T(8,128)S(1)}, f32[3,8,8,128]{3,2,1,0:T(8,128)}, u32[]{:S(2)}) %copy-start.3) | copy-done | bytes 98328
  1.5 0.0 copy-done.6
  1.5 0.0 copy-start.4
  1.5 0.0 copy-start.5
  1.5 2.1 %collective-permute-start.1 = (f32[256,128]{1,0:T(8,128)S(1)}, f32[256,128]{1,0:T(8,128)S(1)}, u32[]{:S(2)}, u32[]{:S(2)}) collective-permute-start(f32[256,128]{1,0:T(8,128)S(1)} %shard_map.112.after_ref.near_ref), channel_id=1, source_target_pairs={{1,0},{0,1},{3,2},{2,3},{5,4},{4,5},{7,6},{6,7},{9,8},{8,9},{11,10... | collective-permute-start | bytes 393224 | tf_op jit(solution)/shard_map/ppermute | solution.py:494
  3.7 0.0 copy-done.4
  3.7 0.0 copy-done.5
  3.7 0.0 copy-start
  3.7 0.0 copy-start.1
  3.7 0.0 copy-start.2
  3.7 2.9 %shard_map.113.mine_ref = f32[128,128]{1,0:T(8,128)S(1)} custom-call(s32[1]{0:T(128)} %bitcast.sec_ref, f32[128,128]{1,0:T(8,128)S(1)} %bitcast.6, s32[128,128]{1,0:T(8,128)S(1)} %bitcast.8, f32[256,128]{1,0:T(8,128)S(1)} %shard_map.112.after_ref.near_ref), custom_call_target="tpu_custom_call" | custom-call | flops 4600000000 | bytes 4096 | tf_op jit(solution)/shard_map/pallas_call | solution.py:33
  6.6 0.8 %collective-permute-start = (f32[128,128]{1,0:T(8,128)S(1)}, f32[128,128]{1,0:T(8,128)S(1)}, u32[]{:S(2)}, u32[]{:S(2)}) collective-permute-start(f32[128,128]{1,0:T(8,128)S(1)} %shard_map.113.mine_ref), channel_id=1, source_target_pairs={{1,0},{0,1},{3,2},{2,3},{5,4},{4,5},{7,6},{6,7},{9,8},{8,9},{11,10... | collective-permute-start | bytes 196616 | tf_op jit(solution)/shard_map/ppermute | solution.py:494
  7.4 0.0 collective-permute-done.1.far_ref
  7.4 0.1 shard_map.114
  7.5 1.4 %collective-permute-start.4 = (f32[208,128]{1,0:T(8,128)S(1)}, f32[208,128]{1,0:T(8,128)S(1)}, u32[]{:S(2)}, u32[]{:S(2)}) collective-permute-start(f32[208,128]{1,0:T(8,128)S(1)} %get-tuple-element.30), channel_id=1, source_target_pairs={{6,0},{0,2},{2,4},{4,6},{7,1},{1,3},{3,5},{5,7},{14,8},{8,10},{10,... | collective-permute-start | bytes 319496 | tf_op jit(solution)/shard_map/ppermute | solution.py:494
  8.8 2.1 %collective-permute-start.5 = (f32[208,128]{1,0:T(8,128)S(1)}, f32[208,128]{1,0:T(8,128)S(1)}, u32[]{:S(2)}, u32[]{:S(2)}) collective-permute-start(f32[208,128]{1,0:T(8,128)S(1)} %get-tuple-element.31), channel_id=1, source_target_pairs={{2,0},{4,2},{6,4},{0,6},{3,1},{5,3},{7,5},{1,7},{10,8},{12,10},{14... | collective-permute-start | bytes 319496 | tf_op jit(solution)/shard_map/ppermute | solution.py:494
  10.9 0.0 copy-done
  10.9 0.0 copy-done.1
  10.9 0.0 copy-done.2
  10.9 0.0 copy-start.7
  10.9 1.5 %shard_map.115.after_ref.base_ref = f32[7,128,128]{2,1,0:T(8,128)S(1)} custom-call(f32[128,128]{1,0:T(8,128)S(1)} %bitcast.7, f32[3,16384]{1,0:T(4,128)S(1)} %copy-done.1, f32[3,16384]{1,0:T(4,128)S(1)} %copy-done.2, s32[8,16384]{1,0:T(8,128)S(1)} %copy-done, f32[6,64,128]{2,1,0:T(8,128)S(1)} %get-tuple-element.26.after_ref.tile_ref), custom_call_target="tpu_custom_call" | custom-call | flops 4600000000 | bytes 4096 | tf_op jit(solution)/shard_map/pallas_call | solution.py:33
  12.4 0.0 collective-permute-done.got_ref
  12.4 1.5 %collective-permute-start.3 = (f32[160,128]{1,0:T(8,128)S(1)}, f32[160,128]{1,0:T(8,128)S(1)}, u32[]{:S(2)}, u32[]{:S(2)}) collective-permute-start(f32[160,128]{1,0:T(8,128)S(1)} %get-tuple-element.29), channel_id=1, source_target_pairs={{2,0},{4,2},{6,4},{0,6},{3,1},{5,3},{7,5},{1,7},{10,8},{12,10},{14... | collective-permute-start | bytes 245768 | tf_op jit(solution)/shard_map/ppermute | solution.py:494
  13.9 0.1 collective-permute-start.2
  14.0 0.0 collective-permute-done.4.low_ref.ylow_ref
  14.0 1.1 %collective-permute-done.5.high_ref.yhigh_ref = f32[208,128]{1,0:T(8,128)S(1)} collective-permute-done((f32[208,128]{1,0:T(8,128)S(1)}, f32[208,128]{1,0:T(8,128)S(1)}, u32[]{:S(2)}, u32[]{:S(2)}) %collective-permute-start.5) | collective-permute-done | bytes 106528 | tf_op jit(solution)/shard_map/ppermute | solution.py:494
  15.1 0.1 shard_map.117
  15.1 2.1 %collective-permute-start.9 = (f32[312,128]{1,0:T(8,128)S(1)}, f32[312,128]{1,0:T(8,128)S(1)}, u32[]{:S(2)}, u32[]{:S(2)}) collective-permute-start(f32[312,128]{1,0:T(8,128)S(1)} %get-tuple-element.36), channel_id=1, source_target_pairs={{8,0},{16,8},{24,16},{0,24},{9,1},{17,9},{25,17},{1,25},{10,2},{18... | collective-permute-start | bytes 479240 | tf_op jit(solution)/shard_map/ppermute | solution.py:494
  17.2 1.2 %collective-permute-start.8 = (f32[312,128]{1,0:T(8,128)S(1)}, f32[312,128]{1,0:T(8,128)S(1)}, u32[]{:S(2)}, u32[]{:S(2)}) collective-permute-start(f32[312,128]{1,0:T(8,128)S(1)} %get-tuple-element.32.after_ref), channel_id=1, source_target_pairs={{24,0},{0,8},{8,16},{16,24},{25,1},{1,9},{9,17},{17,25},{26,2},{2,... | collective-permute-start | bytes 479240 | tf_op jit(solution)/shard_map/ppermute | solution.py:494
  18.4 0.0 copy-done.7
  18.4 1.0 %shard_map.118 = (f32[128,128]{1,0:T(8,128)S(1)}, bf16[256,4096]{1,0:T(8,128)(2,1)S(1)}, bf16[64,4096]{1,0:T(8,128)(2,1)S(1)}) custom-call(s32[4,1024]{1,0:T(4,128)S(1)} %copy-done.7, f32[312,128]{1,0:T(8,128)S(1)} %get-tuple-element.32.after_ref), custom_call_target="tpu_custom_call" | custom-call | flops 2300000000 | bytes 4096 | tf_op jit(solution)/shard_map/pallas_call | solution.py:33
  19.4 0.0 collective-permute-done.3.high_ref.void_high_ref
  19.4 0.0 collective-permute-done.2.low_ref.void_low_ref
  19.4 2.6 %collective-permute-start.7 = (f32[240,128]{1,0:T(8,128)S(1)}, f32[240,128]{1,0:T(8,128)S(1)}, u32[]{:S(2)}, u32[]{:S(2)}) collective-permute-start(f32[240,128]{1,0:T(8,128)S(1)} %get-tuple-element.35), channel_id=1, source_target_pairs={{8,0},{16,8},{24,16},{0,24},{9,1},{17,9},{25,17},{1,25},{10,2},{18... | collective-permute-start | bytes 368648 | tf_op jit(solution)/shard_map/ppermute | solution.py:494
  22.0 1.2 %collective-permute-start.6 = (f32[240,128]{1,0:T(8,128)S(1)}, f32[240,128]{1,0:T(8,128)S(1)}, u32[]{:S(2)}, u32[]{:S(2)}) collective-permute-start(f32[240,128]{1,0:T(8,128)S(1)} %get-tuple-element.34.after_ref), channel_id=1, source_target_pairs={{24,0},{0,8},{8,16},{16,24},{25,1},{1,9},{9,17},{17,25},{26,2},{2,... | collective-permute-start | bytes 368648 | tf_op jit(solution)/shard_map/ppermute | solution.py:494
  23.2 2.5 %shard_map.121.leave_ref = f32[8,32,128]{2,1,0:T(8,128)S(1)} custom-call(s32[1]{0:T(128)} %bitcast.sec_ref, f32[7,128,128]{2,1,0:T(8,128)S(1)} %shard_map.115.after_ref.base_ref, s32[128,128]{1,0:T(8,128)S(1)} %bitcast.9, s32[4,1024]{1,0:T(4,128)S(1)} %copy-done.7, f32[240,128]{1,0:T(8,128)S(1)} %get-tuple-element.34.after_ref), custom_call_target="tpu_custom_call" | custom-call | flops 3449999872 | bytes 4096 | tf_op jit(solution)/shard_map/pallas_call | solution.py:33
  25.6 0.0 collective-permute-done.9.xhigh_ref
  25.7 0.0 collective-permute-done.8.xlow_ref
  25.7 0.5 %shard_map.120 = (f32[3,18,24,256]{3,2,1,0:T(8,128)S(1)}, f32[2,8,24,256]{3,2,1,0:T(8,128)S(1)}, f32[7,6,24,256]{3,2,1,0:T(8,128)S(1)}) custom-call(f32[6,64,128]{2,1,0:T(8,128)S(1)} %get-tuple-element.26.after_ref.tile_ref, f32[208,128]{1,0:T(8,128)S(1)} %collective-permute-done.4.low_ref.ylow_ref, ...), custom_call_target="tpu_custom_call" | custom-call | flops 1150000000 | bytes 4096 | tf_op jit(solution)/shard_map/pallas_call | solution.py:33
  26.1 1.1 %collective-permute-done.7.xhigh_ref = f32[240,128]{1,0:T(8,128)S(1)} collective-permute-done((f32[240,128]{1,0:T(8,128)S(1)}, f32[240,128]{1,0:T(8,128)S(1)}, u32[]{:S(2)}, u32[]{:S(2)}) %collective-permute-start.7) | collective-permute-done | bytes 122912 | tf_op jit(solution)/shard_map/ppermute | solution.py:494
  27.3 0.0 collective-permute-done.6.xlow_ref
  27.3 2.6 %shard_map.122 = (f32[8,8,128]{2,1,0:T(8,128)}, f32[3,8,8,128]{3,2,1,0:T(8,128)}, bf16[512,256]{1,0:T(8,128)(2,1)S(1)}, f32[6,32,128]{2,1,0:T(8,128)S(1)}) custom-call(f32[240,128]{1,0:T(8,128)S(1)} %collective-permute-done.6.xlow_ref, f32[240,128]{1,0:T(8,128)S(1)} %collective-permute-done.7.xhigh_ref, f32[3,18,24,256]{3,2,1,0:T(8,128)S(1)} %get-tuple-element.37.flow_ref, ...), custom_call_target="tpu_custom_call" | custom-call | flops 6899999744 | bytes 4096 | tf_op jit(solution)/shard_map/pallas_call | solution.py:33
  29.9 1.2 %collective-permute-start.13 = (f32[6,8,128]{2,1,0:T(8,128)S(1)}, f32[6,8,128]{2,1,0:T(8,128)S(1)}, u32[]{:S(2)}, u32[]{:S(2)}) collective-permute-start(f32[6,8,128]{2,1,0:T(8,128)S(1)} %get-tuple-element.48), channel_id=1, source_target_pairs={{2,0},{4,2},{6,4},{0,6},{3,1},{5,3},{7,5},{1,7},{10,8},{12,10},{14... | collective-permute-start | bytes 73736 | tf_op jit(solution)/shard_map/ppermute | solution.py:494
  31.1 0.3 collective-permute-start.12
  31.4 1.0 %collective-permute-start.11 = (f32[6,8,128]{2,1,0:T(8,128)S(1)}, f32[6,8,128]{2,1,0:T(8,128)S(1)}, u32[]{:S(2)}, u32[]{:S(2)}) collective-permute-start(f32[6,8,128]{2,1,0:T(8,128)S(1)} %get-tuple-element.50), channel_id=1, source_target_pairs={{8,0},{16,8},{24,16},{0,24},{9,1},{17,9},{25,17},{1,25},{10,2},{18... | collective-permute-start | bytes 73736 | tf_op jit(solution)/shard_map/ppermute | solution.py:494
  32.4 0.8 %collective-permute-start.10 = (f32[6,8,128]{2,1,0:T(8,128)S(1)}, f32[6,8,128]{2,1,0:T(8,128)S(1)}, u32[]{:S(2)}, u32[]{:S(2)}) collective-permute-start(f32[6,8,128]{2,1,0:T(8,128)S(1)} %get-tuple-element.51), channel_id=1, source_target_pairs={{24,0},{0,8},{8,16},{16,24},{25,1},{1,9},{9,17},{17,25},{26,2},{2,... | collective-permute-start | bytes 73736 | tf_op jit(solution)/shard_map/ppermute | solution.py:494
  33.2 4.6 %shard_map.123.moved_ref = f32[6,128,128]{2,1,0:T(8,128)S(1)} custom-call(s32[1]{0:T(128)} %bitcast.sec_ref, bf16[512,256]{1,0:T(8,128)(2,1)S(1)} %get-tuple-element.44.table_ref, s32[128,128]{1,0:T(8,128)S(1)} %bitcast.10, f32[7,128,128]{2,1,0:T(8,128)S(1)} %shard_map.115.after_ref.base_ref), custom_call_target="tpu_custom_call" | custom-call | flops 6899999744 | bytes 4096 | tf_op jit(solution)/shard_map/pallas_call | solution.py:33
  37.8 0.0 collective-permute-done.13.d_ref
  37.8 0.0 collective-permute-done.12.c_ref
  37.9 0.0 collective-permute-done.11.b_ref
  37.9 0.0 collective-permute-done.10.a_ref
  37.9 3.2 %shard_map.124 = (f32[3,16384]{1,0:T(4,128)}, f32[3,16384]{1,0:T(4,128)}) custom-call(bf16[256,4096]{1,0:T(8,128)(2,1)S(1)} %get-tuple-element.42.left_ref, bf16[64,4096]{1,0:T(8,128)(2,1)S(1)} %get-tuple-element.43.low_ref, f32[128,128]{1,0:T(8,128)S(1)} %get-tuple-element.33.after_ref.mask_ref, f32[6,128,128]{2,1,0:T(8,128)S(1)} %shard_map.123.moved_ref, ...), custom_call_target="tpu_custom_call" | custom-call | flops 4600000000 | bytes 4096 | tf_op jit(solution)/shard_map/pallas_call | solution.py:33
  (5 shorter events, 0.1 us)
Async XLA Ops:
  0.6 0.9 %copy-start.3 = (f32[3,8,8,128]{3,2,1,0:T(8,128)S(1)}, f32[3,8,8,128]{3,2,1,0:T(8,128)}, u32[]{:S(2)}) copy-start(f32[3,8,8,128]{3,2,1,0:T(8,128)} %param.9) | copy-start | bytes 294916
  0.6 0.9 %copy-start.6 = (f32[8,8,128]{2,1,0:T(8,128)S(1)}, f32[8,8,128]{2,1,0:T(8,128)}, u32[]{:S(2)}) copy-start(f32[8,8,128]{2,1,0:T(8,128)} %param.8) | copy-start | bytes 98308
  1.5 2.2 %copy-start.4 = (f32[16384]{0:T(1024)S(1)}, f32[16384]{0:T(1024)}, u32[]{:S(2)}) copy-start(f32[16384]{0:T(1024)} %param.12) | copy-start | bytes 196612
  1.5 2.2 %copy-start.5 = (s32[16384]{0:T(1024)S(1)}, s32[16384]{0:T(1024)}, u32[]{:S(2)}) copy-start(s32[16384]{0:T(1024)} %param.13) | copy-start | bytes 196612
  1.5 5.9 %collective-permute-start.1 = (f32[256,128]{1,0:T(8,128)S(1)}, f32[256,128]{1,0:T(8,128)S(1)}, u32[]{:S(2)}, u32[]{:S(2)}) collective-permute-start(f32[256,128]{1,0:T(8,128)S(1)} %shard_map.112.after_ref.near_ref), channel_id=1, source_target_pairs={{1,0},{0,1},{3,2},{2,3},{5,4},{4,5},{7,6},{6,7},{9,8},{8,9},{11,10... | collective-permute-start | bytes 393224 | tf_op jit(solution)/shard_map/ppermute | solution.py:494
  3.7 7.2 %copy-start = (s32[8,16384]{1,0:T(8,128)S(1)}, s32[8,16384]{1,0:T(8,128)}, u32[]{:S(2)}) copy-start(s32[8,16384]{1,0:T(8,128)} %pair_ref.1) | copy-start | bytes 1572868
  3.7 7.2 %copy-start.1 = (f32[3,16384]{1,0:T(4,128)S(1)}, f32[3,16384]{1,0:T(4,128)}, u32[]{:S(2)}) copy-start(f32[3,16384]{1,0:T(4,128)} %pos_ref.1) | copy-start | bytes 589828
  3.7 7.2 %copy-start.2 = (f32[3,16384]{1,0:T(4,128)S(1)}, f32[3,16384]{1,0:T(4,128)}, u32[]{:S(2)}) copy-start(f32[3,16384]{1,0:T(4,128)} %vel_ref.1) | copy-start | bytes 589828
  6.6 5.8 %collective-permute-start = (f32[128,128]{1,0:T(8,128)S(1)}, f32[128,128]{1,0:T(8,128)S(1)}, u32[]{:S(2)}, u32[]{:S(2)}) collective-permute-start(f32[128,128]{1,0:T(8,128)S(1)} %shard_map.113.mine_ref), channel_id=1, source_target_pairs={{1,0},{0,1},{3,2},{2,3},{5,4},{4,5},{7,6},{6,7},{9,8},{8,9},{11,10... | collective-permute-start | bytes 196616 | tf_op jit(solution)/shard_map/ppermute | solution.py:494
  7.5 6.5 %collective-permute-start.4 = (f32[208,128]{1,0:T(8,128)S(1)}, f32[208,128]{1,0:T(8,128)S(1)}, u32[]{:S(2)}, u32[]{:S(2)}) collective-permute-start(f32[208,128]{1,0:T(8,128)S(1)} %get-tuple-element.30), channel_id=1, source_target_pairs={{6,0},{0,2},{2,4},{4,6},{7,1},{1,3},{3,5},{5,7},{14,8},{8,10},{10,... | collective-permute-start | bytes 319496 | tf_op jit(solution)/shard_map/ppermute | solution.py:494
  8.8 6.3 %collective-permute-start.5 = (f32[208,128]{1,0:T(8,128)S(1)}, f32[208,128]{1,0:T(8,128)S(1)}, u32[]{:S(2)}, u32[]{:S(2)}) collective-permute-start(f32[208,128]{1,0:T(8,128)S(1)} %get-tuple-element.31), channel_id=1, source_target_pairs={{2,0},{4,2},{6,4},{0,6},{3,1},{5,3},{7,5},{1,7},{10,8},{12,10},{14... | collective-permute-start | bytes 319496 | tf_op jit(solution)/shard_map/ppermute | solution.py:494
  10.9 7.5 %copy-start.7 = (s32[4,1024]{1,0:T(4,128)S(1)}, s32[4,1024]{1,0:T(4,128)}, u32[]{:S(2)}) copy-start(s32[4,1024]{1,0:T(4,128)} %dep_ref.3) | copy-start | bytes 49156
  12.4 6.9 %collective-permute-start.3 = (f32[160,128]{1,0:T(8,128)S(1)}, f32[160,128]{1,0:T(8,128)S(1)}, u32[]{:S(2)}, u32[]{:S(2)}) collective-permute-start(f32[160,128]{1,0:T(8,128)S(1)} %get-tuple-element.29), channel_id=1, source_target_pairs={{2,0},{4,2},{6,4},{0,6},{3,1},{5,3},{7,5},{1,7},{10,8},{12,10},{14... | collective-permute-start | bytes 245768 | tf_op jit(solution)/shard_map/ppermute | solution.py:494
  13.9 5.5 %collective-permute-start.2 = (f32[160,128]{1,0:T(8,128)S(1)}, f32[160,128]{1,0:T(8,128)S(1)}, u32[]{:S(2)}, u32[]{:S(2)}) collective-permute-start(f32[160,128]{1,0:T(8,128)S(1)} %get-tuple-element.28.after_ref), channel_id=1, source_target_pairs={{6,0},{0,2},{2,4},{4,6},{7,1},{1,3},{3,5},{5,7},{14,8},{8,10},{10,... | collective-permute-start | bytes 245768 | tf_op jit(solution)/shard_map/ppermute | solution.py:494
  15.1 10.5 %collective-permute-start.9 = (f32[312,128]{1,0:T(8,128)S(1)}, f32[312,128]{1,0:T(8,128)S(1)}, u32[]{:S(2)}, u32[]{:S(2)}) collective-permute-start(f32[312,128]{1,0:T(8,128)S(1)} %get-tuple-element.36), channel_id=1, source_target_pairs={{8,0},{16,8},{24,16},{0,24},{9,1},{17,9},{25,17},{1,25},{10,2},{18... | collective-permute-start | bytes 479240 | tf_op jit(solution)/shard_map/ppermute | solution.py:494
  17.2 8.4 %collective-permute-start.8 = (f32[312,128]{1,0:T(8,128)S(1)}, f32[312,128]{1,0:T(8,128)S(1)}, u32[]{:S(2)}, u32[]{:S(2)}) collective-permute-start(f32[312,128]{1,0:T(8,128)S(1)} %get-tuple-element.32.after_ref), channel_id=1, source_target_pairs={{24,0},{0,8},{8,16},{16,24},{25,1},{1,9},{9,17},{17,25},{26,2},{2,... | collective-permute-start | bytes 479240 | tf_op jit(solution)/shard_map/ppermute | solution.py:494
  19.4 7.8 %collective-permute-start.7 = (f32[240,128]{1,0:T(8,128)S(1)}, f32[240,128]{1,0:T(8,128)S(1)}, u32[]{:S(2)}, u32[]{:S(2)}) collective-permute-start(f32[240,128]{1,0:T(8,128)S(1)} %get-tuple-element.35), channel_id=1, source_target_pairs={{8,0},{16,8},{24,16},{0,24},{9,1},{17,9},{25,17},{1,25},{10,2},{18... | collective-permute-start | bytes 368648 | tf_op jit(solution)/shard_map/ppermute | solution.py:494
  22.0 5.3 %collective-permute-start.6 = (f32[240,128]{1,0:T(8,128)S(1)}, f32[240,128]{1,0:T(8,128)S(1)}, u32[]{:S(2)}, u32[]{:S(2)}) collective-permute-start(f32[240,128]{1,0:T(8,128)S(1)} %get-tuple-element.34.after_ref), channel_id=1, source_target_pairs={{24,0},{0,8},{8,16},{16,24},{25,1},{1,9},{9,17},{17,25},{26,2},{2,... | collective-permute-start | bytes 368648 | tf_op jit(solution)/shard_map/ppermute | solution.py:494
  29.9 7.9 %collective-permute-start.13 = (f32[6,8,128]{2,1,0:T(8,128)S(1)}, f32[6,8,128]{2,1,0:T(8,128)S(1)}, u32[]{:S(2)}, u32[]{:S(2)}) collective-permute-start(f32[6,8,128]{2,1,0:T(8,128)S(1)} %get-tuple-element.48), channel_id=1, source_target_pairs={{2,0},{4,2},{6,4},{0,6},{3,1},{5,3},{7,5},{1,7},{10,8},{12,10},{14... | collective-permute-start | bytes 73736 | tf_op jit(solution)/shard_map/ppermute | solution.py:494
  31.1 6.7 %collective-permute-start.12 = (f32[6,8,128]{2,1,0:T(8,128)S(1)}, f32[6,8,128]{2,1,0:T(8,128)S(1)}, u32[]{:S(2)}, u32[]{:S(2)}) collective-permute-start(f32[6,8,128]{2,1,0:T(8,128)S(1)} %get-tuple-element.49), channel_id=1, source_target_pairs={{6,0},{0,2},{2,4},{4,6},{7,1},{1,3},{3,5},{5,7},{14,8},{8,10},{10,... | collective-permute-start | bytes 73736 | tf_op jit(solution)/shard_map/ppermute | solution.py:494
  31.4 6.4 %collective-permute-start.11 = (f32[6,8,128]{2,1,0:T(8,128)S(1)}, f32[6,8,128]{2,1,0:T(8,128)S(1)}, u32[]{:S(2)}, u32[]{:S(2)}) collective-permute-start(f32[6,8,128]{2,1,0:T(8,128)S(1)} %get-tuple-element.50), channel_id=1, source_target_pairs={{8,0},{16,8},{24,16},{0,24},{9,1},{17,9},{25,17},{1,25},{10,2},{18... | collective-permute-start | bytes 73736 | tf_op jit(solution)/shard_map/ppermute | solution.py:494
  32.4 5.5 %collective-permute-start.10 = (f32[6,8,128]{2,1,0:T(8,128)S(1)}, f32[6,8,128]{2,1,0:T(8,128)S(1)}, u32[]{:S(2)}, u32[]{:S(2)}) collective-permute-start(f32[6,8,128]{2,1,0:T(8,128)S(1)} %get-tuple-element.51), channel_id=1, source_target_pairs={{24,0},{0,8},{8,16},{16,24},{25,1},{1,9},{9,17},{17,25},{26,2},{2,... | collective-permute-start | bytes 73736 | tf_op jit(solution)/shard_map/ppermute | solution.py:494
